TPU v7x, 128 devices: a whole 4x4x4 slice. The times are simulated.
128 devices in a mesh: lon: 16 (over y, z_hi, core), lat: 8 (over z_lo, x).
Axes of the slice: x: 4, y: 4, z: 4 (z_hi: 2, z_lo: 2; z = z_hi * 2 + z_lo), core: 2. Of those that a mesh axis runs over, the one named last changes fastest.
Arguments:
- temp: float32 [16, 1024, 4096], P(None, 'lat', 'lon'), may hold values from -6 to 6
- salt: float32 [16, 1024, 4096], P(None, 'lat', 'lon'), may hold values from -6 to 6
- east_face_velocity: float32 [16, 1024, 4096], P(None, 'lat', 'lon'), may hold values from -0.1 to 0.1
- v_face: float32 [16, 1024, 4096], P(None, 'lat', 'lon'), may hold values from -0.1 to 0.1
- kappa: float32 [16, 1024, 4096], P(None, 'lat', 'lon'), may hold values from 0.01 to 0.1
- land_mask: int32 [1024, 4096], P('lat', 'lon'), may hold values 0 or 1
- margin_owner_device: int32 [8, 16, 256, 2], P('lat', 'lon'), may hold values from 0 to 127, all different within a row; in each aligned block of 256 rows (0 to 255, 256 to 511, ..., all dimensions but the last counted through in order) at most 8 rows name the same one
- margin_cell: int32 [8, 16, 256, 2], P('lat', 'lon'), may hold values from 0 to 255
- margin_weight: float32 [8, 16, 256, 2], P('lat', 'lon'), may hold values from 0.2 to 1
- air_temp: float32 [16, 8, 256, 128], P('lon', 'lat'), may hold values from -6 to 6
- wind_speed: float32 [16, 8, 256, 128], P('lon', 'lat'), may hold values from 0.3 to 3
Outputs:
- temp_out: float32 [16, 1024, 4096], P(None, 'lat', 'lon')
- salt_out: float32 [16, 1024, 4096], P(None, 'lat', 'lon')
- density: float32 [16, 1024, 4096], P(None, 'lat', 'lon')
Inputs may be any that keep to these rules, and one draw needn't show every extreme that they name: `margin_owner_device`: each block's 2 owners differ; among one device's 256 blocks no owner is named more than 8 times, a bound that some device reaches.
All inputs are finite; a program needn't handle non-finite values. No bound on the sum of `land_mask` on one device may be relied on, other than what follows from the above.
Results may differ from a plain program's by a relative error of at most 0.00002.
Values sent between devices are 32-bit elements; how exact they have to be, the bound alone decides.
No kernel may reach another device: no remote copies, remote signals or barrier semaphores. Data moves between devices by JAX's collectives and lax.ppermute only.
A program may use at most 192 MiB of HBM per device.

v0:
```python
import jax
import jax.numpy as jnp
from jax import lax
from jax.experimental import pallas as pl
from jax.experimental.pallas import tpu as pltpu
from jax.sharding import PartitionSpec as P

F32 = jnp.float32
BF16 = jnp.bfloat16
AXES = ("lon", "lat")
BULK = 0.1
SLOTS = 8
GROUP = SLOTS + 1
LEVELS = 16
ROWS = 128
LANES = 128
LIMIT = 20 * 1024 * 1024

VM = pl.BlockSpec(memory_space=pltpu.VMEM)
ANY = pl.BlockSpec(memory_space=pl.ANY)


def in_vmem(x):
    return pltpu.with_memory_space_constraint(x, pltpu.VMEM)


def dot(a, b):
    return jnp.dot(a, b, preferred_element_type=F32)


def dot_nt(a, b):
    return lax.dot_general(a, b, (((1,), (1,)), ((), ())), preferred_element_type=F32)


def pieces(x):
    high = x.astype(BF16)
    rest = x - high.astype(F32)
    middle = rest.astype(BF16)
    low = (rest - middle.astype(F32)).astype(BF16)
    return high, middle, low


def pick(onehot, x):
    high, middle, low = pieces(x)
    return dot(onehot, high) + (dot(onehot, middle) + dot(onehot, low))


def iota(shape, dim):
    return lax.broadcasted_iota(jnp.int32, shape, dim)


def roll(x, steps, axis):
    steps = steps % x.shape[axis]
    return x if steps == 0 else pltpu.roll(x, steps, axis)


def as_bf16(flag):
    return flag.astype(F32).astype(BF16)


def request_kernel(owner_ref, cell_ref, weight_ref, surface_ref, out_ref, codes_ref):
    w = weight_ref[...]
    share = w / (w[0:1] + w[1:2])
    before = iota((256, 256), 0)
    after = iota((256, 256), 1)
    perm = as_bf16(before == (after % ROWS) * 2 + after // ROWS)
    lists = jnp.concatenate([owner_ref[...].astype(F32), cell_ref[...].astype(F32)], axis=0)
    lists = dot(lists.astype(BF16), perm)
    share = pick_left(share, perm)
    owner = [lists[m : m + 1].astype(jnp.int32) for m in range(2)]
    cell = [lists[2 + m : 3 + m] for m in range(2)]
    device = iota((128, 256), 0)
    named = [as_bf16(device == owner[m]) for m in range(2)]
    earlier = as_bf16(before < after)
    ones = jnp.ones((256, 256), BF16)
    ahead = [dot(named[0], earlier), dot(named[1], earlier) + dot(named[0], ones)]
    rank = [
        jnp.sum(named[m].astype(F32) * ahead[m], axis=0, keepdims=True).astype(jnp.int32)
        for m in range(2)
    ]
    slot = iota((128, 256), 0)
    ids = sum(
        dot_nt(named[m], jnp.where(slot == rank[m], cell[m], 0.0).astype(BF16)) for m in range(2)
    )
    total = 128 * GROUP
    line = iota((total, 256), 0)
    place = as_bf16(
        (line == owner[0] * GROUP + rank[0]) | (line == owner[1] * GROUP + rank[1])
    )
    id_place = as_bf16(iota((total, 128), 0) == iota((total, 128), 1) * GROUP + SLOTS)
    surface = surface_ref[...]
    blocks = jnp.concatenate([surface[:, :LANES], surface[:, LANES:]], axis=0)
    out_ref[...] = pick(place, blocks) + dot(id_place, ids.astype(BF16))
    table = jnp.concatenate(
        [(owner[m] * SLOTS + rank[m]).astype(F32) for m in range(2)]
        + [share, jnp.zeros((124, 256), F32)],
        axis=0,
    )
    codes_ref[...] = jnp.transpose(table)


def pick_left(x, onehot):
    high, middle, low = pieces(x)
    return dot(high, onehot) + (dot(middle, onehot) + dot(low, onehot))


def make_request(owner, cell, weight, surface):
    return pl.pallas_call(
        request_kernel,
        out_shape=(
            pltpu.VMEM((128 * GROUP, LANES), F32),
            pltpu.VMEM((256, LANES), F32),
        ),
        grid=(1,),
        in_specs=[pl.BlockSpec((2, 256), lambda i: (0, 0))] * 3
        + [pl.BlockSpec((None, ROWS, 2 * LANES), lambda i: (0, 0, 0))],
        out_specs=(VM, VM),
        compiler_params=pltpu.CompilerParams(vmem_limit_bytes=LIMIT),
        cost_estimate=pl.CostEstimate(flops=2 * 10**9, bytes_accessed=2**20, transcendentals=0),
        name="request",
    )(*[pltpu.with_memory_space_constraint(x, pltpu.HBM) for x in (owner, cell, weight, surface)])


def answer_kernel(got_ref, air_ref, wind_ref, out_ref):
    ids = got_ref[pl.ds(SLOTS, 128, stride=GROUP), :].astype(BF16)
    patches = jnp.concatenate([air_ref[...], wind_ref[...]], axis=1)
    high, middle, low = pieces(patches)
    spread = jnp.ones((128, 256), BF16)
    chunk = 128
    for part in range(8):
        line = iota((chunk, 128), 0) + part * chunk
        lane = iota((chunk, 128), 1)
        rows = dot(as_bf16(line // SLOTS == lane), ids)
        rows = jnp.where(lane == line % SLOTS, rows, 0.0)
        wanted = dot(rows.astype(BF16), spread).astype(jnp.int32)
        onehot = as_bf16(wanted == iota((chunk, 256), 1))
        found = dot(onehot, high) + (dot(onehot, middle) + dot(onehot, low))
        for s in range(chunk // SLOTS):
            source = part * (chunk // SLOTS) + s
            cells = got_ref[source * GROUP : source * GROUP + SLOTS, :]
            here = found[s * SLOTS : (s + 1) * SLOTS]
            out_ref[source * SLOTS : (source + 1) * SLOTS, :] = (
                BULK * here[:, LANES:] * (here[:, :LANES] - cells)
            )


def make_answer(got, air, wind):
    return pl.pallas_call(
        answer_kernel,
        out_shape=pltpu.VMEM((128 * SLOTS, LANES), F32),
        in_specs=[VM] * 3,
        out_specs=VM,
        compiler_params=pltpu.CompilerParams(vmem_limit_bytes=LIMIT),
        cost_estimate=pl.CostEstimate(flops=2 * 10**9, bytes_accessed=2**20, transcendentals=0),
        name="answer",
    )(in_vmem(got), air, wind)


def is_odd(axis):
    return lax.rem(lax.axis_index(axis), 2) == 1


def flipped(x):
    back = as_bf16(iota((256, 256), 0) + iota((256, 256), 1) == 255)
    return pick_left(x, back)


def column_edges(load_t, load_s, extra, strip):
    lane = iota((8, LANES), 1)
    west = jnp.zeros((8, LANES), F32)
    east = jnp.zeros((8, LANES), F32)
    other = jnp.zeros((8, LANES), F32)
    for k in range(LEVELS):
        for t, load in enumerate((load_t, load_s)):
            x0, x1 = load(k, strip)
            at = LEVELS * t + k
            west = jnp.where(lane == at, roll(x0, at, 1), west)
            east = jnp.where(lane == at, roll(x1, at - 127, 1), east)
        if extra is not None:
            for f, ref in enumerate(extra):
                at = 32 + 32 * f + k
                x1 = ref[k, pl.ds(strip, 8), LANES:]
                other = jnp.where(lane == at, roll(x1, at - 127, 1), other)
    if extra is not None:
        east = east + (other + roll(other, 16, 1))
    return west, east


def send_columns(west, east, odd, strip, lon_a_ref, lon_b_ref):
    rows = pl.ds(strip, 8)
    lon_a_ref[rows, :] = jnp.where(odd, west, east)
    lon_b_ref[rows, :] = jnp.where(odd, east, west)


def edges_kernel(t_ref, s_ref, u_ref, v_ref, k_ref, lon_a_ref, lon_b_ref, lat_a_ref, lat_b_ref, west_ref):
    odd = is_odd("lon")

    def strip_step(i, carry):
        strip = pl.multiple_of(i * 8, 8)

        def loader(ref):
            return lambda k, r: (ref[k, pl.ds(r, 8), :LANES], ref[k, pl.ds(r, 8), LANES:])

        west, east = column_edges(loader(t_ref), loader(s_ref), (u_ref, k_ref), strip)
        west_ref[pl.ds(strip, 8), :] = west
        send_columns(west, east, odd, strip, lon_a_ref, lon_b_ref)
        return carry

    lax.fori_loop(0, ROWS // 8, strip_step, 0)
    odd_lat = is_odd("lat")
    top = lax.axis_index("lat") == lax.axis_size("lat") - 1
    south = jnp.concatenate(
        [ref[k, 0:1, :] for ref in (t_ref, s_ref) for k in range(LEVELS)], axis=0
    )
    north = jnp.concatenate(
        [ref[k, ROWS - 1 : ROWS, :] for ref in (t_ref, s_ref) for k in range(LEVELS)], axis=0
    )
    faces = jnp.concatenate(
        [ref[k, ROWS - 1 : ROWS, :] for ref in (v_ref, k_ref) for k in range(LEVELS)], axis=0
    )
    fold = flipped(north)
    lat_a_ref[0:32, :] = jnp.where(odd_lat, south, north)
    lat_a_ref[32:64, :] = faces
    lat_b_ref[0:32, :] = jnp.where(odd_lat, jnp.where(top, fold, north), south)
    lat_b_ref[32:64, :] = faces


def make_edges(t, s, u, v, k):
    return pl.pallas_call(
        edges_kernel,
        out_shape=(
            pltpu.VMEM((ROWS, LANES), F32),
            pltpu.VMEM((ROWS, LANES), F32),
            pltpu.VMEM((64, 256), F32),
            pltpu.VMEM((64, 256), F32),
            pltpu.VMEM((ROWS, LANES), F32),
        ),
        in_specs=[VM] * 5,
        out_specs=(VM,) * 5,
        compiler_params=pltpu.CompilerParams(vmem_limit_bytes=LIMIT),
        cost_estimate=pl.CostEstimate(flops=10**7, bytes_accessed=4 * 2**20, transcendentals=0),
        name="edges",
    )(t, s, u, v, k)


def swap_pairs(first, count):
    route = []
    for low in range(first, count - 1, 2):
        route += [(low, low + 1), (low + 1, low)]
    return route


def exchange(lon_a, lon_b, lat_a, lat_b):
    n_lon, n_lat = lax.axis_size("lon"), lax.axis_size("lat")
    ring = swap_pairs(1, n_lon) + [(n_lon - 1, 0), (0, n_lon - 1)]
    got_lon_a = lax.ppermute(lon_a, "lon", swap_pairs(0, n_lon))
    got_lon_b = lax.ppermute(lon_b, "lon", ring)
    got_lat_a = lax.ppermute(lat_a, "lat", swap_pairs(0, n_lat))
    route = [
        (i * n_lat + low, i * n_lat + high) for i in range(n_lon) for low, high in swap_pairs(1, n_lat)
    ]
    route += [(i * n_lat + n_lat - 1, (n_lon - 1 - i) * n_lat + n_lat - 1) for i in range(n_lon)]
    got_lat_b = lax.ppermute(lat_b, AXES, route)
    return got_lon_a, got_lon_b, got_lat_a, got_lat_b


def density_of(t, s):
    return t * (-0.25 - 0.04 * t + 0.03 * s) + 0.8 * s


def twice_density(t, s):
    return t * (-0.5 - 0.08 * t + 0.06 * s) + 1.6 * s


def step_strip(strip, last, load, u_ref, v_ref, k_ref, mask_ref, west_flux_ref, east_ref, north_ref, carry_ref, emit, heat_ref=None):
    rows = pl.ds(strip, 8)
    lane = iota((8, LANES), 1)
    sub = iota((8, LANES), 0)
    first_lane, last_lane = lane == 0, lane == LANES - 1
    row0, row7 = sub == 0, sub == 7
    halves = (slice(0, LANES), slice(LANES, 2 * LANES))
    mask = [mask_ref[rows, h].astype(F32) for h in halves]
    west_flux = west_flux_ref[rows, :]
    east_halo = east_ref[rows, :]
    x = [load(t, 0, strip) for t in range(2)]
    rho = [twice_density(x[0][h], x[1][h]) for h in range(2)]
    below = None
    for k in range(LEVELS):
        if k < LEVELS - 1:
            x_next = [load(t, k + 1, strip) for t in range(2)]
            rho_next = [twice_density(x_next[0][h], x_next[1][h]) for h in range(2)]
            mixing = [0.06 + 0.05 * jnp.tanh(rho[h] - rho_next[h]) for h in range(2)]
        u = [u_ref[k, rows, h] for h in halves]
        v = [v_ref[k, rows, h] for h in halves]
        d = [k_ref[k, rows, h] for h in halves]
        pe = [jnp.maximum(u[h], 0.0) + d[h] for h in range(2)]
        ne = [jnp.minimum(u[h], 0.0) - d[h] for h in range(2)]
        pn = [jnp.maximum(v[h], 0.0) + d[h] for h in range(2)]
        nn = [jnp.minimum(v[h], 0.0) - d[h] for h in range(2)]
        above = [None, None]
        new = [None, None]
        for t in range(2):
            at = LEVELS * t + k
            xt = x[t]
            y = [roll(xt[h], -1, 1) for h in range(2)]
            xe = [
                jnp.where(last_lane, y[1], y[0]),
                jnp.where(last_lane, roll(east_halo, 127 - at, 1), y[1]),
            ]
            east = [pe[h] * xt[h] + ne[h] * xe[h] for h in range(2)]
            z = [roll(east[h], 1, 1) for h in range(2)]
            west = [
                jnp.where(first_lane, roll(west_flux, -at, 1), z[0]),
                jnp.where(first_lane, z[0], z[1]),
            ]
            if last:
                ahead = [jnp.broadcast_to(north_ref[at : at + 1, h], (8, LANES)) for h in halves]
            else:
                ahead = load(t, k, strip + 8)
            xn = [roll(jnp.where(row0, ahead[h], xt[h]), -1, 0) for h in range(2)]
            north = [pn[h] * xt[h] + nn[h] * xn[h] for h in range(2)]
            south = [
                roll(jnp.where(row7, carry_ref[at, :, halves[h]], north[h]), 1, 0) for h in range(2)
            ]
            if not last:
                for h in range(2):
                    carry_ref[at, :, halves[h]] = north[h]
            tend = [(west[h] - east[h]) + (south[h] - north[h]) for h in range(2)]
            if k < LEVELS - 1:
                above[t] = [mixing[h] * (x_next[t][h] - xt[h]) for h in range(2)]
                tend = [tend[h] + above[t][h] for h in range(2)]
            if k > 0:
                tend = [tend[h] - below[t][h] for h in range(2)]
            if heat_ref is not None and t == 0 and k == 0:
                tend = [tend[h] + heat_ref[rows, halves[h]] for h in range(2)]
            new[t] = [xt[h] + mask[h] * tend[h] for h in range(2)]
        emit(k, strip, new)
        below = above
        if k < LEVELS - 1:
            x, rho = x_next, rho_next


def west_fluxes(west, coef, own):
    u = roll(coef, -32, 1)
    d = roll(coef, -64, 1)
    return (jnp.maximum(u, 0.0) + d) * west + (jnp.minimum(u, 0.0) - d) * own


def first_carry(south, faces, load_row, carry_ref):
    for k in range(LEVELS):
        v, d = faces(k), faces(LEVELS + k)
        pn = jnp.maximum(v, 0.0) + d
        nn = jnp.minimum(v, 0.0) - d
        for t in range(2):
            at = LEVELS * t + k
            flux = pn * south(at) + nn * load_row(t, k)
            carry_ref[at] = jnp.broadcast_to(flux, (8, 2 * LANES))


def halo_setup(odd_lon, odd_lat, got, coefs, own_ref, load_row, carry_ref, west_flux_ref, east_ref, north_ref):
    lon_a, lon_b, lat_a, lat_b = got
    c_lon_a, c_lon_b, c_lat_a, c_lat_b = coefs
    west = jnp.where(odd_lon, lon_a[...], lon_b[...])
    coef = jnp.where(odd_lon, c_lon_a[...], c_lon_b[...])
    west_flux_ref[...] = west_fluxes(west, coef, own_ref[...])
    east_ref[...] = jnp.where(odd_lon, lon_b[...], lon_a[...])
    north_ref[...] = jnp.where(odd_lat, lat_b[0:32, :], lat_a[0:32, :])

    def south(at):
        return jnp.where(odd_lat, lat_a[at : at + 1, :], lat_b[at : at + 1, :])

    def faces(at):
        return jnp.where(odd_lat, c_lat_a[32 + at : 33 + at, :], c_lat_b[32 + at : 33 + at, :])

    first_carry(south, faces, load_row, carry_ref)


def pair_loader(refs, top_ref=None):
    def load(t, k, strip):
        rows = pl.ds(strip, 8)
        if t == 0 and k == 0 and top_ref is not None:
            return [top_ref[rows, :LANES], top_ref[rows, LANES:]]
        return [refs[t][k, rows, :LANES], refs[t][k, rows, LANES:]]

    def load_row(t, k):
        if t == 0 and k == 0 and top_ref is not None:
            return top_ref[0:1, :]
        return refs[t][k, 0:1, :]

    return load, load_row


def strips(body):
    def one(i, carry):
        body(pl.multiple_of(i * 8, 8), False)
        return carry

    lax.fori_loop(0, ROWS // 8 - 1, one, 0)
    body(ROWS - 8, True)


def first_kernel(t_ref, s_ref, u_ref, v_ref, k_ref, mask_ref, own_ref, lon_a, lon_b, lat_a, lat_b,
                 t_out, s_out, carry_ref, west_flux_ref, east_ref, north_ref):
    load, load_row = pair_loader((t_ref, s_ref))
    got = (lon_a, lon_b, lat_a, lat_b)
    halo_setup(is_odd("lon"), is_odd("lat"), got, got, own_ref, load_row, carry_ref, west_flux_ref, east_ref, north_ref)
    outs = (t_out, s_out)

    def emit(k, strip, new):
        for t in range(2):
            for h in range(2):
                outs[t][k, pl.ds(strip, 8), h * LANES : (h + 1) * LANES] = new[t][h]

    def body(strip, last):
        step_strip(strip, last, load, u_ref, v_ref, k_ref, mask_ref, west_flux_ref, east_ref, north_ref, carry_ref, emit)

    strips(body)


STEP_SCRATCH = [
    pltpu.VMEM((2 * LEVELS, 8, 2 * LANES), F32),
    pltpu.VMEM((ROWS, LANES), F32),
    pltpu.VMEM((ROWS, LANES), F32),
    pltpu.VMEM((2 * LEVELS, 2 * LANES), F32),
]
STEP_COST = pl.CostEstimate(flops=7 * 10**7, bytes_accessed=25 * 2**20, transcendentals=10**6)


def first_step(t, s, u, v, k, mask, own, got):
    shape = pltpu.VMEM((LEVELS, ROWS, 2 * LANES), F32)
    return pl.pallas_call(
        first_kernel,
        out_shape=(shape, shape),
        in_specs=[VM] * 11,
        out_specs=(VM, VM),
        scratch_shapes=STEP_SCRATCH,
        compiler_params=pltpu.CompilerParams(vmem_limit_bytes=LIMIT),
        cost_estimate=STEP_COST,
        name="first_step",
    )(t, s, u, v, k, mask, own, *got)


def heat_kernel(t_ref, s_ref, mask_ref, back_ref, codes_ref, heat_out, top_out, lon_a_ref, lon_b_ref, lat_a_ref, lat_b_ref, west_ref):
    high, middle, low = pieces(back_ref[...])
    codes = codes_ref[...]
    lane = iota((256, 1024), 1)
    heat = None
    for m in range(2):
        onehot = as_bf16(codes[:, m : m + 1].astype(jnp.int32) == lane)
        flux = dot(onehot, high) + (dot(onehot, middle) + dot(onehot, low))
        part = codes[:, 2 + m : 3 + m] * flux
        heat = part if heat is None else heat + part
    mask = mask_ref[...].astype(F32)
    for h in range(2):
        cols = slice(h * LANES, (h + 1) * LANES)
        heat_out[:, cols] = heat[h * ROWS : (h + 1) * ROWS]
        top_out[:, cols] = t_ref[0, :, cols] + mask[:, cols] * heat[h * ROWS : (h + 1) * ROWS]
    odd = is_odd("lon")
    load, load_row = pair_loader((t_ref, s_ref), top_out)

    def strip_step(i, carry):
        strip = pl.multiple_of(i * 8, 8)
        west, east = column_edges(
            lambda k, r: load(0, k, r), lambda k, r: load(1, k, r), None, strip
        )
        west_ref[pl.ds(strip, 8), :] = west
        send_columns(west, east, odd, strip, lon_a_ref, lon_b_ref)
        return carry

    lax.fori_loop(0, ROWS // 8, strip_step, 0)
    odd_lat = is_odd("lat")
    top = lax.axis_index("lat") == lax.axis_size("lat") - 1
    last_rows = slice(ROWS - 1, ROWS)
    south = jnp.concatenate([load_row(t, k) for t in range(2) for k in range(LEVELS)], axis=0)
    north = jnp.concatenate(
        [top_out[last_rows, :]]
        + [t_ref[k, last_rows, :] for k in range(1, LEVELS)]
        + [s_ref[k, last_rows, :] for k in range(LEVELS)],
        axis=0,
    )
    fold = flipped(north)
    lat_a_ref[...] = jnp.where(odd_lat, south, north)
    lat_b_ref[...] = jnp.where(odd_lat, jnp.where(top, fold, north), south)


def add_heat(t, s, mask, back, codes):
    return pl.pallas_call(
        heat_kernel,
        out_shape=(
            pltpu.VMEM((ROWS, 2 * LANES), F32),
            pltpu.VMEM((ROWS, 2 * LANES), F32),
            pltpu.VMEM((ROWS, LANES), F32),
            pltpu.VMEM((ROWS, LANES), F32),
            pltpu.VMEM((32, 2 * LANES), F32),
            pltpu.VMEM((32, 2 * LANES), F32),
            pltpu.VMEM((ROWS, LANES), F32),
        ),
        in_specs=[VM] * 5,
        out_specs=(VM,) * 7,
        compiler_params=pltpu.CompilerParams(vmem_limit_bytes=LIMIT),
        cost_estimate=pl.CostEstimate(flops=10**9, bytes_accessed=4 * 2**20, transcendentals=0),
        name="heat",
    )(t, s, mask, in_vmem(back), in_vmem(codes))


def second_kernel(t_ref, s_ref, top_ref, heat_ref, u_ref, v_ref, k_ref, mask_ref, own_ref,
                  lon_a, lon_b, lat_a, lat_b, c_lon_a, c_lon_b, c_lat_a, c_lat_b,
                  t_out, s_out, rho_out,
                  carry_ref, west_flux_ref, east_ref, north_ref, t_buf, s_buf, rho_buf, sems):
    load, load_row = pair_loader((t_ref, s_ref), top_ref)
    halo_setup(is_odd("lon"), is_odd("lat"), (lon_a, lon_b, lat_a, lat_b), (c_lon_a, c_lon_b, c_lat_a, c_lat_b),
               own_ref, load_row, carry_ref, west_flux_ref, east_ref, north_ref)
    bufs = (t_buf, s_buf, rho_buf)
    outs = (t_out, s_out, rho_out)

    def emit(k, strip, new):
        for h in range(2):
            at = (k, pl.ds(strip, 8), slice(h * LANES, (h + 1) * LANES))
            for t in range(2):
                bufs[t][at] = new[t][h]
            rho_buf[at] = density_of(new[0][h], new[1][h])

    def copies(strip, index):
        rows = pl.ds(strip, 8)
        return [
            pltpu.make_async_copy(bufs[n].at[:, rows, :], outs[n].at[:, rows, :], sems.at[n, index])
            for n in range(3)
        ]

    def body(strip, last):
        step_strip(strip, last, load, u_ref, v_ref, k_ref, mask_ref, west_flux_ref, east_ref, north_ref, carry_ref, emit, heat_ref)
        index = ROWS // 8 - 1 if last else strip // 8
        for copy in copies(strip, index):
            copy.start()

    strips(body)
    for index in range(ROWS // 8):
        for copy in copies(index * 8, index):
            copy.wait()


def second_step(t, s, top, heat, u, v, k, mask, own, got, coefs):
    shape = jax.ShapeDtypeStruct((LEVELS, ROWS, 2 * LANES), F32)
    buf = pltpu.VMEM((LEVELS, ROWS, 2 * LANES), F32)
    return pl.pallas_call(
        second_kernel,
        out_shape=(shape, shape, shape),
        in_specs=[VM] * 17,
        out_specs=(ANY, ANY, ANY),
        scratch_shapes=STEP_SCRATCH + [buf, buf, buf, pltpu.SemaphoreType.DMA((3, ROWS // 8))],
        compiler_params=pltpu.CompilerParams(vmem_limit_bytes=LIMIT),
        cost_estimate=STEP_COST,
        name="second_step",
    )(t, s, in_vmem(top), in_vmem(heat), u, v, k, mask, in_vmem(own), *[in_vmem(g) for g in got], *coefs)


def body(
    temp,
    salt,
    east_face_velocity,
    v_face,
    kappa,
    land_mask,
    margin_owner_device,
    margin_cell,
    margin_weight,
    air_temp,
    wind_speed,
):
    def lists(x):
        return jnp.transpose(x.reshape(256, 2))

    request, codes = make_request(
        lists(margin_owner_device), lists(margin_cell), lists(margin_weight), temp
    )
    request = request.reshape(128, 1, GROUP * LANES)
    got = lax.all_to_all(request, AXES, split_axis=0, concat_axis=0, tiled=True)
    got = got.reshape(128 * GROUP, LANES)
    t, s, u, v, k = [in_vmem(x) for x in (temp, salt, east_face_velocity, v_face, kappa)]
    mask = in_vmem(land_mask)
    *sent, own = make_edges(t, s, u, v, k)
    halos = exchange(*sent)
    answer = make_answer(got, air_temp.reshape(256, LANES), wind_speed.reshape(256, LANES))
    back = lax.all_to_all(answer, AXES, split_axis=0, concat_axis=0, tiled=True)
    halos = [in_vmem(g) for g in halos]
    t1, s1 = [in_vmem(x) for x in first_step(t, s, u, v, k, mask, in_vmem(own), halos)]
    heat, top, *sent, own = add_heat(t1, s1, mask, back, codes)
    later = exchange(*sent)
    return second_step(t1, s1, top, heat, u, v, k, mask, own, later, halos)


def solution(mesh):
    grid = P(None, "lat", "lon")
    lists = P("lat", "lon", None, None)
    owned = P("lon", "lat", None, None)
    in_specs = (grid,) * 5 + (P("lat", "lon"),) + (lists,) * 3 + (owned,) * 2
    return jax.shard_map(body, mesh=mesh, in_specs=in_specs, out_specs=(grid,) * 3, check_vma=False)
```

profile of v0, /device:TPU:38, one launch (start us, length us, event | category | flops | bytes accessed | tf_op | source)
XLA Modules:
  0.0 108.7 jit_solution(7366928941902222741)
XLA Ops:
  0.7 2.1 %request.1 = (f32[1152,128]{1,0:T(8,128)S(1)}, f32[256,128]{1,0:T(8,128)S(1)}) custom-call(s32[2,256]{1,0:T(2,128)} %bitcast.20, s32[2,256]{1,0:T(2,128)} %bitcast.21, f32[2,256]{1,0:T(2,128)} %bitcast.22, f32[16,128,256]{2,1,0:T(8,128)} %surface_ref.1), custom_call_target="tpu_custom_call" | custom-call | flops 2000000000 | bytes 1048576 | tf_op jit(solution)/shard_map/request/pallas_call | solution.py:108
  2.8 22.2 %all_to_all.16 = f32[128,1,1152]{2,1,0:T(1,128)S(1)} all-to-all(f32[128,1,1152]{2,1,0:T(1,128)S(1)} %bitcast.16), channel_id=1, replica_groups=mesh['lon'=16,'lat'=8] {'lon','lat'}, dimensions={0} | all-to-all | bytes 1179648 | tf_op jit(solution)/shard_map/all_to_all | solution.py:577
  25.0 2.5 %answer.1 = f32[1024,128]{1,0:T(8,128)} custom-call(f32[1152,128]{1,0:T(8,128)S(1)} %bitcast.17, f32[256,128]{1,0:T(8,128)S(1)} %bitcast.18, f32[256,128]{1,0:T(8,128)S(1)} %bitcast.19), custom_call_target="tpu_custom_call" | custom-call | flops 2000000000 | bytes 1048576 | tf_op jit(solution)/shard_map/answer/pallas_call | solution.py:148
  27.4 6.9 %all-to-all-start.1 = ((f32[128,8,128]{2,1,0:T(8,128)}), f32[128,8,128]{2,1,0:T(8,128)S(1)}, u32[]{:S(2)}, u32[]{:S(2)}) async-start(f32[128,8,128]{2,1,0:T(8,128)} %bitcast.10), calls=%async_computation.1 | async-start | bytes 1048576 | tf_op jit(solution)/shard_map/all_to_all | solution.py:584
  34.3 0.0 copy-start.1
  34.4 1.6 %copy-done.1 = f32[16,128,256]{2,1,0:T(8,128)S(1)} copy-done((f32[16,128,256]{2,1,0:T(8,128)S(1)}, f32[16,128,256]{2,1,0:T(8,128)}, u32[]{:S(2)}) %copy-start.1) | copy-done | bytes 2097176
  35.9 1.6 %copy-done.3 = f32[16,128,256]{2,1,0:T(8,128)S(1)} copy-done((f32[16,128,256]{2,1,0:T(8,128)S(1)}, f32[16,128,256]{2,1,0:T(8,128)}, u32[]{:S(2)}) %copy-start.3) | copy-done | bytes 2097176
  37.5 1.6 %copy-done.5 = f32[16,128,256]{2,1,0:T(8,128)S(1)} copy-done((f32[16,128,256]{2,1,0:T(8,128)S(1)}, f32[16,128,256]{2,1,0:T(8,128)}, u32[]{:S(2)}) %copy-start.5) | copy-done | bytes 2097176
  39.1 1.6 %copy-done.6 = f32[16,128,256]{2,1,0:T(8,128)S(1)} copy-done((f32[16,128,256]{2,1,0:T(8,128)S(1)}, f32[16,128,256]{2,1,0:T(8,128)}, u32[]{:S(2)}) %copy-start.6) | copy-done | bytes 2097176
  40.7 3.2 %edges.1 = (f32[128,128]{1,0:T(8,128)S(1)}, f32[128,128]{1,0:T(8,128)S(1)}, f32[64,256]{1,0:T(8,128)S(1)}, f32[64,256]{1,0:T(8,128)S(1)}, f32[128,128]{1,0:T(8,128)S(1)}) custom-call(f32[16,128,256]{2,1,0:T(8,128)S(1)} %copy-done.5, f32[16,128,256]{2,1,0:T(8,128)S(1)} %copy-done.6, f32[16,128,256]{2,1,0:T(8,128)S(1)} %copy-done, ...), custom_call_target="tpu_custom_call" | custom-call | flops 10000000 | bytes 4194304 | tf_op jit(solution)/shard_map/edges/pallas_call | solution.py:229
  43.9 0.2 collective-permute-start
  44.1 4.9 %collective-permute-start.1 = (f32[128,128]{1,0:T(8,128)S(1)}, f32[128,128]{1,0:T(8,128)S(1)}, u32[]{:S(2)}, u32[]{:S(2)}) collective-permute-start(f32[128,128]{1,0:T(8,128)S(1)} %get-tuple-element.21), channel_id=1, source_target_pairs={{8,16},{16,8},{24,32},{32,24},{40,48},{48,40},{56,64},{64,56},{72,... | collective-permute-start | bytes 196616 | tf_op jit(solution)/shard_map/ppermute | solution.py:257
  49.0 0.8 collective-permute-start.2
  49.8 2.1 %collective-permute-start.3 = (f32[64,256]{1,0:T(8,128)S(1)}, f32[64,256]{1,0:T(8,128)S(1)}, u32[]{:S(2)}, u32[]{:S(2)}) collective-permute-start(f32[64,256]{1,0:T(8,128)S(1)} %get-tuple-element.23), channel_id=1, source_target_pairs={{1,2},{2,1},{3,4},{4,3},{5,6},{6,5},{9,10},{10,9},{11,12},{12,11},... | collective-permute-start | bytes 196616 | tf_op jit(solution)/shard_map/ppermute | solution.py:263
  51.9 0.0 collective-permute-done.1.lon_b.c_lon_b
  52.0 1.3 %collective-permute-done.2.lat_a.c_lat_a = f32[64,256]{1,0:T(8,128)S(1)} collective-permute-done((f32[64,256]{1,0:T(8,128)S(1)}, f32[64,256]{1,0:T(8,128)S(1)}, u32[]{:S(2)}, u32[]{:S(2)}) %collective-permute-start.2) | collective-permute-done | bytes 65568 | tf_op jit(solution)/shard_map/ppermute | solution.py:258
  53.3 5.8 %collective-permute-done.3.lat_b.c_lat_b = f32[64,256]{1,0:T(8,128)S(1)} collective-permute-done((f32[64,256]{1,0:T(8,128)S(1)}, f32[64,256]{1,0:T(8,128)S(1)}, u32[]{:S(2)}, u32[]{:S(2)}) %collective-permute-start.3) | collective-permute-done | bytes 65568 | tf_op jit(solution)/shard_map/ppermute | solution.py:263
  59.0 14.5 %first_step.1 = (f32[16,128,256]{2,1,0:T(8,128)S(1)}, f32[16,128,256]{2,1,0:T(8,128)S(1)}) custom-call(f32[16,128,256]{2,1,0:T(8,128)S(1)} %copy-done.5, f32[16,128,256]{2,1,0:T(8,128)S(1)} %copy-done.6, f32[16,128,256]{2,1,0:T(8,128)S(1)} %copy-done, f32[16,128,256]{2,1,0:T(8,128)S(1)} %copy-done.1, f32[16,128,256]{2,1,0:T(8,128)S(1)} %copy-done.3, ...), custom_call_target="tpu_custom_call" | custom-call | flops 70000000 | bytes 26214400 | tf_op jit(solution)/shard_map/first_step/pallas_call | solution.py:431
  73.5 0.0 copy-start.7
  73.5 1.3 %copy-done.7 = f32[16,128,256]{2,1,0:T(8,128)} copy-done((f32[16,128,256]{2,1,0:T(8,128)}, f32[16,128,256]{2,1,0:T(8,128)S(1)}, u32[]{:S(2)}) %copy-start.7) | copy-done | bytes 2097176
  74.8 1.3 %copy-done.9 = f32[16,128,256]{2,1,0:T(8,128)} copy-done((f32[16,128,256]{2,1,0:T(8,128)}, f32[16,128,256]{2,1,0:T(8,128)S(1)}, u32[]{:S(2)}) %copy-start.9) | copy-done | bytes 2097176
  76.1 0.0 all-to-all-done.1
  76.1 1.6 %copy-done.8 = f32[16,128,256]{2,1,0:T(8,128)S(1)} copy-done((f32[16,128,256]{2,1,0:T(8,128)S(1)}, f32[16,128,256]{2,1,0:T(8,128)}, u32[]{:S(2)}) %copy-start.8) | copy-done | bytes 2097176
  77.7 1.6 %copy-done.10 = f32[16,128,256]{2,1,0:T(8,128)S(1)} copy-done((f32[16,128,256]{2,1,0:T(8,128)S(1)}, f32[16,128,256]{2,1,0:T(8,128)}, u32[]{:S(2)}) %copy-start.10) | copy-done | bytes 2097176
  79.3 3.5 %heat.1 = (f32[128,256]{1,0:T(8,128)S(1)}, f32[128,256]{1,0:T(8,128)S(1)}, f32[128,128]{1,0:T(8,128)S(1)}, f32[128,128]{1,0:T(8,128)S(1)}, f32[32,256]{1,0:T(8,1...) custom-call(f32[16,128,256]{2,1,0:T(8,128)S(1)} %copy-done.8, f32[16,128,256]{2,1,0:T(8,128)S(1)} %copy-done.10, ...), custom_call_target="tpu_custom_call" | custom-call | flops 1000000000 | bytes 4194304 | tf_op jit(solution)/shard_map/heat/pallas_call | solution.py:487
  82.8 0.0 collective-permute-start.4
  82.8 2.4 %collective-permute-start.5 = (f32[128,128]{1,0:T(8,128)S(1)}, f32[128,128]{1,0:T(8,128)S(1)}, u32[]{:S(2)}, u32[]{:S(2)}) collective-permute-start(f32[128,128]{1,0:T(8,128)S(1)} %get-tuple-element.32), channel_id=1, source_target_pairs={{8,16},{16,8},{24,32},{32,24},{40,48},{48,40},{56,64},{64,56},{72,... | collective-permute-start | bytes 196616 | tf_op jit(solution)/shard_map/ppermute | solution.py:257
  85.2 5.0 %collective-permute-start.7 = (f32[32,256]{1,0:T(8,128)S(1)}, f32[32,256]{1,0:T(8,128)S(1)}, u32[]{:S(2)}, u32[]{:S(2)}) collective-permute-start(f32[32,256]{1,0:T(8,128)S(1)} %get-tuple-element.34), channel_id=1, source_target_pairs={{1,2},{2,1},{3,4},{4,3},{5,6},{6,5},{9,10},{10,9},{11,12},{12,11},... | collective-permute-start | bytes 98312 | tf_op jit(solution)/shard_map/ppermute | solution.py:263
  90.2 3.8 %collective-permute-done.7.lat_b = f32[32,256]{1,0:T(8,128)S(1)} collective-permute-done((f32[32,256]{1,0:T(8,128)S(1)}, f32[32,256]{1,0:T(8,128)S(1)}, u32[]{:S(2)}, u32[]{:S(2)}) %collective-permute-start.7) | collective-permute-done | bytes 32800 | tf_op jit(solution)/shard_map/ppermute | solution.py:263
  94.0 0.0 collective-permute-done.4.lon_a
  94.0 0.0 collective-permute-done.5.lon_b
  94.0 14.6 %second_step.1 = (f32[16,128,256]{2,1,0:T(8,128)}, f32[16,128,256]{2,1,0:T(8,128)}, f32[16,128,256]{2,1,0:T(8,128)}) custom-call(f32[16,128,256]{2,1,0:T(8,128)S(1)} %copy-done.8, f32[16,128,256]{2,1,0:T(8,128)S(1)} %copy-done.10, f32[128,256]{1,0:T(8,128)S(1)} %get-tuple-element.28.top_ref, f32[128,256]{1,0:T(8,128)S(1)} %get-tuple-element.29.heat_ref, ...), custom_call_target="tpu_custom_call" | custom-call | flops 70000000 | bytes 26214400 | tf_op jit(solution)/shard_map/second_step/pallas_call | solution.py:545
  (21 shorter events, 0.0 us)
Async XLA Ops:
  0.6 24.3 %copy-start.12 = (f32[1,1,256,128]{3,2,1,0:T(8,128)S(1)}, f32[1,1,256,128]{3,2,1,0:T(8,128)}, u32[]{:S(2)}) copy-start(f32[1,1,256,128]{3,2,1,0:T(8,128)} %param.20) | copy-start | bytes 393220
  0.6 24.3 %copy-start.13 = (f32[1,1,256,128]{3,2,1,0:T(8,128)S(1)}, f32[1,1,256,128]{3,2,1,0:T(8,128)}, u32[]{:S(2)}) copy-start(f32[1,1,256,128]{3,2,1,0:T(8,128)} %param.21) | copy-start | bytes 393220
  25.0 9.4 %copy-start = (f32[16,128,256]{2,1,0:T(8,128)S(1)}, f32[16,128,256]{2,1,0:T(8,128)}, u32[]{:S(2)}) copy-start(f32[16,128,256]{2,1,0:T(8,128)} %u_ref.5) | copy-start | bytes 6291460
  27.4 48.7 %all-to-all-start.1 = ((f32[128,8,128]{2,1,0:T(8,128)}), f32[128,8,128]{2,1,0:T(8,128)S(1)}, u32[]{:S(2)}, u32[]{:S(2)}) async-start(f32[128,8,128]{2,1,0:T(8,128)} %bitcast.10), calls=%async_computation.1 | async-start | bytes 1048576 | tf_op jit(solution)/shard_map/all_to_all | solution.py:584
  34.3 1.6 %copy-start.1 = (f32[16,128,256]{2,1,0:T(8,128)S(1)}, f32[16,128,256]{2,1,0:T(8,128)}, u32[]{:S(2)}) copy-start(f32[16,128,256]{2,1,0:T(8,128)} %v_ref.5) | copy-start | bytes 6291460
  35.9 1.6 %copy-start.3 = (f32[16,128,256]{2,1,0:T(8,128)S(1)}, f32[16,128,256]{2,1,0:T(8,128)}, u32[]{:S(2)}) copy-start(f32[16,128,256]{2,1,0:T(8,128)} %k_ref.5) | copy-start | bytes 6291460
  37.5 1.6 %copy-start.5 = (f32[16,128,256]{2,1,0:T(8,128)S(1)}, f32[16,128,256]{2,1,0:T(8,128)}, u32[]{:S(2)}) copy-start(f32[16,128,256]{2,1,0:T(8,128)} %surface_ref.1) | copy-start | bytes 6291460
  39.1 1.6 %copy-start.6 = (f32[16,128,256]{2,1,0:T(8,128)S(1)}, f32[16,128,256]{2,1,0:T(8,128)}, u32[]{:S(2)}) copy-start(f32[16,128,256]{2,1,0:T(8,128)} %s_ref.3) | copy-start | bytes 6291460
  40.7 18.3 %copy-start.11 = (s32[128,256]{1,0:T(8,128)S(1)}, s32[128,256]{1,0:T(8,128)}, u32[]{:S(2)}) copy-start(s32[128,256]{1,0:T(8,128)} %mask_ref.5) | copy-start | bytes 393220
  43.9 8.1 %collective-permute-start = (f32[128,128]{1,0:T(8,128)S(1)}, f32[128,128]{1,0:T(8,128)S(1)}, u32[]{:S(2)}, u32[]{:S(2)}) collective-permute-start(f32[128,128]{1,0:T(8,128)S(1)} %get-tuple-element.20), channel_id=1, source_target_pairs={{0,8},{8,0},{16,24},{24,16},{32,40},{40,32},{48,56},{56,48},{64,72... | collective-permute-start | bytes 196616 | tf_op jit(solution)/shard_map/ppermute | solution.py:256
  44.1 7.8 %collective-permute-start.1 = (f32[128,128]{1,0:T(8,128)S(1)}, f32[128,128]{1,0:T(8,128)S(1)}, u32[]{:S(2)}, u32[]{:S(2)}) collective-permute-start(f32[128,128]{1,0:T(8,128)S(1)} %get-tuple-element.21), channel_id=1, source_target_pairs={{8,16},{16,8},{24,32},{32,24},{40,48},{48,40},{56,64},{64,56},{72,... | collective-permute-start | bytes 196616 | tf_op jit(solution)/shard_map/ppermute | solution.py:257
  49.0 4.3 %collective-permute-start.2 = (f32[64,256]{1,0:T(8,128)S(1)}, f32[64,256]{1,0:T(8,128)S(1)}, u32[]{:S(2)}, u32[]{:S(2)}) collective-permute-start(f32[64,256]{1,0:T(8,128)S(1)} %get-tuple-element.22), channel_id=1, source_target_pairs={{0,1},{1,0},{2,3},{3,2},{4,5},{5,4},{6,7},{7,6},{8,9},{9,8},{10,11... | collective-permute-start | bytes 196616 | tf_op jit(solution)/shard_map/ppermute | solution.py:258
  49.8 9.2 %collective-permute-start.3 = (f32[64,256]{1,0:T(8,128)S(1)}, f32[64,256]{1,0:T(8,128)S(1)}, u32[]{:S(2)}, u32[]{:S(2)}) collective-permute-start(f32[64,256]{1,0:T(8,128)S(1)} %get-tuple-element.23), channel_id=1, source_target_pairs={{1,2},{2,1},{3,4},{4,3},{5,6},{6,5},{9,10},{10,9},{11,12},{12,11},... | collective-permute-start | bytes 196616 | tf_op jit(solution)/shard_map/ppermute | solution.py:263
  73.5 1.3 %copy-start.7 = (f32[16,128,256]{2,1,0:T(8,128)}, f32[16,128,256]{2,1,0:T(8,128)S(1)}, u32[]{:S(2)}) copy-start(f32[16,128,256]{2,1,0:T(8,128)S(1)} %get-tuple-element.24.t_ref) | copy-start | bytes 6291460
  74.8 1.3 %copy-start.9 = (f32[16,128,256]{2,1,0:T(8,128)}, f32[16,128,256]{2,1,0:T(8,128)S(1)}, u32[]{:S(2)}) copy-start(f32[16,128,256]{2,1,0:T(8,128)S(1)} %get-tuple-element.25.s_ref) | copy-start | bytes 6291460
  76.1 1.6 %copy-start.8 = (f32[16,128,256]{2,1,0:T(8,128)S(1)}, f32[16,128,256]{2,1,0:T(8,128)}, u32[]{:S(2)}) copy-start(f32[16,128,256]{2,1,0:T(8,128)} %copy-done.7) | copy-start | bytes 6291460
  77.7 1.6 %copy-start.10 = (f32[16,128,256]{2,1,0:T(8,128)S(1)}, f32[16,128,256]{2,1,0:T(8,128)}, u32[]{:S(2)}) copy-start(f32[16,128,256]{2,1,0:T(8,128)} %copy-done.9) | copy-start | bytes 6291460
  79.3 14.7 %copy-start.2 = (f32[16,128,256]{2,1,0:T(8,128)S(1)}, f32[16,128,256]{2,1,0:T(8,128)}, u32[]{:S(2)}) copy-start(f32[16,128,256]{2,1,0:T(8,128)} %v_ref.5) | copy-start | bytes 6291460
  79.3 14.7 %copy-start.4 = (f32[16,128,256]{2,1,0:T(8,128)S(1)}, f32[16,128,256]{2,1,0:T(8,128)}, u32[]{:S(2)}) copy-start(f32[16,128,256]{2,1,0:T(8,128)} %k_ref.5) | copy-start | bytes 6291460
  82.8 11.2 %collective-permute-start.4 = (f32[128,128]{1,0:T(8,128)S(1)}, f32[128,128]{1,0:T(8,128)S(1)}, u32[]{:S(2)}, u32[]{:S(2)}) collective-permute-start(f32[128,128]{1,0:T(8,128)S(1)} %get-tuple-element.31), channel_id=1, source_target_pairs={{0,8},{8,0},{16,24},{24,16},{32,40},{40,32},{48,56},{56,48},{64,72... | collective-permute-start | bytes 196616 | tf_op jit(solution)/shard_map/ppermute | solution.py:256
  82.8 11.2 %collective-permute-start.5 = (f32[128,128]{1,0:T(8,128)S(1)}, f32[128,128]{1,0:T(8,128)S(1)}, u32[]{:S(2)}, u32[]{:S(2)}) collective-permute-start(f32[128,128]{1,0:T(8,128)S(1)} %get-tuple-element.32), channel_id=1, source_target_pairs={{8,16},{16,8},{24,32},{32,24},{40,48},{48,40},{56,64},{64,56},{72,... | collective-permute-start | bytes 196616 | tf_op jit(solution)/shard_map/ppermute | solution.py:257
  85.2 5.0 %collective-permute-start.6 = (f32[32,256]{1,0:T(8,128)S(1)}, f32[32,256]{1,0:T(8,128)S(1)}, u32[]{:S(2)}, u32[]{:S(2)}) collective-permute-start(f32[32,256]{1,0:T(8,128)S(1)} %get-tuple-element.33), channel_id=1, source_target_pairs={{0,1},{1,0},{2,3},{3,2},{4,5},{5,4},{6,7},{7,6},{8,9},{9,8},{10,11... | collective-permute-start | bytes 98312 | tf_op jit(solution)/shard_map/ppermute | solution.py:258
  85.2 8.8 %collective-permute-start.7 = (f32[32,256]{1,0:T(8,128)S(1)}, f32[32,256]{1,0:T(8,128)S(1)}, u32[]{:S(2)}, u32[]{:S(2)}) collective-permute-start(f32[32,256]{1,0:T(8,128)S(1)} %get-tuple-element.34), channel_id=1, source_target_pairs={{1,2},{2,1},{3,4},{4,3},{5,6},{6,5},{9,10},{10,9},{11,12},{12,11},... | collective-permute-start | bytes 98312 | tf_op jit(solution)/shard_map/ppermute | solution.py:263
where the time goes:
time: 109 us
  Pallas kernels  40.3 us (37%)
  starting transfers between devices  22.3 us (20%)
  blocking collectives  22.2 us (20%)
  local copies, waits for them, and re-layouts  12.2 us (11%)
  waiting for transfers between devices  10.9 us (10%)
    all_to_all x1, blocking collectives, body(): got = lax.all_to_all(request, AXES, split_axis=0, concat_axis=0, tiled=True)  22.2 us
    pallas_call x1, Pallas kernels, second_step(): pl.pallas_call(second_kernel, out_shape=(shape, shape, shape), in_specs=[...  14.6 us
    pallas_call x1, Pallas kernels, first_step(): pl.pallas_call(first_kernel, out_shape=(shape, shape), in_specs=[VM] * 11...  14.5 us
    unnamed x28, local copies, waits for them, and re-layouts  12.2 us
    ppermute x2, waiting for transfers between devices, exchange(): got_lat_b = lax.ppermute(lat_b, AXES, route)  9.6 us
    ppermute x2, starting transfers between devices, exchange(): got_lon_b = lax.ppermute(lon_b, 'lon', ring)  7.24 us
    ppermute x2, starting transfers between devices, exchange(): got_lat_b = lax.ppermute(lat_b, AXES, route)  7.07 us
    all_to_all x1, starting transfers between devices, body(): back = lax.all_to_all(answer, AXES, split_axis=0, concat_axis=0, tiled=True)  6.89 us
  transfers between devices with their start and end apart: 9, of which 3 were waited for; matrix products, arithmetic and copies ran while one was open for 0% of the time, Pallas kernels for 16%

commit v1 on v0

v1 whole, which is shorter than its diff:
```python
import jax
import jax.numpy as jnp
from jax import lax
from jax.experimental import pallas as pl
from jax.experimental.pallas import tpu as pltpu
from jax.sharding import PartitionSpec as P

F32 = jnp.float32
BF16 = jnp.bfloat16
AXES = ("lon", "lat")
BULK = 0.1
SLOTS = 8
GROUP = SLOTS + 1
LEVELS = 16
ROWS = 128
LANES = 128
STRIPS = ROWS // 8
LIMIT = 24 * 1024 * 1024

VM = pl.BlockSpec(memory_space=pltpu.VMEM)
ANY = pl.BlockSpec(memory_space=pl.ANY)


def in_vmem(x):
    return pltpu.with_memory_space_constraint(x, pltpu.VMEM)


def dot(a, b):
    return jnp.dot(a, b, preferred_element_type=F32)


def dot_nt(a, b):
    return lax.dot_general(a, b, (((1,), (1,)), ((), ())), preferred_element_type=F32)


def pieces(x):
    high = x.astype(BF16)
    rest = x - high.astype(F32)
    middle = rest.astype(BF16)
    low = (rest - middle.astype(F32)).astype(BF16)
    return high, middle, low


def pick(onehot, x):
    high, middle, low = pieces(x)
    return dot(onehot, high) + (dot(onehot, middle) + dot(onehot, low))


def iota(shape, dim):
    return lax.broadcasted_iota(jnp.int32, shape, dim)


def roll(x, steps, axis):
    steps = steps % x.shape[axis]
    return x if steps == 0 else pltpu.roll(x, steps, axis)


def as_bf16(flag):
    return flag.astype(F32).astype(BF16)


def make_lists(owner_ref, cell_ref, weight_ref):
    w = weight_ref[...]
    share = w / (w[0:1] + w[1:2])
    before = iota((256, 256), 0)
    after = iota((256, 256), 1)
    perm = as_bf16(before == (after % ROWS) * 2 + after // ROWS)
    lists = jnp.concatenate([owner_ref[...].astype(F32), cell_ref[...].astype(F32)], axis=0)
    lists = dot(lists.astype(BF16), perm)
    share = pick_left(share, perm)
    owner = [lists[m : m + 1].astype(jnp.int32) for m in range(2)]
    cell = [lists[2 + m : 3 + m] for m in range(2)]
    return owner, cell, share


def write_request(owner, cell, share, surface, out_ref, codes_ref):
    device = iota((128, 256), 0)
    named = [as_bf16(device == owner[m]) for m in range(2)]
    earlier = as_bf16(iota((256, 256), 0) < iota((256, 256), 1))
    ones = jnp.ones((256, 256), BF16)
    ahead = [dot(named[0], earlier), dot(named[1], earlier) + dot(named[0], ones)]
    rank = [
        jnp.sum(named[m].astype(F32) * ahead[m], axis=0, keepdims=True).astype(jnp.int32)
        for m in range(2)
    ]
    slot = iota((128, 256), 0)
    ids = sum(
        dot_nt(named[m], jnp.where(slot == rank[m], cell[m], 0.0).astype(BF16)) for m in range(2)
    )
    total = 128 * GROUP
    line = iota((total, 256), 0)
    place = as_bf16(
        (line == owner[0] * GROUP + rank[0]) | (line == owner[1] * GROUP + rank[1])
    )
    id_place = as_bf16(iota((total, 128), 0) == iota((total, 128), 1) * GROUP + SLOTS)
    blocks = jnp.concatenate([surface[:, :LANES], surface[:, LANES:]], axis=0)
    out_ref[...] = pick(place, blocks) + dot(id_place, ids.astype(BF16))
    table = jnp.concatenate(
        [(owner[m] * SLOTS + rank[m]).astype(F32) for m in range(2)]
        + [share, jnp.zeros((124, 256), F32)],
        axis=0,
    )
    codes_ref[...] = jnp.transpose(table)


def pick_left(x, onehot):
    high, middle, low = pieces(x)
    return dot(high, onehot) + (dot(middle, onehot) + dot(low, onehot))


CHUNKS = 4
CHUNK = ROWS // CHUNKS


def request_kernel(owner_ref, cell_ref, weight_ref, t_ref, s_ref, u_ref, v_ref, k_ref,
                   out_ref, codes_ref, lon_a_ref, lon_b_ref, lat_a_ref, lat_b_ref, west_ref,
                   surface_buf, t_buf, s_buf, u_buf, k_buf, v_row, k_row, sems, more_sems):
    last = pl.ds(ROWS - 8, 8)
    first = pltpu.make_async_copy(t_ref.at[0], surface_buf, more_sems.at[0])
    rows = [
        pltpu.make_async_copy(v_ref.at[:, last, :], v_row, more_sems.at[1]),
        pltpu.make_async_copy(k_ref.at[:, last, :], k_row, more_sems.at[2]),
    ]
    eastern = pl.ds(LANES, LANES)

    def chunk_copies(c):
        part = pl.ds(c * CHUNK, CHUNK)
        return [
            pltpu.make_async_copy(t_ref.at[:, part, :], t_buf.at[:, part, :], sems.at[0, c]),
            pltpu.make_async_copy(s_ref.at[:, part, :], s_buf.at[:, part, :], sems.at[1, c]),
            pltpu.make_async_copy(u_ref.at[:, part, eastern], u_buf.at[:, part, :], sems.at[2, c]),
            pltpu.make_async_copy(k_ref.at[:, part, eastern], k_buf.at[:, part, :], sems.at[3, c]),
        ]

    first.start()
    for c in range(CHUNKS):
        for copy in chunk_copies(c):
            copy.start()
    for copy in rows:
        copy.start()
    owner, cell, share = make_lists(owner_ref, cell_ref, weight_ref)
    first.wait()
    write_request(owner, cell, share, surface_buf[...], out_ref, codes_ref)
    odd = is_odd("lon")

    for c in range(CHUNKS):
        for copy in chunk_copies(c):
            copy.wait()

        part = slice(c * CHUNK, (c + 1) * CHUNK)
        west, east = column_edges((t_buf, s_buf), (u_buf, k_buf), part, CHUNK)
        west_ref[part, :] = west
        lon_a_ref[part, :] = jnp.where(odd, west, east)
        lon_b_ref[part, :] = jnp.where(odd, east, west)
    for copy in rows:
        copy.wait()
    south = jnp.concatenate(
        [ref[k, 0:1, :] for ref in (t_buf, s_buf) for k in range(LEVELS)], axis=0
    )
    north = jnp.concatenate(
        [ref[k, ROWS - 1 : ROWS, :] for ref in (t_buf, s_buf) for k in range(LEVELS)], axis=0
    )
    faces = jnp.concatenate(
        [ref[k, 7:8, :] for ref in (v_row, k_row) for k in range(LEVELS)], axis=0
    )
    send_rows(south, north, lat_a_ref, lat_b_ref)
    lat_a_ref[32:64, :] = faces
    lat_b_ref[32:64, :] = faces


def send_rows(south, north, lat_a_ref, lat_b_ref):
    odd = is_odd("lat")
    top = lax.axis_index("lat") == lax.axis_size("lat") - 1
    lat_a_ref[0:32, :] = jnp.where(odd, south, north)
    lat_b_ref[0:32, :] = jnp.where(odd, jnp.where(top, flipped(north), north), south)


def in_hbm(x):
    return pltpu.with_memory_space_constraint(x, pltpu.HBM)


def make_request(owner, cell, weight, fields):
    field = pltpu.VMEM((LEVELS, ROWS, 2 * LANES), F32)
    half = pltpu.VMEM((LEVELS, ROWS, LANES), F32)
    row = pltpu.VMEM((LEVELS, 8, 2 * LANES), F32)
    return pl.pallas_call(
        request_kernel,
        out_shape=(
            pltpu.VMEM((128 * GROUP, LANES), F32),
            pltpu.VMEM((256, LANES), F32),
            pltpu.VMEM((ROWS, LANES), F32),
            pltpu.VMEM((ROWS, LANES), F32),
            pltpu.VMEM((64, 2 * LANES), F32),
            pltpu.VMEM((64, 2 * LANES), F32),
            pltpu.VMEM((ROWS, LANES), F32),
        ),
        grid=(1,),
        in_specs=[pl.BlockSpec((2, 256), lambda i: (0, 0))] * 3 + [ANY] * 5,
        out_specs=(VM,) * 7,
        scratch_shapes=[
            pltpu.VMEM((ROWS, 2 * LANES), F32), field, field, half, half, row, row,
            pltpu.SemaphoreType.DMA((4, CHUNKS)),
            pltpu.SemaphoreType.DMA((3,)),
        ],
        compiler_params=pltpu.CompilerParams(vmem_limit_bytes=LIMIT),
        cost_estimate=pl.CostEstimate(flops=2 * 10**9, bytes_accessed=8 * 2**20, transcendentals=0),
        name="request",
    )(*[in_hbm(x) for x in (owner, cell, weight, *fields)])


def answer_kernel(got_ref, air_ref, wind_ref, *rest):
    out_ref = rest[-1]
    ids = got_ref[pl.ds(SLOTS, 128, stride=GROUP), :].astype(BF16)
    patches = jnp.concatenate([air_ref[...], wind_ref[...]], axis=1)
    high, middle, low = pieces(patches)
    spread = jnp.ones((128, 256), BF16)
    chunk = 128
    for part in range(8):
        line = iota((chunk, 128), 0) + part * chunk
        lane = iota((chunk, 128), 1)
        rows = dot(as_bf16(line // SLOTS == lane), ids)
        rows = jnp.where(lane == line % SLOTS, rows, 0.0)
        wanted = dot(rows.astype(BF16), spread).astype(jnp.int32)
        onehot = as_bf16(wanted == iota((chunk, 256), 1))
        found = dot(onehot, high) + (dot(onehot, middle) + dot(onehot, low))
        for s in range(chunk // SLOTS):
            source = part * (chunk // SLOTS) + s
            cells = got_ref[source * GROUP : source * GROUP + SLOTS, :]
            here = found[s * SLOTS : (s + 1) * SLOTS]
            out_ref[source * SLOTS : (source + 1) * SLOTS, :] = (
                BULK * here[:, LANES:] * (here[:, :LANES] - cells)
            )


def make_answer(got, air, wind, after):
    return pl.pallas_call(
        answer_kernel,
        out_shape=pltpu.VMEM((128 * SLOTS, LANES), F32),
        in_specs=[VM] * 3 + [ANY] * len(after),
        out_specs=VM,
        compiler_params=pltpu.CompilerParams(vmem_limit_bytes=LIMIT),
        cost_estimate=pl.CostEstimate(flops=2 * 10**9, bytes_accessed=2**20, transcendentals=0),
        name="answer",
    )(in_vmem(got), air, wind, *after)


def is_odd(axis):
    return lax.rem(lax.axis_index(axis), 2) == 1


def flipped(x):
    back = as_bf16(iota((256, 256), 0) + iota((256, 256), 1) == 255)
    return pick_left(x, back)


class Columns:
    def __init__(self, rows):
        self.lane = iota((rows, LANES), 1)
        self.west = jnp.zeros((rows, LANES), F32)
        self.east = jnp.zeros((rows, LANES), F32)

    def add_west(self, at, x):
        self.west = jnp.where(self.lane == at, roll(x, at, 1), self.west)

    def add_east(self, at, x):
        self.east = jnp.where(self.lane == at, roll(x, at - 127, 1), self.east)


def column_edges(tracers, extra, rows, count):
    columns = Columns(count)
    for t, ref in enumerate(tracers):
        for k in range(LEVELS):
            columns.add_west(LEVELS * t + k, ref[k, rows, :LANES])
    for t, ref in enumerate(tracers):
        for k in range(LEVELS):
            columns.add_east(LEVELS * t + k, ref[k, rows, LANES:])
    for f, ref in enumerate(extra):
        for k in range(LEVELS):
            columns.add_east(64 + LEVELS * f + k, ref[k, rows, :])
    faces = jnp.where(columns.lane >= 64, columns.east, 0.0)
    tracers_east = jnp.where(columns.lane < 64, columns.east, 0.0)
    u = jnp.where(columns.lane < 80, faces, 0.0)
    d = faces - u
    u = roll(u, -32, 1)
    d = roll(d, -16, 1)
    east = tracers_east + (u + roll(u, 16, 1)) + (d + roll(d, 16, 1))
    return columns.west, east


def swap_pairs(first, count):
    route = []
    for low in range(first, count - 1, 2):
        route += [(low, low + 1), (low + 1, low)]
    return route


def exchange(lon_a, lon_b, lat_a, lat_b):
    n_lon, n_lat = lax.axis_size("lon"), lax.axis_size("lat")
    ring = swap_pairs(1, n_lon) + [(n_lon - 1, 0), (0, n_lon - 1)]
    got_lon_a = lax.ppermute(lon_a, "lon", swap_pairs(0, n_lon))
    got_lon_b = lax.ppermute(lon_b, "lon", ring)
    got_lat_a = lax.ppermute(lat_a, "lat", swap_pairs(0, n_lat))
    route = [
        (i * n_lat + low, i * n_lat + high) for i in range(n_lon) for low, high in swap_pairs(1, n_lat)
    ]
    route += [(i * n_lat + n_lat - 1, (n_lon - 1 - i) * n_lat + n_lat - 1) for i in range(n_lon)]
    got_lat_b = lax.ppermute(lat_b, AXES, route)
    return got_lon_a, got_lon_b, got_lat_a, got_lat_b


def density_of(t, s):
    return t * (-0.25 - 0.04 * t + 0.03 * s) + 0.8 * s


def twice_density(t, s):
    return t * (-0.5 - 0.08 * t + 0.06 * s) + 1.6 * s


def step_strip(strip, last, load, u_ref, v_ref, k_ref, mask_ref, side_ref, north_ref, carry_ref, emit, heat_ref=None):
    rows = pl.ds(strip, 8)
    lane = iota((8, LANES), 1)
    sub = iota((8, LANES), 0)
    first_lane, last_lane = lane == 0, lane == LANES - 1
    row0, row7 = sub == 0, sub == 7
    halves = (slice(0, LANES), slice(LANES, 2 * LANES))
    mask = [mask_ref[rows, h].astype(F32) for h in halves]
    x = [load(t, 0, strip) for t in range(2)]
    rho = [twice_density(x[0][h], x[1][h]) for h in range(2)]
    below = None
    for k in range(LEVELS):
        if k < LEVELS - 1:
            x_next = [load(t, k + 1, strip) for t in range(2)]
            rho_next = [twice_density(x_next[0][h], x_next[1][h]) for h in range(2)]
            mixing = [0.06 + 0.05 * jnp.tanh(rho[h] - rho_next[h]) for h in range(2)]
        u = [u_ref[k, rows, h] for h in halves]
        v = [v_ref[k, rows, h] for h in halves]
        d = [k_ref[k, rows, h] for h in halves]
        pe = [jnp.maximum(u[h], 0.0) + d[h] for h in range(2)]
        ne = [jnp.minimum(u[h], 0.0) - d[h] for h in range(2)]
        pn = [jnp.maximum(v[h], 0.0) + d[h] for h in range(2)]
        nn = [jnp.minimum(v[h], 0.0) - d[h] for h in range(2)]
        above = [None, None]
        new = [None, None]
        for t in range(2):
            at = LEVELS * t + k
            xt = x[t]
            side = side_ref[at, rows, :]
            y = [roll(xt[h], -1, 1) for h in range(2)]
            xe = [
                jnp.where(last_lane, y[1], y[0]),
                jnp.where(last_lane, side, y[1]),
            ]
            east = [pe[h] * xt[h] + ne[h] * xe[h] for h in range(2)]
            z = [roll(east[h], 1, 1) for h in range(2)]
            west = [
                jnp.where(first_lane, side, z[0]),
                jnp.where(first_lane, z[0], z[1]),
            ]
            if last:
                ahead = [jnp.broadcast_to(north_ref[at : at + 1, h], (8, LANES)) for h in halves]
            else:
                ahead = load(t, k, strip + 8)
            xn = [roll(jnp.where(row0, ahead[h], xt[h]), -1, 0) for h in range(2)]
            north = [pn[h] * xt[h] + nn[h] * xn[h] for h in range(2)]
            south = [
                roll(jnp.where(row7, carry_ref[at, :, halves[h]], north[h]), 1, 0) for h in range(2)
            ]
            if not last:
                for h in range(2):
                    carry_ref[at, :, halves[h]] = north[h]
            tend = [(west[h] - east[h]) + (south[h] - north[h]) for h in range(2)]
            if k < LEVELS - 1:
                above[t] = [mixing[h] * (x_next[t][h] - xt[h]) for h in range(2)]
                tend = [tend[h] + above[t][h] for h in range(2)]
            if k > 0:
                tend = [tend[h] - below[t][h] for h in range(2)]
            if heat_ref is not None and t == 0 and k == 0:
                tend = [tend[h] + heat_ref[rows, halves[h]] for h in range(2)]
            new[t] = [xt[h] + mask[h] * tend[h] for h in range(2)]
        emit(k, strip, new)
        below = above
        if k < LEVELS - 1:
            x, rho = x_next, rho_next


def west_fluxes(west, coef, own):
    u = roll(coef, -32, 1)
    d = roll(coef, -64, 1)
    return (jnp.maximum(u, 0.0) + d) * west + (jnp.minimum(u, 0.0) - d) * own


def first_carry(south, faces, load_row, carry_ref):
    for k in range(LEVELS):
        v, d = faces(k), faces(LEVELS + k)
        pn = jnp.maximum(v, 0.0) + d
        nn = jnp.minimum(v, 0.0) - d
        for t in range(2):
            at = LEVELS * t + k
            flux = pn * south(at) + nn * load_row(t, k)
            carry_ref[at] = jnp.broadcast_to(flux, (8, 2 * LANES))


def halo_setup(odd_lon, odd_lat, got, coefs, own_ref, load_row, carry_ref, side_ref, north_ref):
    lon_a, lon_b, lat_a, lat_b = got
    c_lon_a, c_lon_b, c_lat_a, c_lat_b = coefs
    west = jnp.where(odd_lon, lon_a[...], lon_b[...])
    coef = jnp.where(odd_lon, c_lon_a[...], c_lon_b[...])
    flux = west_fluxes(west, coef, own_ref[...])
    east = jnp.where(odd_lon, lon_b[...], lon_a[...])
    last_lane = iota((ROWS, LANES), 1) == LANES - 1
    for at in range(2 * LEVELS):
        side_ref[at] = jnp.where(last_lane, roll(east, 127 - at, 1), roll(flux, -at, 1))
    north_ref[...] = jnp.where(odd_lat, lat_b[0:32, :], lat_a[0:32, :])

    def south(at):
        return jnp.where(odd_lat, lat_a[at : at + 1, :], lat_b[at : at + 1, :])

    def faces(at):
        return jnp.where(odd_lat, c_lat_a[32 + at : 33 + at, :], c_lat_b[32 + at : 33 + at, :])

    first_carry(south, faces, load_row, carry_ref)


def pair_loader(refs, top_ref=None):
    def load(t, k, strip):
        rows = pl.ds(strip, 8)
        if t == 0 and k == 0 and top_ref is not None:
            return [top_ref[rows, :LANES], top_ref[rows, LANES:]]
        return [refs[t][k, rows, :LANES], refs[t][k, rows, LANES:]]

    def load_row(t, k):
        if t == 0 and k == 0 and top_ref is not None:
            return top_ref[0:1, :]
        return refs[t][k, 0:1, :]

    return load, load_row


def strips(body):
    def one(i, carry):
        body(pl.multiple_of(i * 8, 8), False)
        return carry

    lax.fori_loop(0, ROWS // 8 - 1, one, 0)
    body(ROWS - 8, True)


def first_kernel(t_hbm, s_hbm, u_hbm, v_hbm, k_hbm, mask_hbm, own_ref, lon_a, lon_b, lat_a, lat_b,
                 t_out, s_out, top_out, west_out, east_out, south_out, north_out,
                 carry_ref, side_ref, north_ref,
                 t_ref, s_ref, u_ref, v_ref, k_ref, t_new, s_new, mask_ref, sems, out_sems):
    sources = (t_hbm, s_hbm, u_hbm, v_hbm, k_hbm)
    bufs = (t_ref, s_ref, u_ref, v_ref, k_ref)
    new_bufs = (t_new, s_new)
    outs = (t_out, s_out)

    def copy_in(f, index):
        rows = pl.ds(pl.multiple_of(index * 8, 8), 8)
        return pltpu.make_async_copy(sources[f].at[:, rows, :], bufs[f].at[:, rows, :], sems.at[f, index])

    def copy_out(t, index):
        rows = pl.ds(pl.multiple_of(index * 8, 8), 8)
        return pltpu.make_async_copy(new_bufs[t].at[:, rows, :], outs[t].at[:, rows, :], out_sems.at[t, index])

    def start(index, carry):
        for f in range(5):
            copy_in(f, index).start()
        return carry

    mask_copy = pltpu.make_async_copy(mask_hbm, mask_ref, sems.at[5, 0])
    start(0, 0)
    mask_copy.start()
    lax.fori_loop(1, STRIPS, start, 0)
    copy_in(0, 0).wait()
    copy_in(1, 0).wait()
    load, load_row = pair_loader((t_ref, s_ref))
    got = (lon_a, lon_b, lat_a, lat_b)
    halo_setup(is_odd("lon"), is_odd("lat"), got, got, own_ref, load_row, carry_ref, side_ref, north_ref)
    mask_copy.wait()

    def body(strip, last):
        index = STRIPS - 1 if last else strip // 8
        for f in range(2, 5):
            copy_in(f, index).wait()
        if not last:
            for f in range(2):
                copy_in(f, index + 1).wait()
        columns = Columns(8)

        def emit(k, strip, new):
            rows = pl.ds(strip, 8)
            for t in range(2):
                for h in range(2):
                    new_bufs[t][k, rows, h * LANES : (h + 1) * LANES] = new[t][h]
                    if t == 0 and k == 0:
                        top_out[rows, h * LANES : (h + 1) * LANES] = new[t][h]
                columns.add_west(LEVELS * t + k, new[t][0])
                columns.add_east(LEVELS * t + k, new[t][1])

        step_strip(strip, last, load, u_ref, v_ref, k_ref, mask_ref, side_ref, north_ref, carry_ref, emit)
        west_out[pl.ds(strip, 8), :] = columns.west
        east_out[pl.ds(strip, 8), :] = columns.east
        for t in range(2):
            copy_out(t, index).start()

    strips(body)
    south_out[...] = jnp.concatenate([ref[k, 0:1, :] for ref in new_bufs for k in range(LEVELS)], axis=0)
    north_out[...] = jnp.concatenate(
        [ref[k, ROWS - 1 : ROWS, :] for ref in new_bufs for k in range(LEVELS)], axis=0
    )

    def finish(index, carry):
        for t in range(2):
            copy_out(t, index).wait()
        return carry

    lax.fori_loop(0, STRIPS, finish, 0)


STEP_SCRATCH = [
    pltpu.VMEM((2 * LEVELS, 8, 2 * LANES), F32),
    pltpu.VMEM((2 * LEVELS, ROWS, LANES), F32),
    pltpu.VMEM((2 * LEVELS, 2 * LANES), F32),
]
STEP_COST = pl.CostEstimate(flops=7 * 10**7, bytes_accessed=25 * 2**20, transcendentals=10**6)


def first_step(fields, mask, own, got):
    shape = pltpu.HBM((LEVELS, ROWS, 2 * LANES), F32)
    buf = pltpu.VMEM((LEVELS, ROWS, 2 * LANES), F32)
    return pl.pallas_call(
        first_kernel,
        out_shape=(
            shape,
            shape,
            pltpu.VMEM((ROWS, 2 * LANES), F32),
            pltpu.VMEM((ROWS, LANES), F32),
            pltpu.VMEM((ROWS, LANES), F32),
            pltpu.VMEM((2 * LEVELS, 2 * LANES), F32),
            pltpu.VMEM((2 * LEVELS, 2 * LANES), F32),
        ),
        in_specs=[ANY] * 6 + [VM] * 5,
        out_specs=(ANY, ANY) + (VM,) * 5,
        scratch_shapes=STEP_SCRATCH
        + [buf] * 7
        + [pltpu.VMEM((ROWS, 2 * LANES), jnp.int32), pltpu.SemaphoreType.DMA((6, STRIPS)), pltpu.SemaphoreType.DMA((2, STRIPS))],
        compiler_params=pltpu.CompilerParams(vmem_limit_bytes=LIMIT),
        cost_estimate=STEP_COST,
        name="first_step",
    )(*[in_hbm(x) for x in fields], in_hbm(mask), own, *got)


def heat_kernel(top_ref, west_ref, east_ref, south_ref, north_ref, mask_hbm, back_ref, codes_ref,
                heat_out, top_out, lon_a_ref, lon_b_ref, lat_a_ref, lat_b_ref, own_out, mask_ref, sem):
    mask_copy = pltpu.make_async_copy(mask_hbm, mask_ref, sem)
    mask_copy.start()
    high, middle, low = pieces(back_ref[...])
    codes = codes_ref[...]
    lane = iota((256, 1024), 1)
    heat = None
    for m in range(2):
        onehot = as_bf16(codes[:, m : m + 1].astype(jnp.int32) == lane)
        flux = dot(onehot, high) + (dot(onehot, middle) + dot(onehot, low))
        part = codes[:, 2 + m : 3 + m] * flux
        heat = part if heat is None else heat + part
    mask_copy.wait()
    mask = mask_ref[...].astype(F32)
    added = []
    for h in range(2):
        cols = slice(h * LANES, (h + 1) * LANES)
        here = heat[h * ROWS : (h + 1) * ROWS]
        heat_out[:, cols] = here
        added.append(mask[:, cols] * here)
        top_out[:, cols] = top_ref[:, cols] + added[h]
    first = iota((ROWS, LANES), 1) == 0
    west = west_ref[...] + jnp.where(first, added[0], 0.0)
    east = east_ref[...] + jnp.where(first, roll(added[1], 1, 1), 0.0)
    own_out[...] = west
    odd = is_odd("lon")
    lon_a_ref[...] = jnp.where(odd, west, east)
    lon_b_ref[...] = jnp.where(odd, east, west)
    south = jnp.concatenate([top_out[0:1, :], south_ref[1:, :]], axis=0)
    north = jnp.concatenate([top_out[ROWS - 1 : ROWS, :], north_ref[1:, :]], axis=0)
    send_rows(south, north, lat_a_ref, lat_b_ref)


def add_heat(top, west, east, south, north, mask, back, codes):
    return pl.pallas_call(
        heat_kernel,
        out_shape=(
            pltpu.VMEM((ROWS, 2 * LANES), F32),
            pltpu.VMEM((ROWS, 2 * LANES), F32),
            pltpu.VMEM((ROWS, LANES), F32),
            pltpu.VMEM((ROWS, LANES), F32),
            pltpu.VMEM((32, 2 * LANES), F32),
            pltpu.VMEM((32, 2 * LANES), F32),
            pltpu.VMEM((ROWS, LANES), F32),
        ),
        in_specs=[VM] * 5 + [ANY] + [VM] * 2,
        out_specs=(VM,) * 7,
        scratch_shapes=[pltpu.VMEM((ROWS, 2 * LANES), jnp.int32), pltpu.SemaphoreType.DMA],
        compiler_params=pltpu.CompilerParams(vmem_limit_bytes=LIMIT),
        cost_estimate=pl.CostEstimate(flops=10**9, bytes_accessed=2**20, transcendentals=0),
        name="heat",
    )(*[in_vmem(x) for x in (top, west, east, south, north)], in_hbm(mask), in_vmem(back), in_vmem(codes))


def second_kernel(t_hbm, s_hbm, u_hbm, v_hbm, k_hbm, mask_hbm, top_ref, heat_ref, own_ref,
                  lon_a, lon_b, lat_a, lat_b, c_lon_a, c_lon_b, c_lat_a, c_lat_b,
                  t_out, s_out, rho_out,
                  carry_ref, side_ref, north_ref,
                  t_ref, s_ref, u_ref, v_ref, k_ref, t_buf, s_buf, rho_buf, mask_ref, in_sems, sems):
    sources = (t_hbm, s_hbm, u_hbm, v_hbm, k_hbm)
    held = (t_ref, s_ref, u_ref, v_ref, k_ref)

    def copy_in(t, index):
        rows = pl.ds(pl.multiple_of(index * 8, 8), 8)
        return pltpu.make_async_copy(sources[t].at[:, rows, :], held[t].at[:, rows, :], in_sems.at[t, index])

    def start(index, carry):
        for f in range(5):
            copy_in(f, index).start()
        return carry

    mask_copy = pltpu.make_async_copy(mask_hbm, mask_ref, in_sems.at[5, 0])
    start(0, 0)
    mask_copy.start()
    lax.fori_loop(1, STRIPS, start, 0)
    copy_in(0, 0).wait()
    copy_in(1, 0).wait()
    load, load_row = pair_loader((t_ref, s_ref), top_ref)
    halo_setup(is_odd("lon"), is_odd("lat"), (lon_a, lon_b, lat_a, lat_b), (c_lon_a, c_lon_b, c_lat_a, c_lat_b),
               own_ref, load_row, carry_ref, side_ref, north_ref)
    mask_copy.wait()
    bufs = (t_buf, s_buf, rho_buf)
    outs = (t_out, s_out, rho_out)

    def emit(k, strip, new):
        for h in range(2):
            at = (k, pl.ds(strip, 8), slice(h * LANES, (h + 1) * LANES))
            for t in range(2):
                bufs[t][at] = new[t][h]
            rho_buf[at] = density_of(new[0][h], new[1][h])

    def copies(index):
        rows = pl.ds(pl.multiple_of(index * 8, 8), 8)
        return [
            pltpu.make_async_copy(bufs[n].at[:, rows, :], outs[n].at[:, rows, :], sems.at[n, index])
            for n in range(3)
        ]

    def body(strip, last):
        index = STRIPS - 1 if last else strip // 8
        for f in range(2, 5):
            copy_in(f, index).wait()
        if not last:
            for t in range(2):
                copy_in(t, index + 1).wait()
        step_strip(strip, last, load, u_ref, v_ref, k_ref, mask_ref, side_ref, north_ref, carry_ref, emit, heat_ref)
        for copy in copies(index):
            copy.start()

    strips(body)

    def finish(index, carry):
        for copy in copies(index):
            copy.wait()
        return carry

    lax.fori_loop(0, STRIPS, finish, 0)


def second_step(t, s, fields, mask, top, heat, own, got, coefs):
    shape = jax.ShapeDtypeStruct((LEVELS, ROWS, 2 * LANES), F32)
    buf = pltpu.VMEM((LEVELS, ROWS, 2 * LANES), F32)
    return pl.pallas_call(
        second_kernel,
        out_shape=(shape, shape, shape),
        in_specs=[ANY] * 6 + [VM] * 11,
        out_specs=(ANY, ANY, ANY),
        scratch_shapes=STEP_SCRATCH
        + [buf] * 8
        + [pltpu.VMEM((ROWS, 2 * LANES), jnp.int32), pltpu.SemaphoreType.DMA((6, STRIPS)), pltpu.SemaphoreType.DMA((3, STRIPS))],
        compiler_params=pltpu.CompilerParams(vmem_limit_bytes=LIMIT),
        cost_estimate=STEP_COST,
        name="second_step",
    )(in_hbm(t), in_hbm(s), *[in_hbm(x) for x in fields], in_hbm(mask), in_vmem(top), in_vmem(heat), in_vmem(own), *[in_vmem(g) for g in got], *coefs)


def body(
    temp,
    salt,
    east_face_velocity,
    v_face,
    kappa,
    land_mask,
    margin_owner_device,
    margin_cell,
    margin_weight,
    air_temp,
    wind_speed,
):
    def lists(x):
        return jnp.transpose(x.reshape(256, 2))

    fields = (temp, salt, east_face_velocity, v_face, kappa)
    request, codes, *sent, own = make_request(
        lists(margin_owner_device), lists(margin_cell), lists(margin_weight), fields
    )
    request = request.reshape(128, 1, GROUP * LANES)
    got = lax.all_to_all(request, AXES, split_axis=0, concat_axis=0, tiled=True)
    got = got.reshape(128 * GROUP, LANES)
    halos = [in_vmem(g) for g in exchange(*sent)]
    answer = make_answer(got, air_temp.reshape(256, LANES), wind_speed.reshape(256, LANES), halos)
    back = lax.all_to_all(answer, AXES, split_axis=0, concat_axis=0, tiled=True)
    t1, s1, *edges = first_step(fields, land_mask, in_vmem(own), halos)
    heat, top, *sent, own = add_heat(*edges, land_mask, back, codes)
    later = exchange(*sent)
    return second_step(t1, s1, fields[2:], land_mask, top, heat, own, later, halos)


def solution(mesh):
    grid = P(None, "lat", "lon")
    lists = P("lat", "lon", None, None)
    owned = P("lon", "lat", None, None)
    in_specs = (grid,) * 5 + (P("lat", "lon"),) + (lists,) * 3 + (owned,) * 2
    return jax.shard_map(body, mesh=mesh, in_specs=in_specs, out_specs=(grid,) * 3, check_vma=False)
```

time: 109 us -> 79.3 us (0.73)
  blocking collectives: 22.2 us -> 0 us
  local copies, waits for them, and re-layouts: 12.2 us -> 0.01 us
  starting transfers between devices: 22.3 us -> 32.5 us
  Pallas kernels: 40.3 us -> 31.4 us
  waiting for transfers between devices: 10.9 us -> 14.2 us
    all_to_all x1 -> x0, blocking collectives: 22.2 us -> none  [body(): got = lax.all_to_all(request, AXES, split_axis=0, concat_axis=0, tiled=True)]
    unnamed x28 -> x4, local copies, waits for them, and re-layouts: 12.2 us -> 0.01 us
    all_to_all x0 -> x1, starting transfers between devices: none -> 10.2 us  [body(): got = lax.all_to_all(request, AXES, split_axis=0, concat_axis=0, tiled=True)]
    pallas_call x2 -> x1, Pallas kernels: 17.6 us -> 10.6 us  [first_step(): pl.pallas_call(first_kernel, out_shape=(shape, shape, pltpu.VMEM((ROWS, 2...]
    ppermute x2, waiting for transfers between devices: 0.01 us -> 4.81 us  [exchange(): got_lon_b = lax.ppermute(lon_b, 'lon', ring)]
    pallas_call x1, Pallas kernels: 14.6 us -> 9.95 us  [second_step(): pl.pallas_call(second_kernel, out_shape=(shape, shape, shape), in_specs=[...]
    pallas_call x1, Pallas kernels: 2.13 us -> 6.42 us  [make_request(): pl.pallas_call(request_kernel, out_shape=(pltpu.VMEM((128 * GROUP, LANES)...]
    ppermute x2, starting transfers between devices: 7.07 us -> 4.71 us  [exchange(): got_lat_b = lax.ppermute(lat_b, AXES, route)]
  transfers between devices with their start and end apart: 9 -> 10, of which waited for: 3 -> 5; matrix products, arithmetic and copies ran while one was open for 0% -> 0% of each run, Pallas kernels for 16% -> 13%
where the time goes in v1:
time: 79.3 us; the launch traced here: 78.9 us
  starting transfers between devices  32.5 us (41%)
  Pallas kernels  31.4 us (40%)
  waiting for transfers between devices  14.2 us (18%)
    pallas_call x1, Pallas kernels, first_step(): pl.pallas_call(first_kernel, out_shape=(shape, shape, pltpu.VMEM((ROWS, 2...  10.6 us
    all_to_all x1, starting transfers between devices, body(): got = lax.all_to_all(request, AXES, split_axis=0, concat_axis=0, tiled=True)  10.2 us
    pallas_call x1, Pallas kernels, second_step(): pl.pallas_call(second_kernel, out_shape=(shape, shape, shape), in_specs=[...  9.95 us
    ppermute x2, starting transfers between devices, exchange(): got_lon_b = lax.ppermute(lon_b, 'lon', ring)  9.02 us
    ppermute x2, waiting for transfers between devices, exchange(): got_lat_b = lax.ppermute(lat_b, AXES, route)  8.03 us
    all_to_all x1, starting transfers between devices, body(): back = lax.all_to_all(answer, AXES, split_axis=0, concat_axis=0, tiled=True)  6.56 us
    pallas_call x1, Pallas kernels, make_request(): pl.pallas_call(request_kernel, out_shape=(pltpu.VMEM((128 * GROUP, LANES)...  6.42 us
    ppermute x2, waiting for transfers between devices, exchange(): got_lon_b = lax.ppermute(lon_b, 'lon', ring)  4.81 us
  transfers between devices with their start and end apart: 10, of which 5 were waited for; matrix products, arithmetic and copies ran while one was open for 0% of the time, Pallas kernels for 13%

profile of v1, /device:TPU:38, one launch (start us, length us, event | category | flops | bytes accessed | tf_op | source)
XLA Modules:
  0.0 78.9 jit_solution(1099596591474285330)
XLA Ops:
  0.6 0.0 copy-start
  0.6 0.0 copy-start.1
  0.7 6.4 %request.1 = (f32[1152,128]{1,0:T(8,128)}, f32[256,128]{1,0:T(8,128)S(1)}, f32[128,128]{1,0:T(8,128)S(1)}, f32[128,128]{1,0:T(8,128)S(1)}, f32[64,256]{1,0:T(8,1...) custom-call(s32[2,256]{1,0:T(2,128)} %bitcast.19, s32[2,256]{1,0:T(2,128)} %bitcast.20, f32[2,256]{1,0:T(2,128)} %bitcast.21, ...), custom_call_target="tpu_custom_call" | custom-call | flops 2000000000 | bytes 8388608 | tf_op jit(solution)/shard_map/request/pallas_call | solution.py:186
  7.1 10.2 %all-to-all-start = ((f32[128,1,1152]{2,1,0:T(1,128)}), f32[128,1,1152]{2,1,0:T(1,128)S(1)}, u32[]{:S(2)}, u32[]{:S(2)}) async-start(f32[128,1,1152]{2,1,0:T(1,128)} %bitcast.6), calls=%async_computation | async-start | bytes 1179648 | tf_op jit(solution)/shard_map/all_to_all | solution.py:711
  17.3 0.2 collective-permute-start
  17.5 4.9 %collective-permute-start.1 = (f32[128,128]{1,0:T(8,128)S(1)}, f32[128,128]{1,0:T(8,128)S(1)}, u32[]{:S(2)}, u32[]{:S(2)}) collective-permute-start(f32[128,128]{1,0:T(8,128)S(1)} %get-tuple-element.26), channel_id=1, source_target_pairs={{8,16},{16,8},{24,32},{32,24},{40,48},{48,40},{56,64},{64,56},{72,... | collective-permute-start | bytes 196616 | tf_op jit(solution)/shard_map/ppermute | solution.py:301
  22.4 0.8 %collective-permute-start.2 = (f32[64,256]{1,0:T(8,128)S(1)}, f32[64,256]{1,0:T(8,128)S(1)}, u32[]{:S(2)}, u32[]{:S(2)}) collective-permute-start(f32[64,256]{1,0:T(8,128)S(1)} %get-tuple-element.27), channel_id=1, source_target_pairs={{0,1},{1,0},{2,3},{3,2},{4,5},{5,4},{6,7},{7,6},{8,9},{9,8},{10,11... | collective-permute-start | bytes 196616 | tf_op jit(solution)/shard_map/ppermute | solution.py:302
  23.2 2.1 %collective-permute-start.3 = (f32[64,256]{1,0:T(8,128)S(1)}, f32[64,256]{1,0:T(8,128)S(1)}, u32[]{:S(2)}, u32[]{:S(2)}) collective-permute-start(f32[64,256]{1,0:T(8,128)S(1)} %get-tuple-element.28), channel_id=1, source_target_pairs={{1,2},{2,1},{3,4},{4,3},{5,6},{6,5},{9,10},{10,9},{11,12},{12,11},... | collective-permute-start | bytes 196616 | tf_op jit(solution)/shard_map/ppermute | solution.py:307
  25.3 0.0 collective-permute-done.lon_a.rest_0_.c_lon_a
  25.3 4.8 %collective-permute-done.1.lon_b.rest_1_.c_lon_b = f32[128,128]{1,0:T(8,128)S(1)} collective-permute-done((f32[128,128]{1,0:T(8,128)S(1)}, f32[128,128]{1,0:T(8,128)S(1)}, u32[]{:S(2)}, u32[]{:S(2)}) %collective-permute-start.1) | collective-permute-done | bytes 65568 | tf_op jit(solution)/shard_map/ppermute | solution.py:301
  30.1 0.0 collective-permute-done.2.lat_a.rest_2_.c_lat_a
  30.2 2.3 %collective-permute-done.3.lat_b.rest_3_.c_lat_b = f32[64,256]{1,0:T(8,128)S(1)} collective-permute-done((f32[64,256]{1,0:T(8,128)S(1)}, f32[64,256]{1,0:T(8,128)S(1)}, u32[]{:S(2)}, u32[]{:S(2)}) %collective-permute-start.3) | collective-permute-done | bytes 65568 | tf_op jit(solution)/shard_map/ppermute | solution.py:307
  32.4 0.0 all-to-all-done
  32.4 0.0 copy-done
  32.4 0.0 copy-done.1
  32.4 2.5 %answer.1 = f32[1024,128]{1,0:T(8,128)} custom-call(f32[1152,128]{1,0:T(8,128)S(1)} %bitcast.15, f32[256,128]{1,0:T(8,128)S(1)} %bitcast.17, f32[256,128]{1,0:T(8,128)S(1)} %bitcast.18, f32[128,128]{1,0:T(8,128)S(1)} %collective-permute-done.lon_a.rest_0_.c_lon_a, f32[128,128]{1,0:T(8,128)S(1)} %collective-permute-done.1.lon_b.rest_1_.c_lon_b, ...), custom_call_target="tpu_custom_call" | custom-call | flops 2000000000 | bytes 1048576 | tf_op jit(solution)/shard_map/answer/pallas_call | solution.py:236
  34.9 6.6 %all-to-all-start.1 = ((f32[128,8,128]{2,1,0:T(8,128)}), f32[128,8,128]{2,1,0:T(8,128)S(1)}, u32[]{:S(2)}, u32[]{:S(2)}) async-start(f32[128,8,128]{2,1,0:T(8,128)} %bitcast.10), calls=%async_computation.1 | async-start | bytes 1048576 | tf_op jit(solution)/shard_map/all_to_all | solution.py:715
  41.5 10.6 %first_step.1 = (f32[16,128,256]{2,1,0:T(8,128)}, f32[16,128,256]{2,1,0:T(8,128)}, f32[128,256]{1,0:T(8,128)S(1)}, f32[128,128]{1,0:T(8,128)S(1)}, f32[128,128]{...) custom-call(f32[16,128,256]{2,1,0:T(8,128)} %t_hbm.1, f32[16,128,256]{2,1,0:T(8,128)} %s_hbm.1, ...), custom_call_target="tpu_custom_call" | custom-call | flops 70000000 | bytes 26214400 | tf_op jit(solution)/shard_map/first_step/pallas_call | solution.py:531
  52.0 0.9 %all-to-all-done.1 = f32[128,8,128]{2,1,0:T(8,128)S(1)} async-done(((f32[128,8,128]{2,1,0:T(8,128)}), f32[128,8,128]{2,1,0:T(8,128)S(1)}, u32[]{:S(2)}, u32[]{:S(2)}) %all-to-all-start.1) | async-done | bytes 524320 | tf_op jit(solution)/shard_map/all_to_all | solution.py:715
  52.9 2.0 %heat.1 = (f32[128,256]{1,0:T(8,128)S(1)}, f32[128,256]{1,0:T(8,128)S(1)}, f32[128,128]{1,0:T(8,128)S(1)}, f32[128,128]{1,0:T(8,128)S(1)}, f32[32,256]{1,0:T(8,1...) custom-call(f32[128,256]{1,0:T(8,128)S(1)} %get-tuple-element.31.top_ref, ...), custom_call_target="tpu_custom_call" | custom-call | flops 1000000000 | bytes 1048576 | tf_op jit(solution)/shard_map/heat/pallas_call | solution.py:588
  55.0 0.1 collective-permute-start.4
  55.1 4.1 %collective-permute-start.5 = (f32[128,128]{1,0:T(8,128)S(1)}, f32[128,128]{1,0:T(8,128)S(1)}, u32[]{:S(2)}, u32[]{:S(2)}) collective-permute-start(f32[128,128]{1,0:T(8,128)S(1)} %get-tuple-element.42), channel_id=1, source_target_pairs={{8,16},{16,8},{24,32},{32,24},{40,48},{48,40},{56,64},{64,56},{72,... | collective-permute-start | bytes 196616 | tf_op jit(solution)/shard_map/ppermute | solution.py:301
  59.2 0.8 %collective-permute-start.6 = (f32[32,256]{1,0:T(8,128)S(1)}, f32[32,256]{1,0:T(8,128)S(1)}, u32[]{:S(2)}, u32[]{:S(2)}) collective-permute-start(f32[32,256]{1,0:T(8,128)S(1)} %get-tuple-element.43), channel_id=1, source_target_pairs={{0,1},{1,0},{2,3},{3,2},{4,5},{5,4},{6,7},{7,6},{8,9},{9,8},{10,11... | collective-permute-start | bytes 98312 | tf_op jit(solution)/shard_map/ppermute | solution.py:302
  60.1 2.6 %collective-permute-start.7 = (f32[32,256]{1,0:T(8,128)S(1)}, f32[32,256]{1,0:T(8,128)S(1)}, u32[]{:S(2)}, u32[]{:S(2)}) collective-permute-start(f32[32,256]{1,0:T(8,128)S(1)} %get-tuple-element.44), channel_id=1, source_target_pairs={{1,2},{2,1},{3,4},{4,3},{5,6},{6,5},{9,10},{10,9},{11,12},{12,11},... | collective-permute-start | bytes 98312 | tf_op jit(solution)/shard_map/ppermute | solution.py:307
  62.7 0.4 collective-permute-done.6.lat_a
  63.1 5.8 %collective-permute-done.7.lat_b = f32[32,256]{1,0:T(8,128)S(1)} collective-permute-done((f32[32,256]{1,0:T(8,128)S(1)}, f32[32,256]{1,0:T(8,128)S(1)}, u32[]{:S(2)}, u32[]{:S(2)}) %collective-permute-start.7) | collective-permute-done | bytes 32800 | tf_op jit(solution)/shard_map/ppermute | solution.py:307
  68.9 0.0 collective-permute-done.4.lon_a
  68.9 0.0 collective-permute-done.5.lon_b
  68.9 9.9 %second_step.1 = (f32[16,128,256]{2,1,0:T(8,128)}, f32[16,128,256]{2,1,0:T(8,128)}, f32[16,128,256]{2,1,0:T(8,128)}) custom-call(f32[16,128,256]{2,1,0:T(8,128)} %get-tuple-element.29.t_hbm, f32[16,128,256]{2,1,0:T(8,128)} %get-tuple-element.30.s_hbm, f32[16,128,256]{2,1,0:T(8,128)} %u_hbm.3, f32[16,128,256]{2,1,0:T(8,128)} %v_hbm.3, f32[16,128,256]{2,1,0:T(8,128)} %k_hbm.3, ...), custom_call_target="tpu_custom_call" | custom-call | flops 70000000 | bytes 26214400 | tf_op jit(solution)/shard_map/second_step/pallas_call | solution.py:676
Async XLA Ops:
  0.6 31.8 %copy-start = (f32[1,1,256,128]{3,2,1,0:T(8,128)S(1)}, f32[1,1,256,128]{3,2,1,0:T(8,128)}, u32[]{:S(2)}) copy-start(f32[1,1,256,128]{3,2,1,0:T(8,128)} %param.20) | copy-start | bytes 393220
  0.6 31.8 %copy-start.1 = (f32[1,1,256,128]{3,2,1,0:T(8,128)S(1)}, f32[1,1,256,128]{3,2,1,0:T(8,128)}, u32[]{:S(2)}) copy-start(f32[1,1,256,128]{3,2,1,0:T(8,128)} %param.21) | copy-start | bytes 393220
  7.1 25.3 %all-to-all-start = ((f32[128,1,1152]{2,1,0:T(1,128)}), f32[128,1,1152]{2,1,0:T(1,128)S(1)}, u32[]{:S(2)}, u32[]{:S(2)}) async-start(f32[128,1,1152]{2,1,0:T(1,128)} %bitcast.6), calls=%async_computation | async-start | bytes 1179648 | tf_op jit(solution)/shard_map/all_to_all | solution.py:711
  17.3 8.1 %collective-permute-start = (f32[128,128]{1,0:T(8,128)S(1)}, f32[128,128]{1,0:T(8,128)S(1)}, u32[]{:S(2)}, u32[]{:S(2)}) collective-permute-start(f32[128,128]{1,0:T(8,128)S(1)} %get-tuple-element.25), channel_id=1, source_target_pairs={{0,8},{8,0},{16,24},{24,16},{32,40},{40,32},{48,56},{56,48},{64,72... | collective-permute-start | bytes 196616 | tf_op jit(solution)/shard_map/ppermute | solution.py:300
  17.5 12.6 %collective-permute-start.1 = (f32[128,128]{1,0:T(8,128)S(1)}, f32[128,128]{1,0:T(8,128)S(1)}, u32[]{:S(2)}, u32[]{:S(2)}) collective-permute-start(f32[128,128]{1,0:T(8,128)S(1)} %get-tuple-element.26), channel_id=1, source_target_pairs={{8,16},{16,8},{24,32},{32,24},{40,48},{48,40},{56,64},{64,56},{72,... | collective-permute-start | bytes 196616 | tf_op jit(solution)/shard_map/ppermute | solution.py:301
  22.4 7.8 %collective-permute-start.2 = (f32[64,256]{1,0:T(8,128)S(1)}, f32[64,256]{1,0:T(8,128)S(1)}, u32[]{:S(2)}, u32[]{:S(2)}) collective-permute-start(f32[64,256]{1,0:T(8,128)S(1)} %get-tuple-element.27), channel_id=1, source_target_pairs={{0,1},{1,0},{2,3},{3,2},{4,5},{5,4},{6,7},{7,6},{8,9},{9,8},{10,11... | collective-permute-start | bytes 196616 | tf_op jit(solution)/shard_map/ppermute | solution.py:302
  23.2 9.2 %collective-permute-start.3 = (f32[64,256]{1,0:T(8,128)S(1)}, f32[64,256]{1,0:T(8,128)S(1)}, u32[]{:S(2)}, u32[]{:S(2)}) collective-permute-start(f32[64,256]{1,0:T(8,128)S(1)} %get-tuple-element.28), channel_id=1, source_target_pairs={{1,2},{2,1},{3,4},{4,3},{5,6},{6,5},{9,10},{10,9},{11,12},{12,11},... | collective-permute-start | bytes 196616 | tf_op jit(solution)/shard_map/ppermute | solution.py:307
  34.9 18.1 %all-to-all-start.1 = ((f32[128,8,128]{2,1,0:T(8,128)}), f32[128,8,128]{2,1,0:T(8,128)S(1)}, u32[]{:S(2)}, u32[]{:S(2)}) async-start(f32[128,8,128]{2,1,0:T(8,128)} %bitcast.10), calls=%async_computation.1 | async-start | bytes 1048576 | tf_op jit(solution)/shard_map/all_to_all | solution.py:715
  55.0 13.9 %collective-permute-start.4 = (f32[128,128]{1,0:T(8,128)S(1)}, f32[128,128]{1,0:T(8,128)S(1)}, u32[]{:S(2)}, u32[]{:S(2)}) collective-permute-start(f32[128,128]{1,0:T(8,128)S(1)} %get-tuple-element.41), channel_id=1, source_target_pairs={{0,8},{8,0},{16,24},{24,16},{32,40},{40,32},{48,56},{56,48},{64,72... | collective-permute-start | bytes 196616 | tf_op jit(solution)/shard_map/ppermute | solution.py:300
  55.1 13.8 %collective-permute-start.5 = (f32[128,128]{1,0:T(8,128)S(1)}, f32[128,128]{1,0:T(8,128)S(1)}, u32[]{:S(2)}, u32[]{:S(2)}) collective-permute-start(f32[128,128]{1,0:T(8,128)S(1)} %get-tuple-element.42), channel_id=1, source_target_pairs={{8,16},{16,8},{24,32},{32,24},{40,48},{48,40},{56,64},{64,56},{72,... | collective-permute-start | bytes 196616 | tf_op jit(solution)/shard_map/ppermute | solution.py:301
  59.2 3.9 %collective-permute-start.6 = (f32[32,256]{1,0:T(8,128)S(1)}, f32[32,256]{1,0:T(8,128)S(1)}, u32[]{:S(2)}, u32[]{:S(2)}) collective-permute-start(f32[32,256]{1,0:T(8,128)S(1)} %get-tuple-element.43), channel_id=1, source_target_pairs={{0,1},{1,0},{2,3},{3,2},{4,5},{5,4},{6,7},{7,6},{8,9},{9,8},{10,11... | collective-permute-start | bytes 98312 | tf_op jit(solution)/shard_map/ppermute | solution.py:302
  60.1 8.8 %collective-permute-start.7 = (f32[32,256]{1,0:T(8,128)S(1)}, f32[32,256]{1,0:T(8,128)S(1)}, u32[]{:S(2)}, u32[]{:S(2)}) collective-permute-start(f32[32,256]{1,0:T(8,128)S(1)} %get-tuple-element.44), channel_id=1, source_target_pairs={{1,2},{2,1},{3,4},{4,3},{5,6},{6,5},{9,10},{10,9},{11,12},{12,11},... | collective-permute-start | bytes 98312 | tf_op jit(solution)/shard_map/ppermute | solution.py:307

commit v2 on v1

--- a/solution.py
+++ b/solution.py
@@ -10,7 +10,6 @@
 AXES = ("lon", "lat")
 BULK = 0.1
 SLOTS = 8
-GROUP = SLOTS + 1
 LEVELS = 16
 ROWS = 128
 LANES = 128
@@ -73,7 +72,8 @@
     return owner, cell, share
 
 
-def write_request(owner, cell, share, surface, out_ref, codes_ref):
+def request_kernel(owner_ref, cell_ref, weight_ref, ids_ref, codes_ref):
+    owner, cell, share = make_lists(owner_ref, cell_ref, weight_ref)
     device = iota((128, 256), 0)
     named = [as_bf16(device == owner[m]) for m in range(2)]
     earlier = as_bf16(iota((256, 256), 0) < iota((256, 256), 1))
@@ -87,14 +87,7 @@
     ids = sum(
         dot_nt(named[m], jnp.where(slot == rank[m], cell[m], 0.0).astype(BF16)) for m in range(2)
     )
-    total = 128 * GROUP
-    line = iota((total, 256), 0)
-    place = as_bf16(
-        (line == owner[0] * GROUP + rank[0]) | (line == owner[1] * GROUP + rank[1])
-    )
-    id_place = as_bf16(iota((total, 128), 0) == iota((total, 128), 1) * GROUP + SLOTS)
-    blocks = jnp.concatenate([surface[:, :LANES], surface[:, LANES:]], axis=0)
-    out_ref[...] = pick(place, blocks) + dot(id_place, ids.astype(BF16))
+    ids_ref[...] = ids[:, :SLOTS]
     table = jnp.concatenate(
         [(owner[m] * SLOTS + rank[m]).astype(F32) for m in range(2)]
         + [share, jnp.zeros((124, 256), F32)],
@@ -103,6 +96,23 @@
     codes_ref[...] = jnp.transpose(table)
 
 
+def in_hbm(x):
+    return pltpu.with_memory_space_constraint(x, pltpu.HBM)
+
+
+def make_request(owner, cell, weight):
+    return pl.pallas_call(
+        request_kernel,
+        out_shape=(pltpu.VMEM((128, SLOTS), F32), pltpu.VMEM((256, LANES), F32)),
+        grid=(1,),
+        in_specs=[pl.BlockSpec((2, 256), lambda i: (0, 0))] * 3,
+        out_specs=(VM,) * 2,
+        compiler_params=pltpu.CompilerParams(vmem_limit_bytes=LIMIT),
+        cost_estimate=pl.CostEstimate(flops=5 * 10**8, bytes_accessed=2**18, transcendentals=0),
+        name="request",
+    )(*[in_hbm(x) for x in (owner, cell, weight)])
+
+
 def pick_left(x, onehot):
     high, middle, low = pieces(x)
     return dot(high, onehot) + (dot(middle, onehot) + dot(low, onehot))
@@ -112,14 +122,13 @@
 CHUNK = ROWS // CHUNKS
 
 
-def request_kernel(owner_ref, cell_ref, weight_ref, t_ref, s_ref, u_ref, v_ref, k_ref,
-                   out_ref, codes_ref, lon_a_ref, lon_b_ref, lat_a_ref, lat_b_ref, west_ref,
-                   surface_buf, t_buf, s_buf, u_buf, k_buf, v_row, k_row, sems, more_sems):
+def edges_kernel(t_ref, s_ref, u_ref, v_ref, k_ref,
+                 lon_a_ref, lon_b_ref, lat_a_ref, lat_b_ref, west_ref,
+                 t_buf, s_buf, u_buf, k_buf, v_row, k_row, sems, more_sems):
     last = pl.ds(ROWS - 8, 8)
-    first = pltpu.make_async_copy(t_ref.at[0], surface_buf, more_sems.at[0])
     rows = [
-        pltpu.make_async_copy(v_ref.at[:, last, :], v_row, more_sems.at[1]),
-        pltpu.make_async_copy(k_ref.at[:, last, :], k_row, more_sems.at[2]),
+        pltpu.make_async_copy(v_ref.at[:, last, :], v_row, more_sems.at[0]),
+        pltpu.make_async_copy(k_ref.at[:, last, :], k_row, more_sems.at[1]),
     ]
     eastern = pl.ds(LANES, LANES)
 
@@ -132,15 +141,11 @@
             pltpu.make_async_copy(k_ref.at[:, part, eastern], k_buf.at[:, part, :], sems.at[3, c]),
         ]
 
-    first.start()
     for c in range(CHUNKS):
         for copy in chunk_copies(c):
             copy.start()
     for copy in rows:
         copy.start()
-    owner, cell, share = make_lists(owner_ref, cell_ref, weight_ref)
-    first.wait()
-    write_request(owner, cell, share, surface_buf[...], out_ref, codes_ref)
     odd = is_odd("lon")
 
     for c in range(CHUNKS):
@@ -175,73 +180,65 @@
     lat_b_ref[0:32, :] = jnp.where(odd, jnp.where(top, flipped(north), north), south)
 
 
-def in_hbm(x):
-    return pltpu.with_memory_space_constraint(x, pltpu.HBM)
-
-
-def make_request(owner, cell, weight, fields):
+def make_edges(fields):
     field = pltpu.VMEM((LEVELS, ROWS, 2 * LANES), F32)
     half = pltpu.VMEM((LEVELS, ROWS, LANES), F32)
     row = pltpu.VMEM((LEVELS, 8, 2 * LANES), F32)
     return pl.pallas_call(
-        request_kernel,
+        edges_kernel,
         out_shape=(
-            pltpu.VMEM((128 * GROUP, LANES), F32),
-            pltpu.VMEM((256, LANES), F32),
             pltpu.VMEM((ROWS, LANES), F32),
             pltpu.VMEM((ROWS, LANES), F32),
             pltpu.VMEM((64, 2 * LANES), F32),
             pltpu.VMEM((64, 2 * LANES), F32),
             pltpu.VMEM((ROWS, LANES), F32),
         ),
-        grid=(1,),
-        in_specs=[pl.BlockSpec((2, 256), lambda i: (0, 0))] * 3 + [ANY] * 5,
-        out_specs=(VM,) * 7,
+        in_specs=[ANY] * 5,
+        out_specs=(VM,) * 5,
         scratch_shapes=[
-            pltpu.VMEM((ROWS, 2 * LANES), F32), field, field, half, half, row, row,
+            field, field, half, half, row, row,
             pltpu.SemaphoreType.DMA((4, CHUNKS)),
-            pltpu.SemaphoreType.DMA((3,)),
+            pltpu.SemaphoreType.DMA((2,)),
         ],
         compiler_params=pltpu.CompilerParams(vmem_limit_bytes=LIMIT),
-        cost_estimate=pl.CostEstimate(flops=2 * 10**9, bytes_accessed=8 * 2**20, transcendentals=0),
-        name="request",
-    )(*[in_hbm(x) for x in (owner, cell, weight, *fields)])
-
-
-def answer_kernel(got_ref, air_ref, wind_ref, *rest):
-    out_ref = rest[-1]
-    ids = got_ref[pl.ds(SLOTS, 128, stride=GROUP), :].astype(BF16)
+        cost_estimate=pl.CostEstimate(flops=10**8, bytes_accessed=8 * 2**20, transcendentals=0),
+        name="edges",
+    )(*[in_hbm(x) for x in fields])
+
+
+def answer_kernel(ids_ref, air_ref, wind_ref, *rest):
+    out_ref = rest[4]
+    ids = ids_ref[...].astype(BF16)
     patches = jnp.concatenate([air_ref[...], wind_ref[...]], axis=1)
     high, middle, low = pieces(patches)
-    spread = jnp.ones((128, 256), BF16)
+    spread = jnp.ones((SLOTS, 256), BF16)
     chunk = 128
     for part in range(8):
         line = iota((chunk, 128), 0) + part * chunk
         lane = iota((chunk, 128), 1)
         rows = dot(as_bf16(line // SLOTS == lane), ids)
-        rows = jnp.where(lane == line % SLOTS, rows, 0.0)
+        rows = jnp.where(lane[:, :SLOTS] == line[:, :SLOTS] % SLOTS, rows, 0.0)
         wanted = dot(rows.astype(BF16), spread).astype(jnp.int32)
         onehot = as_bf16(wanted == iota((chunk, 256), 1))
         found = dot(onehot, high) + (dot(onehot, middle) + dot(onehot, low))
-        for s in range(chunk // SLOTS):
-            source = part * (chunk // SLOTS) + s
-            cells = got_ref[source * GROUP : source * GROUP + SLOTS, :]
-            here = found[s * SLOTS : (s + 1) * SLOTS]
-            out_ref[source * SLOTS : (source + 1) * SLOTS, :] = (
-                BULK * here[:, LANES:] * (here[:, :LANES] - cells)
-            )
-
-
-def make_answer(got, air, wind, after):
-    return pl.pallas_call(
+        sources = slice(part * 16, part * 16 + 16)
+        out_ref[sources, :SLOTS, :] = found[:, :LANES].reshape(16, SLOTS, LANES)
+        out_ref[sources, SLOTS:, :] = found[:, LANES:].reshape(16, SLOTS, LANES)
+
+
+def make_answer(ids, air, wind, through):
+    out = pl.pallas_call(
         answer_kernel,
-        out_shape=pltpu.VMEM((128 * SLOTS, LANES), F32),
-        in_specs=[VM] * 3 + [ANY] * len(after),
-        out_specs=VM,
+        out_shape=(pltpu.VMEM((128, 2 * SLOTS, LANES), F32),)
+        + tuple(pltpu.VMEM(x.shape, F32) for x in through),
+        in_specs=[VM] * 3 + [ANY] * 4,
+        out_specs=(VM,) + (ANY,) * 4,
+        input_output_aliases={3: 1, 4: 2, 5: 3, 6: 4},
         compiler_params=pltpu.CompilerParams(vmem_limit_bytes=LIMIT),
-        cost_estimate=pl.CostEstimate(flops=2 * 10**9, bytes_accessed=2**20, transcendentals=0),
+        cost_estimate=pl.CostEstimate(flops=10**9, bytes_accessed=2**21, transcendentals=0),
         name="answer",
-    )(in_vmem(got), air, wind, *after)
+    )(in_vmem(ids), air, wind, *[in_vmem(x) for x in through])
+    return out[0], out[1:]
 
 
 def is_odd(axis):
@@ -550,17 +547,24 @@
     )(*[in_hbm(x) for x in fields], in_hbm(mask), own, *got)
 
 
-def heat_kernel(top_ref, west_ref, east_ref, south_ref, north_ref, mask_hbm, back_ref, codes_ref,
-                heat_out, top_out, lon_a_ref, lon_b_ref, lat_a_ref, lat_b_ref, own_out, mask_ref, sem):
-    mask_copy = pltpu.make_async_copy(mask_hbm, mask_ref, sem)
+def heat_kernel(top_ref, west_ref, east_ref, south_ref, north_ref, mask_hbm, t_hbm, back_ref, codes_ref,
+                heat_out, top_out, lon_a_ref, lon_b_ref, lat_a_ref, lat_b_ref, own_out, mask_ref, t_ref, sems):
+    mask_copy = pltpu.make_async_copy(mask_hbm, mask_ref, sems.at[0])
     mask_copy.start()
-    high, middle, low = pieces(back_ref[...])
+    t_copy = pltpu.make_async_copy(t_hbm.at[0], t_ref, sems.at[1])
+    t_copy.start()
+    air = back_ref[:, :SLOTS, :].reshape(128 * SLOTS, LANES)
+    wind = back_ref[:, SLOTS:, :].reshape(128 * SLOTS, LANES)
+    high, middle, low = pieces(jnp.concatenate([air, wind], axis=1))
     codes = codes_ref[...]
     lane = iota((256, 1024), 1)
+    t_copy.wait()
+    surface = jnp.concatenate([t_ref[:, :LANES], t_ref[:, LANES:]], axis=0)
     heat = None
     for m in range(2):
         onehot = as_bf16(codes[:, m : m + 1].astype(jnp.int32) == lane)
-        flux = dot(onehot, high) + (dot(onehot, middle) + dot(onehot, low))
+        found = dot(onehot, high) + (dot(onehot, middle) + dot(onehot, low))
+        flux = BULK * found[:, LANES:] * (found[:, :LANES] - surface)
         part = codes[:, 2 + m : 3 + m] * flux
         heat = part if heat is None else heat + part
     mask_copy.wait()
@@ -584,7 +588,7 @@
     send_rows(south, north, lat_a_ref, lat_b_ref)
 
 
-def add_heat(top, west, east, south, north, mask, back, codes):
+def add_heat(top, west, east, south, north, mask, temp, back, codes):
     return pl.pallas_call(
         heat_kernel,
         out_shape=(
@@ -596,13 +600,17 @@
             pltpu.VMEM((32, 2 * LANES), F32),
             pltpu.VMEM((ROWS, LANES), F32),
         ),
-        in_specs=[VM] * 5 + [ANY] + [VM] * 2,
+        in_specs=[VM] * 5 + [ANY] * 2 + [VM] * 2,
         out_specs=(VM,) * 7,
-        scratch_shapes=[pltpu.VMEM((ROWS, 2 * LANES), jnp.int32), pltpu.SemaphoreType.DMA],
+        scratch_shapes=[
+            pltpu.VMEM((ROWS, 2 * LANES), jnp.int32),
+            pltpu.VMEM((ROWS, 2 * LANES), F32),
+            pltpu.SemaphoreType.DMA((2,)),
+        ],
         compiler_params=pltpu.CompilerParams(vmem_limit_bytes=LIMIT),
         cost_estimate=pl.CostEstimate(flops=10**9, bytes_accessed=2**20, transcendentals=0),
         name="heat",
-    )(*[in_vmem(x) for x in (top, west, east, south, north)], in_hbm(mask), in_vmem(back), in_vmem(codes))
+    )(*[in_vmem(x) for x in (top, west, east, south, north)], in_hbm(mask), in_hbm(temp), in_vmem(back), in_vmem(codes))
 
 
 def second_kernel(t_hbm, s_hbm, u_hbm, v_hbm, k_hbm, mask_hbm, top_ref, heat_ref, own_ref,
@@ -704,17 +712,18 @@
         return jnp.transpose(x.reshape(256, 2))
 
     fields = (temp, salt, east_face_velocity, v_face, kappa)
-    request, codes, *sent, own = make_request(
-        lists(margin_owner_device), lists(margin_cell), lists(margin_weight), fields
+    ids, codes = make_request(
+        lists(margin_owner_device), lists(margin_cell), lists(margin_weight)
     )
-    request = request.reshape(128, 1, GROUP * LANES)
-    got = lax.all_to_all(request, AXES, split_axis=0, concat_axis=0, tiled=True)
-    got = got.reshape(128 * GROUP, LANES)
+    ids = lax.all_to_all(ids, AXES, split_axis=0, concat_axis=0, tiled=True)
+    *sent, own = make_edges(fields)
+    answer, sent = make_answer(
+        ids, air_temp.reshape(256, LANES), wind_speed.reshape(256, LANES), sent
+    )
+    back = lax.all_to_all(answer, AXES, split_axis=0, concat_axis=0, tiled=True)
     halos = [in_vmem(g) for g in exchange(*sent)]
-    answer = make_answer(got, air_temp.reshape(256, LANES), wind_speed.reshape(256, LANES), halos)
-    back = lax.all_to_all(answer, AXES, split_axis=0, concat_axis=0, tiled=True)
     t1, s1, *edges = first_step(fields, land_mask, in_vmem(own), halos)
-    heat, top, *sent, own = add_heat(*edges, land_mask, back, codes)
+    heat, top, *sent, own = add_heat(*edges, land_mask, temp, back, codes)
     later = exchange(*sent)
     return second_step(t1, s1, fields[2:], land_mask, top, heat, own, later, halos)
 

time: 79.3 us -> 83.5 us (1.053)
  waiting for transfers between devices: 14.2 us -> 17.9 us
    ppermute x2, waiting for transfers between devices: 4.81 us -> 9.87 us  [exchange(): got_lon_b = lax.ppermute(lon_b, 'lon', ring)]
    ppermute x2, waiting for transfers between devices: 8.03 us -> 5.2 us  [exchange(): got_lat_b = lax.ppermute(lat_b, AXES, route)]
    all_to_all x1, waiting for transfers between devices: 0.01 us -> 2.83 us  [body(): ids = lax.all_to_all(ids, AXES, split_axis=0, concat_axis=0, tiled=True)]
    ppermute x2, starting transfers between devices: 4.71 us -> 6.62 us  [exchange(): got_lat_b = lax.ppermute(lat_b, AXES, route)]
    ppermute x2, starting transfers between devices: 9.02 us -> 7.62 us  [exchange(): got_lon_b = lax.ppermute(lon_b, 'lon', ring)]
    all_to_all x1, waiting for transfers between devices: 0.9 us -> 0.01 us  [body(): back = lax.all_to_all(answer, AXES, split_axis=0, concat_axis=0, tiled=True)]
    ppermute x2, starting transfers between devices: 1.68 us -> 0.84 us  [exchange(): got_lat_a = lax.ppermute(lat_a, 'lat', swap_pairs(0, n_lat))]
    pallas_call x2 -> x3, Pallas kernels: 8.87 us -> 9 us  [the longest x1 4.41 us: make_edges(): pl.pallas_call(edges_kernel, out_shape=(pltpu.VMEM((ROWS, LANES), F32), p...]
  transfers between devices with their start and end apart: 10 -> 10, of which waited for: 5 -> 4; matrix products, arithmetic and copies ran while one was open for 0% -> 0% of each run, Pallas kernels for 13% -> 18%
where the time goes in v2:
time: 83.5 us; the launch traced here: 83.2 us
  starting transfers between devices  32.7 us (39%)
  Pallas kernels  31.8 us (38%)
  waiting for transfers between devices  17.9 us (21%)
    pallas_call x1, Pallas kernels, first_step(): pl.pallas_call(first_kernel, out_shape=(shape, shape, pltpu.VMEM((ROWS, 2...  10.6 us
    all_to_all x1, starting transfers between devices, body(): ids = lax.all_to_all(ids, AXES, split_axis=0, concat_axis=0, tiled=True)  10.2 us
    pallas_call x1, Pallas kernels, second_step(): pl.pallas_call(second_kernel, out_shape=(shape, shape, shape), in_specs=[...  9.95 us
    ppermute x2, waiting for transfers between devices, exchange(): got_lon_b = lax.ppermute(lon_b, 'lon', ring)  9.87 us
    ppermute x2, starting transfers between devices, exchange(): got_lon_b = lax.ppermute(lon_b, 'lon', ring)  7.62 us
    all_to_all x1, starting transfers between devices, body(): back = lax.all_to_all(answer, AXES, split_axis=0, concat_axis=0, tiled=True)  6.95 us
    ppermute x2, starting transfers between devices, exchange(): got_lat_b = lax.ppermute(lat_b, AXES, route)  6.62 us
    ppermute x2, waiting for transfers between devices, exchange(): got_lat_b = lax.ppermute(lat_b, AXES, route)  5.2 us
  transfers between devices with their start and end apart: 10, of which 4 were waited for; matrix products, arithmetic and copies ran while one was open for 0% of the time, Pallas kernels for 18%

profile of v2, /device:TPU:38, one launch (start us, length us, event | category | flops | bytes accessed | tf_op | source)
XLA Modules:
  0.0 83.2 jit_solution(11740085811689922018)
XLA Ops:
  0.6 1.9 %request.1 = (f32[128,8]{1,0:T(8,128)}, f32[256,128]{1,0:T(8,128)S(1)}) custom-call(s32[2,256]{1,0:T(2,128)} %bitcast.18, s32[2,256]{1,0:T(2,128)} %bitcast.19, f32[2,256]{1,0:T(2,128)} %bitcast.20), custom_call_target="tpu_custom_call" | custom-call | flops 500000000 | bytes 262144 | tf_op jit(solution)/shard_map/request/pallas_call | solution.py:104
  2.6 10.2 %all-to-all-start = ((f32[128,1,8]{2,1,0:T(1,128)}), f32[128,1,8]{2,1,0:T(1,128)S(1)}, u32[]{:S(2)}, u32[]{:S(2)}) async-start(f32[128,1,8]{2,1,0:T(1,128)} %bitcast.7), calls=%async_computation | async-start | bytes 131072 | tf_op jit(solution)/shard_map/all_to_all | solution.py:718
  12.8 0.0 copy-start
  12.8 0.0 copy-start.1
  12.8 4.4 %edges.1 = (f32[128,128]{1,0:T(8,128)S(1)}, f32[128,128]{1,0:T(8,128)S(1)}, f32[64,256]{1,0:T(8,128)S(1)}, f32[64,256]{1,0:T(8,128)S(1)}, f32[128,128]{1,0:T(8,128)S(1)}) custom-call(f32[16,128,256]{2,1,0:T(8,128)} %t_hbm.3, f32[16,128,256]{2,1,0:T(8,128)} %s_hbm.1, f32[16,128,256]{2,1,0:T(8,128)} %u_hbm.3, f32[16,128,256]{2,1,0:T(8,128)} %v_hbm.3, ...), custom_call_target="tpu_custom_call" | custom-call | flops 100000000 | bytes 8388608 | tf_op jit(solution)/shard_map/edges/pallas_call | solution.py:187
  17.2 2.8 %all-to-all-done = f32[128,1,8]{2,1,0:T(1,128)S(1)} async-done(((f32[128,1,8]{2,1,0:T(1,128)}), f32[128,1,8]{2,1,0:T(1,128)S(1)}, u32[]{:S(2)}, u32[]{:S(2)}) %all-to-all-start) | async-done | bytes 4128 | tf_op jit(solution)/shard_map/all_to_all | solution.py:718
  20.0 0.0 copy-done
  20.0 0.0 copy-done.1
  20.0 2.6 %answer.1 = (f32[128,16,128]{2,1,0:T(8,128)}, f32[128,128]{1,0:T(8,128)S(1)}, f32[128,128]{1,0:T(8,128)S(1)}, f32[64,256]{1,0:T(8,128)S(1)}, f32[64,256]{1,0:T(8,128)S(1)}) custom-call(f32[128,8]{1,0:T(8,128)S(1)} %bitcast.15, f32[256,128]{1,0:T(8,128)S(1)} %bitcast.16, ...), custom_call_target="tpu_custom_call", output_to_operand_aliasing={{1}: (3, {}), {2}: (4, {}), {3}: (5, {}), {4}: (6, {})} | custom-call | flops 1000000000 | bytes 2097152 | tf_op jit(solution)/shard_map/answer/pallas_call | solution.py:230
  22.7 7.0 %all-to-all-start.1 = ((f32[128,16,128]{2,1,0:T(8,128)}), f32[128,16,128]{2,1,0:T(8,128)S(1)}, u32[]{:S(2)}, u32[]{:S(2)}) async-start(f32[128,16,128]{2,1,0:T(8,128)} %get-tuple-element.46), calls=%async_computation.1 | async-start | bytes 2097152 | tf_op jit(solution)/shard_map/all_to_all | solution.py:723
  29.7 0.2 collective-permute-start
  29.9 4.9 %collective-permute-start.1 = (f32[128,128]{1,0:T(8,128)S(1)}, f32[128,128]{1,0:T(8,128)S(1)}, u32[]{:S(2)}, u32[]{:S(2)}) collective-permute-start(f32[128,128]{1,0:T(8,128)S(1)} %get-tuple-element.36), channel_id=1, source_target_pairs={{8,16},{16,8},{24,32},{32,24},{40,48},{48,40},{56,64},{64,56},{72,... | collective-permute-start | bytes 196616 | tf_op jit(solution)/shard_map/ppermute | solution.py:298
  34.8 0.8 %collective-permute-start.2 = (f32[64,256]{1,0:T(8,128)S(1)}, f32[64,256]{1,0:T(8,128)S(1)}, u32[]{:S(2)}, u32[]{:S(2)}) collective-permute-start(f32[64,256]{1,0:T(8,128)S(1)} %get-tuple-element.37), channel_id=1, source_target_pairs={{0,1},{1,0},{2,3},{3,2},{4,5},{5,4},{6,7},{7,6},{8,9},{9,8},{10,11... | collective-permute-start | bytes 196616 | tf_op jit(solution)/shard_map/ppermute | solution.py:299
  35.6 2.1 %collective-permute-start.3 = (f32[64,256]{1,0:T(8,128)S(1)}, f32[64,256]{1,0:T(8,128)S(1)}, u32[]{:S(2)}, u32[]{:S(2)}) collective-permute-start(f32[64,256]{1,0:T(8,128)S(1)} %get-tuple-element.38), channel_id=1, source_target_pairs={{1,2},{2,1},{3,4},{4,3},{5,6},{6,5},{9,10},{10,9},{11,12},{12,11},... | collective-permute-start | bytes 196616 | tf_op jit(solution)/shard_map/ppermute | solution.py:304
  37.7 0.0 collective-permute-done.lon_a.c_lon_a
  37.7 9.9 %collective-permute-done.1.lon_b.c_lon_b = f32[128,128]{1,0:T(8,128)S(1)} collective-permute-done((f32[128,128]{1,0:T(8,128)S(1)}, f32[128,128]{1,0:T(8,128)S(1)}, u32[]{:S(2)}, u32[]{:S(2)}) %collective-permute-start.1) | collective-permute-done | bytes 65568 | tf_op jit(solution)/shard_map/ppermute | solution.py:298
  47.6 0.0 collective-permute-done.2.lat_a.c_lat_a
  47.6 0.9 %collective-permute-done.3.lat_b.c_lat_b = f32[64,256]{1,0:T(8,128)S(1)} collective-permute-done((f32[64,256]{1,0:T(8,128)S(1)}, f32[64,256]{1,0:T(8,128)S(1)}, u32[]{:S(2)}, u32[]{:S(2)}) %collective-permute-start.3) | collective-permute-done | bytes 65568 | tf_op jit(solution)/shard_map/ppermute | solution.py:304
  48.5 10.6 %first_step.1 = (f32[16,128,256]{2,1,0:T(8,128)}, f32[16,128,256]{2,1,0:T(8,128)}, f32[128,256]{1,0:T(8,128)S(1)}, f32[128,128]{1,0:T(8,128)S(1)}, f32[128,128]{...) custom-call(f32[16,128,256]{2,1,0:T(8,128)} %t_hbm.3, f32[16,128,256]{2,1,0:T(8,128)} %s_hbm.1, ...), custom_call_target="tpu_custom_call" | custom-call | flops 70000000 | bytes 26214400 | tf_op jit(solution)/shard_map/first_step/pallas_call | solution.py:528
  59.1 0.0 all-to-all-done.1.back_ref
  59.1 2.3 %heat.1 = (f32[128,256]{1,0:T(8,128)S(1)}, f32[128,256]{1,0:T(8,128)S(1)}, f32[128,128]{1,0:T(8,128)S(1)}, f32[128,128]{1,0:T(8,128)S(1)}, f32[32,256]{1,0:T(8,1...) custom-call(f32[128,256]{1,0:T(8,128)S(1)} %get-tuple-element.41.top_ref, ...), custom_call_target="tpu_custom_call" | custom-call | flops 1000000000 | bytes 1048576 | tf_op jit(solution)/shard_map/heat/pallas_call | solution.py:592
  61.4 0.3 collective-permute-start.4
  61.6 2.7 %collective-permute-start.5 = (f32[128,128]{1,0:T(8,128)S(1)}, f32[128,128]{1,0:T(8,128)S(1)}, u32[]{:S(2)}, u32[]{:S(2)}) collective-permute-start(f32[128,128]{1,0:T(8,128)S(1)} %get-tuple-element.52), channel_id=1, source_target_pairs={{8,16},{16,8},{24,32},{32,24},{40,48},{48,40},{56,64},{64,56},{72,... | collective-permute-start | bytes 196616 | tf_op jit(solution)/shard_map/ppermute | solution.py:298
  64.4 0.0 collective-permute-start.6
  64.4 4.5 %collective-permute-start.7 = (f32[32,256]{1,0:T(8,128)S(1)}, f32[32,256]{1,0:T(8,128)S(1)}, u32[]{:S(2)}, u32[]{:S(2)}) collective-permute-start(f32[32,256]{1,0:T(8,128)S(1)} %get-tuple-element.54), channel_id=1, source_target_pairs={{1,2},{2,1},{3,4},{4,3},{5,6},{6,5},{9,10},{10,9},{11,12},{12,11},... | collective-permute-start | bytes 98312 | tf_op jit(solution)/shard_map/ppermute | solution.py:304
  68.9 0.0 collective-permute-done.6.lat_a
  68.9 4.3 %collective-permute-done.7.lat_b = f32[32,256]{1,0:T(8,128)S(1)} collective-permute-done((f32[32,256]{1,0:T(8,128)S(1)}, f32[32,256]{1,0:T(8,128)S(1)}, u32[]{:S(2)}, u32[]{:S(2)}) %collective-permute-start.7) | collective-permute-done | bytes 32800 | tf_op jit(solution)/shard_map/ppermute | solution.py:304
  73.2 0.0 collective-permute-done.4.lon_a
  73.2 0.0 collective-permute-done.5.lon_b
  73.2 9.9 %second_step.1 = (f32[16,128,256]{2,1,0:T(8,128)}, f32[16,128,256]{2,1,0:T(8,128)}, f32[16,128,256]{2,1,0:T(8,128)}) custom-call(f32[16,128,256]{2,1,0:T(8,128)} %get-tuple-element.39.t_hbm, f32[16,128,256]{2,1,0:T(8,128)} %get-tuple-element.40.s_hbm, f32[16,128,256]{2,1,0:T(8,128)} %u_hbm.3, f32[16,128,256]{2,1,0:T(8,128)} %v_hbm.3, f32[16,128,256]{2,1,0:T(8,128)} %k_hbm.3, ...), custom_call_target="tpu_custom_call" | custom-call | flops 70000000 | bytes 26214400 | tf_op jit(solution)/shard_map/second_step/pallas_call | solution.py:684
Async XLA Ops:
  2.6 17.5 %all-to-all-start = ((f32[128,1,8]{2,1,0:T(1,128)}), f32[128,1,8]{2,1,0:T(1,128)S(1)}, u32[]{:S(2)}, u32[]{:S(2)}) async-start(f32[128,1,8]{2,1,0:T(1,128)} %bitcast.7), calls=%async_computation | async-start | bytes 131072 | tf_op jit(solution)/shard_map/all_to_all | solution.py:718
  12.8 7.3 %copy-start = (f32[1,1,256,128]{3,2,1,0:T(8,128)S(1)}, f32[1,1,256,128]{3,2,1,0:T(8,128)}, u32[]{:S(2)}) copy-start(f32[1,1,256,128]{3,2,1,0:T(8,128)} %param.20) | copy-start | bytes 393220
  12.8 7.3 %copy-start.1 = (f32[1,1,256,128]{3,2,1,0:T(8,128)S(1)}, f32[1,1,256,128]{3,2,1,0:T(8,128)}, u32[]{:S(2)}) copy-start(f32[1,1,256,128]{3,2,1,0:T(8,128)} %param.21) | copy-start | bytes 393220
  22.7 36.4 %all-to-all-start.1 = ((f32[128,16,128]{2,1,0:T(8,128)}), f32[128,16,128]{2,1,0:T(8,128)S(1)}, u32[]{:S(2)}, u32[]{:S(2)}) async-start(f32[128,16,128]{2,1,0:T(8,128)} %get-tuple-element.46), calls=%async_computation.1 | async-start | bytes 2097152 | tf_op jit(solution)/shard_map/all_to_all | solution.py:723
  29.7 8.1 %collective-permute-start = (f32[128,128]{1,0:T(8,128)S(1)}, f32[128,128]{1,0:T(8,128)S(1)}, u32[]{:S(2)}, u32[]{:S(2)}) collective-permute-start(f32[128,128]{1,0:T(8,128)S(1)} %get-tuple-element.35), channel_id=1, source_target_pairs={{0,8},{8,0},{16,24},{24,16},{32,40},{40,32},{48,56},{56,48},{64,72... | collective-permute-start | bytes 196616 | tf_op jit(solution)/shard_map/ppermute | solution.py:297
  29.9 17.7 %collective-permute-start.1 = (f32[128,128]{1,0:T(8,128)S(1)}, f32[128,128]{1,0:T(8,128)S(1)}, u32[]{:S(2)}, u32[]{:S(2)}) collective-permute-start(f32[128,128]{1,0:T(8,128)S(1)} %get-tuple-element.36), channel_id=1, source_target_pairs={{8,16},{16,8},{24,32},{32,24},{40,48},{48,40},{56,64},{64,56},{72,... | collective-permute-start | bytes 196616 | tf_op jit(solution)/shard_map/ppermute | solution.py:298
  34.8 12.8 %collective-permute-start.2 = (f32[64,256]{1,0:T(8,128)S(1)}, f32[64,256]{1,0:T(8,128)S(1)}, u32[]{:S(2)}, u32[]{:S(2)}) collective-permute-start(f32[64,256]{1,0:T(8,128)S(1)} %get-tuple-element.37), channel_id=1, source_target_pairs={{0,1},{1,0},{2,3},{3,2},{4,5},{5,4},{6,7},{7,6},{8,9},{9,8},{10,11... | collective-permute-start | bytes 196616 | tf_op jit(solution)/shard_map/ppermute | solution.py:299
  35.6 12.9 %collective-permute-start.3 = (f32[64,256]{1,0:T(8,128)S(1)}, f32[64,256]{1,0:T(8,128)S(1)}, u32[]{:S(2)}, u32[]{:S(2)}) collective-permute-start(f32[64,256]{1,0:T(8,128)S(1)} %get-tuple-element.38), channel_id=1, source_target_pairs={{1,2},{2,1},{3,4},{4,3},{5,6},{6,5},{9,10},{10,9},{11,12},{12,11},... | collective-permute-start | bytes 196616 | tf_op jit(solution)/shard_map/ppermute | solution.py:304
  61.4 11.8 %collective-permute-start.4 = (f32[128,128]{1,0:T(8,128)S(1)}, f32[128,128]{1,0:T(8,128)S(1)}, u32[]{:S(2)}, u32[]{:S(2)}) collective-permute-start(f32[128,128]{1,0:T(8,128)S(1)} %get-tuple-element.51), channel_id=1, source_target_pairs={{0,8},{8,0},{16,24},{24,16},{32,40},{40,32},{48,56},{56,48},{64,72... | collective-permute-start | bytes 196616 | tf_op jit(solution)/shard_map/ppermute | solution.py:297
  61.6 11.6 %collective-permute-start.5 = (f32[128,128]{1,0:T(8,128)S(1)}, f32[128,128]{1,0:T(8,128)S(1)}, u32[]{:S(2)}, u32[]{:S(2)}) collective-permute-start(f32[128,128]{1,0:T(8,128)S(1)} %get-tuple-element.52), channel_id=1, source_target_pairs={{8,16},{16,8},{24,32},{32,24},{40,48},{48,40},{56,64},{64,56},{72,... | collective-permute-start | bytes 196616 | tf_op jit(solution)/shard_map/ppermute | solution.py:298
  64.4 4.5 %collective-permute-start.6 = (f32[32,256]{1,0:T(8,128)S(1)}, f32[32,256]{1,0:T(8,128)S(1)}, u32[]{:S(2)}, u32[]{:S(2)}) collective-permute-start(f32[32,256]{1,0:T(8,128)S(1)} %get-tuple-element.53), channel_id=1, source_target_pairs={{0,1},{1,0},{2,3},{3,2},{4,5},{5,4},{6,7},{7,6},{8,9},{9,8},{10,11... | collective-permute-start | bytes 98312 | tf_op jit(solution)/shard_map/ppermute | solution.py:299
  64.4 8.8 %collective-permute-start.7 = (f32[32,256]{1,0:T(8,128)S(1)}, f32[32,256]{1,0:T(8,128)S(1)}, u32[]{:S(2)}, u32[]{:S(2)}) collective-permute-start(f32[32,256]{1,0:T(8,128)S(1)} %get-tuple-element.54), channel_id=1, source_target_pairs={{1,2},{2,1},{3,4},{4,3},{5,6},{6,5},{9,10},{10,9},{11,12},{12,11},... | collective-permute-start | bytes 98312 | tf_op jit(solution)/shard_map/ppermute | solution.py:304

commit v3 on v2

--- a/solution.py
+++ b/solution.py
@@ -207,7 +207,7 @@
 
 
 def answer_kernel(ids_ref, air_ref, wind_ref, *rest):
-    out_ref = rest[4]
+    out_ref = rest[-1]
     ids = ids_ref[...].astype(BF16)
     patches = jnp.concatenate([air_ref[...], wind_ref[...]], axis=1)
     high, middle, low = pieces(patches)
@@ -226,19 +226,16 @@
         out_ref[sources, SLOTS:, :] = found[:, LANES:].reshape(16, SLOTS, LANES)
 
 
-def make_answer(ids, air, wind, through):
-    out = pl.pallas_call(
+def make_answer(ids, air, wind, after):
+    return pl.pallas_call(
         answer_kernel,
-        out_shape=(pltpu.VMEM((128, 2 * SLOTS, LANES), F32),)
-        + tuple(pltpu.VMEM(x.shape, F32) for x in through),
-        in_specs=[VM] * 3 + [ANY] * 4,
-        out_specs=(VM,) + (ANY,) * 4,
-        input_output_aliases={3: 1, 4: 2, 5: 3, 6: 4},
+        out_shape=pltpu.VMEM((128, 2 * SLOTS, LANES), F32),
+        in_specs=[VM] * 3 + [ANY] * len(after),
+        out_specs=VM,
         compiler_params=pltpu.CompilerParams(vmem_limit_bytes=LIMIT),
         cost_estimate=pl.CostEstimate(flops=10**9, bytes_accessed=2**21, transcendentals=0),
         name="answer",
-    )(in_vmem(ids), air, wind, *[in_vmem(x) for x in through])
-    return out[0], out[1:]
+    )(in_vmem(ids), air, wind, *after)
 
 
 def is_odd(axis):
@@ -547,12 +544,18 @@
     )(*[in_hbm(x) for x in fields], in_hbm(mask), own, *got)
 
 
-def heat_kernel(top_ref, west_ref, east_ref, south_ref, north_ref, mask_hbm, t_hbm, back_ref, codes_ref,
-                heat_out, top_out, lon_a_ref, lon_b_ref, lat_a_ref, lat_b_ref, own_out, mask_ref, t_ref, sems):
+def heat_kernel(top_ref, west_ref, east_ref, south_ref, north_ref, mask_hbm, t_hbm, t1_hbm, s1_hbm, back_ref, codes_ref,
+                t1_out, s1_out, heat_out, top_out, lon_a_ref, lon_b_ref, lat_a_ref, lat_b_ref, own_out, mask_ref, t_ref, sems):
     mask_copy = pltpu.make_async_copy(mask_hbm, mask_ref, sems.at[0])
     mask_copy.start()
     t_copy = pltpu.make_async_copy(t_hbm.at[0], t_ref, sems.at[1])
     t_copy.start()
+    moves = [
+        pltpu.make_async_copy(t1_hbm, t1_out, sems.at[2]),
+        pltpu.make_async_copy(s1_hbm, s1_out, sems.at[3]),
+    ]
+    for move in moves:
+        move.start()
     air = back_ref[:, :SLOTS, :].reshape(128 * SLOTS, LANES)
     wind = back_ref[:, SLOTS:, :].reshape(128 * SLOTS, LANES)
     high, middle, low = pieces(jnp.concatenate([air, wind], axis=1))
@@ -586,12 +589,17 @@
     south = jnp.concatenate([top_out[0:1, :], south_ref[1:, :]], axis=0)
     north = jnp.concatenate([top_out[ROWS - 1 : ROWS, :], north_ref[1:, :]], axis=0)
     send_rows(south, north, lat_a_ref, lat_b_ref)
-
-
-def add_heat(top, west, east, south, north, mask, temp, back, codes):
+    for move in moves:
+        move.wait()
+
+
+def add_heat(t1, s1, top, west, east, south, north, mask, temp, back, codes):
+    field = pltpu.VMEM((LEVELS, ROWS, 2 * LANES), F32)
     return pl.pallas_call(
         heat_kernel,
         out_shape=(
+            field,
+            field,
             pltpu.VMEM((ROWS, 2 * LANES), F32),
             pltpu.VMEM((ROWS, 2 * LANES), F32),
             pltpu.VMEM((ROWS, LANES), F32),
@@ -600,42 +608,40 @@
             pltpu.VMEM((32, 2 * LANES), F32),
             pltpu.VMEM((ROWS, LANES), F32),
         ),
-        in_specs=[VM] * 5 + [ANY] * 2 + [VM] * 2,
-        out_specs=(VM,) * 7,
+        in_specs=[VM] * 5 + [ANY] * 4 + [VM] * 2,
+        out_specs=(VM,) * 9,
         scratch_shapes=[
             pltpu.VMEM((ROWS, 2 * LANES), jnp.int32),
             pltpu.VMEM((ROWS, 2 * LANES), F32),
-            pltpu.SemaphoreType.DMA((2,)),
+            pltpu.SemaphoreType.DMA((4,)),
         ],
         compiler_params=pltpu.CompilerParams(vmem_limit_bytes=LIMIT),
         cost_estimate=pl.CostEstimate(flops=10**9, bytes_accessed=2**20, transcendentals=0),
         name="heat",
-    )(*[in_vmem(x) for x in (top, west, east, south, north)], in_hbm(mask), in_hbm(temp), in_vmem(back), in_vmem(codes))
-
-
-def second_kernel(t_hbm, s_hbm, u_hbm, v_hbm, k_hbm, mask_hbm, top_ref, heat_ref, own_ref,
+    )(*[in_vmem(x) for x in (top, west, east, south, north)], in_hbm(mask), in_hbm(temp), in_hbm(t1), in_hbm(s1), in_vmem(back), in_vmem(codes))
+
+
+def second_kernel(t_ref, s_ref, u_hbm, v_hbm, k_hbm, mask_hbm, top_ref, heat_ref, own_ref,
                   lon_a, lon_b, lat_a, lat_b, c_lon_a, c_lon_b, c_lat_a, c_lat_b,
                   t_out, s_out, rho_out,
                   carry_ref, side_ref, north_ref,
-                  t_ref, s_ref, u_ref, v_ref, k_ref, t_buf, s_buf, rho_buf, mask_ref, in_sems, sems):
-    sources = (t_hbm, s_hbm, u_hbm, v_hbm, k_hbm)
-    held = (t_ref, s_ref, u_ref, v_ref, k_ref)
+                  u_ref, v_ref, k_ref, t_buf, s_buf, rho_buf, mask_ref, in_sems, sems):
+    sources = (u_hbm, v_hbm, k_hbm)
+    held = (u_ref, v_ref, k_ref)
 
     def copy_in(t, index):
         rows = pl.ds(pl.multiple_of(index * 8, 8), 8)
         return pltpu.make_async_copy(sources[t].at[:, rows, :], held[t].at[:, rows, :], in_sems.at[t, index])
 
     def start(index, carry):
-        for f in range(5):
+        for f in range(3):
             copy_in(f, index).start()
         return carry
 
-    mask_copy = pltpu.make_async_copy(mask_hbm, mask_ref, in_sems.at[5, 0])
+    mask_copy = pltpu.make_async_copy(mask_hbm, mask_ref, in_sems.at[3, 0])
     start(0, 0)
     mask_copy.start()
     lax.fori_loop(1, STRIPS, start, 0)
-    copy_in(0, 0).wait()
-    copy_in(1, 0).wait()
     load, load_row = pair_loader((t_ref, s_ref), top_ref)
     halo_setup(is_odd("lon"), is_odd("lat"), (lon_a, lon_b, lat_a, lat_b), (c_lon_a, c_lon_b, c_lat_a, c_lat_b),
                own_ref, load_row, carry_ref, side_ref, north_ref)
@@ -659,11 +665,8 @@
 
     def body(strip, last):
         index = STRIPS - 1 if last else strip // 8
-        for f in range(2, 5):
+        for f in range(3):
             copy_in(f, index).wait()
-        if not last:
-            for t in range(2):
-                copy_in(t, index + 1).wait()
         step_strip(strip, last, load, u_ref, v_ref, k_ref, mask_ref, side_ref, north_ref, carry_ref, emit, heat_ref)
         for copy in copies(index):
             copy.start()
@@ -684,15 +687,15 @@
     return pl.pallas_call(
         second_kernel,
         out_shape=(shape, shape, shape),
-        in_specs=[ANY] * 6 + [VM] * 11,
+        in_specs=[VM] * 2 + [ANY] * 4 + [VM] * 11,
         out_specs=(ANY, ANY, ANY),
         scratch_shapes=STEP_SCRATCH
-        + [buf] * 8
-        + [pltpu.VMEM((ROWS, 2 * LANES), jnp.int32), pltpu.SemaphoreType.DMA((6, STRIPS)), pltpu.SemaphoreType.DMA((3, STRIPS))],
+        + [buf] * 6
+        + [pltpu.VMEM((ROWS, 2 * LANES), jnp.int32), pltpu.SemaphoreType.DMA((4, STRIPS)), pltpu.SemaphoreType.DMA((3, STRIPS))],
         compiler_params=pltpu.CompilerParams(vmem_limit_bytes=LIMIT),
         cost_estimate=STEP_COST,
         name="second_step",
-    )(in_hbm(t), in_hbm(s), *[in_hbm(x) for x in fields], in_hbm(mask), in_vmem(top), in_vmem(heat), in_vmem(own), *[in_vmem(g) for g in got], *coefs)
+    )(in_vmem(t), in_vmem(s), *[in_hbm(x) for x in fields], in_hbm(mask), in_vmem(top), in_vmem(heat), in_vmem(own), *[in_vmem(g) for g in got], *coefs)
 
 
 def body(
@@ -717,13 +720,13 @@
     )
     ids = lax.all_to_all(ids, AXES, split_axis=0, concat_axis=0, tiled=True)
     *sent, own = make_edges(fields)
-    answer, sent = make_answer(
-        ids, air_temp.reshape(256, LANES), wind_speed.reshape(256, LANES), sent
+    halos = [in_vmem(g) for g in exchange(*sent)]
+    answer = make_answer(
+        ids, air_temp.reshape(256, LANES), wind_speed.reshape(256, LANES), halos
     )
     back = lax.all_to_all(answer, AXES, split_axis=0, concat_axis=0, tiled=True)
-    halos = [in_vmem(g) for g in exchange(*sent)]
     t1, s1, *edges = first_step(fields, land_mask, in_vmem(own), halos)
-    heat, top, *sent, own = add_heat(*edges, land_mask, temp, back, codes)
+    t1, s1, heat, top, *sent, own = add_heat(t1, s1, *edges, land_mask, temp, back, codes)
     later = exchange(*sent)
     return second_step(t1, s1, fields[2:], land_mask, top, heat, own, later, halos)
 

time: 83.5 us -> 81.4 us (0.975)
  blocking collectives: 0 us -> 16.8 us
  starting transfers between devices: 32.7 us -> 22.6 us
  waiting for transfers between devices: 17.9 us -> 10.3 us
  Pallas kernels: 31.8 us -> 30.1 us
    all_to_all x0 -> x1, blocking collectives: none -> 16.8 us  [body(): ids = lax.all_to_all(ids, AXES, split_axis=0, concat_axis=0, tiled=True)]
    all_to_all x1 -> x0, starting transfers between devices: 10.2 us -> none  [body(): ids = lax.all_to_all(ids, AXES, split_axis=0, concat_axis=0, tiled=True)]
    ppermute x2, waiting for transfers between devices: 9.87 us -> 0.01 us  [exchange(): got_lon_b = lax.ppermute(lon_b, 'lon', ring)]
    all_to_all x1, waiting for transfers between devices: 0.01 us -> 6.56 us  [body(): back = lax.all_to_all(answer, AXES, split_axis=0, concat_axis=0, tiled=True)]
    all_to_all x1 -> x0, waiting for transfers between devices: 2.83 us -> none  [body(): ids = lax.all_to_all(ids, AXES, split_axis=0, concat_axis=0, tiled=True)]
    ppermute x2, waiting for transfers between devices: 5.2 us -> 3.68 us  [exchange(): got_lat_b = lax.ppermute(lat_b, AXES, route)]
    pallas_call x1, Pallas kernels: 9.95 us -> 8.74 us  [second_step(): pl.pallas_call(second_kernel, out_shape=(shape, shape, shape), in_specs=[...]
    ppermute x2, starting transfers between devices: 0.84 us -> 1.93 us  [exchange(): got_lat_a = lax.ppermute(lat_a, 'lat', swap_pairs(0, n_lat))]
  transfers between devices with their start and end apart: 10 -> 9, of which waited for: 4 -> 2; matrix products, arithmetic and copies ran while one was open for 0% -> 0% of each run, Pallas kernels for 18% -> 15%
where the time goes in v3:
time: 81.4 us; the launch traced here: 80.5 us
  Pallas kernels  30.1 us (37%)
  starting transfers between devices  22.6 us (28%)
  blocking collectives  16.8 us (21%)
  waiting for transfers between devices  10.3 us (13%)
    all_to_all x1, blocking collectives, body(): ids = lax.all_to_all(ids, AXES, split_axis=0, concat_axis=0, tiled=True)  16.8 us
    pallas_call x1, Pallas kernels, first_step(): pl.pallas_call(first_kernel, out_shape=(shape, shape, pltpu.VMEM((ROWS, 2...  10.5 us
    pallas_call x1, Pallas kernels, second_step(): pl.pallas_call(second_kernel, out_shape=(shape, shape, shape), in_specs=[...  8.74 us
    ppermute x2, starting transfers between devices, exchange(): got_lat_b = lax.ppermute(lat_b, AXES, route)  7.05 us
    all_to_all x1, starting transfers between devices, body(): back = lax.all_to_all(answer, AXES, split_axis=0, concat_axis=0, tiled=True)  6.8 us
    ppermute x2, starting transfers between devices, exchange(): got_lon_b = lax.ppermute(lon_b, 'lon', ring)  6.63 us
    all_to_all x1, waiting for transfers between devices, body(): back = lax.all_to_all(answer, AXES, split_axis=0, concat_axis=0, tiled=True)  6.56 us
    pallas_call x1, Pallas kernels, make_edges(): pl.pallas_call(edges_kernel, out_shape=(pltpu.VMEM((ROWS, LANES), F32), p...  4.41 us
  transfers between devices with their start and end apart: 9, of which 2 were waited for; matrix products, arithmetic and copies ran while one was open for 0% of the time, Pallas kernels for 15%

profile of v3, /device:TPU:38, one launch (start us, length us, event | category | flops | bytes accessed | tf_op | source)
XLA Modules:
  0.0 80.5 jit_solution(18039019066061865169)
XLA Ops:
  0.6 0.0 copy-start.1
  0.6 0.0 copy-start
  0.7 4.4 %edges.1 = (f32[128,128]{1,0:T(8,128)S(1)}, f32[128,128]{1,0:T(8,128)S(1)}, f32[64,256]{1,0:T(8,128)S(1)}, f32[64,256]{1,0:T(8,128)S(1)}, f32[128,128]{1,0:T(8,128)S(1)}) custom-call(f32[16,128,256]{2,1,0:T(8,128)} %t_hbm.3, f32[16,128,256]{2,1,0:T(8,128)} %s_hbm.1, f32[16,128,256]{2,1,0:T(8,128)} %u_hbm.3, f32[16,128,256]{2,1,0:T(8,128)} %v_hbm.3, ...), custom_call_target="tpu_custom_call" | custom-call | flops 100000000 | bytes 8388608 | tf_op jit(solution)/shard_map/edges/pallas_call | solution.py:187
  5.1 0.1 collective-permute-start
  5.2 5.5 %collective-permute-start.1 = (f32[128,128]{1,0:T(8,128)S(1)}, f32[128,128]{1,0:T(8,128)S(1)}, u32[]{:S(2)}, u32[]{:S(2)}) collective-permute-start(f32[128,128]{1,0:T(8,128)S(1)} %get-tuple-element.28), channel_id=1, source_target_pairs={{8,16},{16,8},{24,32},{32,24},{40,48},{48,40},{56,64},{64,56},{72,... | collective-permute-start | bytes 196616 | tf_op jit(solution)/shard_map/ppermute | solution.py:295
  10.7 0.8 %collective-permute-start.2 = (f32[64,256]{1,0:T(8,128)S(1)}, f32[64,256]{1,0:T(8,128)S(1)}, u32[]{:S(2)}, u32[]{:S(2)}) collective-permute-start(f32[64,256]{1,0:T(8,128)S(1)} %get-tuple-element.29), channel_id=1, source_target_pairs={{0,1},{1,0},{2,3},{3,2},{4,5},{5,4},{6,7},{7,6},{8,9},{9,8},{10,11... | collective-permute-start | bytes 196616 | tf_op jit(solution)/shard_map/ppermute | solution.py:296
  11.5 1.9 %collective-permute-start.3 = (f32[64,256]{1,0:T(8,128)S(1)}, f32[64,256]{1,0:T(8,128)S(1)}, u32[]{:S(2)}, u32[]{:S(2)}) collective-permute-start(f32[64,256]{1,0:T(8,128)S(1)} %get-tuple-element.30), channel_id=1, source_target_pairs={{1,2},{2,1},{3,4},{4,3},{5,6},{6,5},{9,10},{10,9},{11,12},{12,11},... | collective-permute-start | bytes 196616 | tf_op jit(solution)/shard_map/ppermute | solution.py:301
  13.4 1.3 %request.1 = (f32[128,8]{1,0:T(8,128)S(1)}, f32[256,128]{1,0:T(8,128)S(1)}) custom-call(s32[2,256]{1,0:T(2,128)} %bitcast.19, s32[2,256]{1,0:T(2,128)} %bitcast.20, f32[2,256]{1,0:T(2,128)} %bitcast.21), custom_call_target="tpu_custom_call" | custom-call | flops 500000000 | bytes 262144 | tf_op jit(solution)/shard_map/request/pallas_call | solution.py:104
  14.7 16.8 %all_to_all.16 = f32[128,1,8]{2,1,0:T(1,128)S(1)} all-to-all(f32[128,1,8]{2,1,0:T(1,128)S(1)} %bitcast.16), channel_id=1, replica_groups=mesh['lon'=16,'lat'=8] {'lon','lat'}, dimensions={0} | all-to-all | bytes 8192 | tf_op jit(solution)/shard_map/all_to_all | solution.py:721
  31.6 0.0 collective-permute-done.lon_a.rest_0_.c_lon_a
  31.6 0.0 collective-permute-done.1.lon_b.rest_1_.c_lon_b
  31.6 0.0 collective-permute-done.2.lat_a.rest_2_.c_lat_a
  31.6 0.0 collective-permute-done.3.lat_b.rest_3_.c_lat_b
  31.6 0.0 copy-done.1
  31.6 0.0 copy-done
  31.6 2.6 %answer.1 = f32[128,16,128]{2,1,0:T(8,128)} custom-call(f32[128,8]{1,0:T(8,128)S(1)} %bitcast.15, f32[256,128]{1,0:T(8,128)S(1)} %bitcast.17, f32[256,128]{1,0:T(8,128)S(1)} %bitcast.18, f32[128,128]{1,0:T(8,128)S(1)} %collective-permute-done.lon_a.rest_0_.c_lon_a, f32[128,128]{1,0:T(8,128)S(1)} %collective-permute-done.1.lon_b.rest_1_.c_lon_b, ...), custom_call_target="tpu_custom_call" | custom-call | flops 1000000000 | bytes 2097152 | tf_op jit(solution)/shard_map/answer/pallas_call | solution.py:230
  34.3 6.8 %all-to-all-start.1 = ((f32[128,16,128]{2,1,0:T(8,128)}), f32[128,16,128]{2,1,0:T(8,128)S(1)}, u32[]{:S(2)}, u32[]{:S(2)}) async-start(f32[128,16,128]{2,1,0:T(8,128)} %answer.1), calls=%async_computation.1 | async-start | bytes 2097152 | tf_op jit(solution)/shard_map/all_to_all | solution.py:727
  41.1 10.5 %first_step.1 = (f32[16,128,256]{2,1,0:T(8,128)}, f32[16,128,256]{2,1,0:T(8,128)}, f32[128,256]{1,0:T(8,128)S(1)}, f32[128,128]{1,0:T(8,128)S(1)}, f32[128,128]{...) custom-call(f32[16,128,256]{2,1,0:T(8,128)} %t_hbm.3, f32[16,128,256]{2,1,0:T(8,128)} %s_hbm.1, ...), custom_call_target="tpu_custom_call" | custom-call | flops 70000000 | bytes 26214400 | tf_op jit(solution)/shard_map/first_step/pallas_call | solution.py:525
  51.6 6.6 %all-to-all-done.1.back_ref = f32[128,16,128]{2,1,0:T(8,128)S(1)} async-done(((f32[128,16,128]{2,1,0:T(8,128)}), f32[128,16,128]{2,1,0:T(8,128)S(1)}, u32[]{:S(2)}, u32[]{:S(2)}) %all-to-all-start.1) | async-done | bytes 1048608 | tf_op jit(solution)/shard_map/all_to_all | solution.py:727
  58.2 2.4 %heat.1 = (f32[16,128,256]{2,1,0:T(8,128)S(1)}, f32[16,128,256]{2,1,0:T(8,128)S(1)}, f32[128,256]{1,0:T(8,128)S(1)}, f32[128,256]{1,0:T(8,128)S(1)}, f32[128,128...) custom-call(f32[128,256]{1,0:T(8,128)S(1)} %get-tuple-element.31.top, ...), custom_call_target="tpu_custom_call" | custom-call | flops 1000000000 | bytes 1048576 | tf_op jit(solution)/shard_map/heat/pallas_call | solution.py:598
  60.6 0.1 collective-permute-start.4
  60.7 1.1 %collective-permute-start.5 = (f32[128,128]{1,0:T(8,128)S(1)}, f32[128,128]{1,0:T(8,128)S(1)}, u32[]{:S(2)}, u32[]{:S(2)}) collective-permute-start(f32[128,128]{1,0:T(8,128)S(1)} %get-tuple-element.46), channel_id=1, source_target_pairs={{8,16},{16,8},{24,32},{32,24},{40,48},{48,40},{56,64},{64,56},{72,... | collective-permute-start | bytes 196616 | tf_op jit(solution)/shard_map/ppermute | solution.py:295
  61.8 1.1 %collective-permute-start.6 = (f32[32,256]{1,0:T(8,128)S(1)}, f32[32,256]{1,0:T(8,128)S(1)}, u32[]{:S(2)}, u32[]{:S(2)}) collective-permute-start(f32[32,256]{1,0:T(8,128)S(1)} %get-tuple-element.47), channel_id=1, source_target_pairs={{0,1},{1,0},{2,3},{3,2},{4,5},{5,4},{6,7},{7,6},{8,9},{9,8},{10,11... | collective-permute-start | bytes 98312 | tf_op jit(solution)/shard_map/ppermute | solution.py:296
  62.9 5.1 %collective-permute-start.7 = (f32[32,256]{1,0:T(8,128)S(1)}, f32[32,256]{1,0:T(8,128)S(1)}, u32[]{:S(2)}, u32[]{:S(2)}) collective-permute-start(f32[32,256]{1,0:T(8,128)S(1)} %get-tuple-element.48), channel_id=1, source_target_pairs={{1,2},{2,1},{3,4},{4,3},{5,6},{6,5},{9,10},{10,9},{11,12},{12,11},... | collective-permute-start | bytes 98312 | tf_op jit(solution)/shard_map/ppermute | solution.py:301
  68.0 0.0 collective-permute-done.6.lat_a
  68.0 3.7 %collective-permute-done.7.lat_b = f32[32,256]{1,0:T(8,128)S(1)} collective-permute-done((f32[32,256]{1,0:T(8,128)S(1)}, f32[32,256]{1,0:T(8,128)S(1)}, u32[]{:S(2)}, u32[]{:S(2)}) %collective-permute-start.7) | collective-permute-done | bytes 32800 | tf_op jit(solution)/shard_map/ppermute | solution.py:301
  71.7 0.0 collective-permute-done.4.lon_a
  71.7 0.0 collective-permute-done.5.lon_b
  71.7 8.7 %second_step.1 = (f32[16,128,256]{2,1,0:T(8,128)}, f32[16,128,256]{2,1,0:T(8,128)}, f32[16,128,256]{2,1,0:T(8,128)}) custom-call(f32[16,128,256]{2,1,0:T(8,128)S(1)} %get-tuple-element.40.t_ref, f32[16,128,256]{2,1,0:T(8,128)S(1)} %get-tuple-element.41.s_ref, f32[16,128,256]{2,1,0:T(8,128)} %u_hbm.3, f32[16,128,256]{2,1,0:T(8,128)} %v_hbm.3, ...), custom_call_target="tpu_custom_call" | custom-call | flops 70000000 | bytes 26214400 | tf_op jit(solution)/shard_map/second_step/pallas_call | solution.py:687
Async XLA Ops:
  0.6 31.0 %copy-start.1 = (f32[1,1,256,128]{3,2,1,0:T(8,128)S(1)}, f32[1,1,256,128]{3,2,1,0:T(8,128)}, u32[]{:S(2)}) copy-start(f32[1,1,256,128]{3,2,1,0:T(8,128)} %param.21) | copy-start | bytes 393220
  0.6 31.0 %copy-start = (f32[1,1,256,128]{3,2,1,0:T(8,128)S(1)}, f32[1,1,256,128]{3,2,1,0:T(8,128)}, u32[]{:S(2)}) copy-start(f32[1,1,256,128]{3,2,1,0:T(8,128)} %param.20) | copy-start | bytes 393220
  5.1 26.5 %collective-permute-start = (f32[128,128]{1,0:T(8,128)S(1)}, f32[128,128]{1,0:T(8,128)S(1)}, u32[]{:S(2)}, u32[]{:S(2)}) collective-permute-start(f32[128,128]{1,0:T(8,128)S(1)} %get-tuple-element.27), channel_id=1, source_target_pairs={{0,8},{8,0},{16,24},{24,16},{32,40},{40,32},{48,56},{56,48},{64,72... | collective-permute-start | bytes 196616 | tf_op jit(solution)/shard_map/ppermute | solution.py:294
  5.2 26.4 %collective-permute-start.1 = (f32[128,128]{1,0:T(8,128)S(1)}, f32[128,128]{1,0:T(8,128)S(1)}, u32[]{:S(2)}, u32[]{:S(2)}) collective-permute-start(f32[128,128]{1,0:T(8,128)S(1)} %get-tuple-element.28), channel_id=1, source_target_pairs={{8,16},{16,8},{24,32},{32,24},{40,48},{48,40},{56,64},{64,56},{72,... | collective-permute-start | bytes 196616 | tf_op jit(solution)/shard_map/ppermute | solution.py:295
  10.7 20.9 %collective-permute-start.2 = (f32[64,256]{1,0:T(8,128)S(1)}, f32[64,256]{1,0:T(8,128)S(1)}, u32[]{:S(2)}, u32[]{:S(2)}) collective-permute-start(f32[64,256]{1,0:T(8,128)S(1)} %get-tuple-element.29), channel_id=1, source_target_pairs={{0,1},{1,0},{2,3},{3,2},{4,5},{5,4},{6,7},{7,6},{8,9},{9,8},{10,11... | collective-permute-start | bytes 196616 | tf_op jit(solution)/shard_map/ppermute | solution.py:296
  11.5 20.1 %collective-permute-start.3 = (f32[64,256]{1,0:T(8,128)S(1)}, f32[64,256]{1,0:T(8,128)S(1)}, u32[]{:S(2)}, u32[]{:S(2)}) collective-permute-start(f32[64,256]{1,0:T(8,128)S(1)} %get-tuple-element.30), channel_id=1, source_target_pairs={{1,2},{2,1},{3,4},{4,3},{5,6},{6,5},{9,10},{10,9},{11,12},{12,11},... | collective-permute-start | bytes 196616 | tf_op jit(solution)/shard_map/ppermute | solution.py:301
  34.3 23.9 %all-to-all-start.1 = ((f32[128,16,128]{2,1,0:T(8,128)}), f32[128,16,128]{2,1,0:T(8,128)S(1)}, u32[]{:S(2)}, u32[]{:S(2)}) async-start(f32[128,16,128]{2,1,0:T(8,128)} %answer.1), calls=%async_computation.1 | async-start | bytes 2097152 | tf_op jit(solution)/shard_map/all_to_all | solution.py:727
  60.6 11.1 %collective-permute-start.4 = (f32[128,128]{1,0:T(8,128)S(1)}, f32[128,128]{1,0:T(8,128)S(1)}, u32[]{:S(2)}, u32[]{:S(2)}) collective-permute-start(f32[128,128]{1,0:T(8,128)S(1)} %get-tuple-element.45), channel_id=1, source_target_pairs={{0,8},{8,0},{16,24},{24,16},{32,40},{40,32},{48,56},{56,48},{64,72... | collective-permute-start | bytes 196616 | tf_op jit(solution)/shard_map/ppermute | solution.py:294
  60.7 11.0 %collective-permute-start.5 = (f32[128,128]{1,0:T(8,128)S(1)}, f32[128,128]{1,0:T(8,128)S(1)}, u32[]{:S(2)}, u32[]{:S(2)}) collective-permute-start(f32[128,128]{1,0:T(8,128)S(1)} %get-tuple-element.46), channel_id=1, source_target_pairs={{8,16},{16,8},{24,32},{32,24},{40,48},{48,40},{56,64},{64,56},{72,... | collective-permute-start | bytes 196616 | tf_op jit(solution)/shard_map/ppermute | solution.py:295
  61.8 6.3 %collective-permute-start.6 = (f32[32,256]{1,0:T(8,128)S(1)}, f32[32,256]{1,0:T(8,128)S(1)}, u32[]{:S(2)}, u32[]{:S(2)}) collective-permute-start(f32[32,256]{1,0:T(8,128)S(1)} %get-tuple-element.47), channel_id=1, source_target_pairs={{0,1},{1,0},{2,3},{3,2},{4,5},{5,4},{6,7},{7,6},{8,9},{9,8},{10,11... | collective-permute-start | bytes 98312 | tf_op jit(solution)/shard_map/ppermute | solution.py:296
  62.9 8.8 %collective-permute-start.7 = (f32[32,256]{1,0:T(8,128)S(1)}, f32[32,256]{1,0:T(8,128)S(1)}, u32[]{:S(2)}, u32[]{:S(2)}) collective-permute-start(f32[32,256]{1,0:T(8,128)S(1)} %get-tuple-element.48), channel_id=1, source_target_pairs={{1,2},{2,1},{3,4},{4,3},{5,6},{6,5},{9,10},{10,9},{11,12},{12,11},... | collective-permute-start | bytes 98312 | tf_op jit(solution)/shard_map/ppermute | solution.py:301

commit v4 on v3

--- a/solution.py
+++ b/solution.py
@@ -10,6 +10,7 @@
 AXES = ("lon", "lat")
 BULK = 0.1
 SLOTS = 8
+GROUP = SLOTS + 1
 LEVELS = 16
 ROWS = 128
 LANES = 128
@@ -72,8 +73,7 @@
     return owner, cell, share
 
 
-def request_kernel(owner_ref, cell_ref, weight_ref, ids_ref, codes_ref):
-    owner, cell, share = make_lists(owner_ref, cell_ref, weight_ref)
+def write_request(owner, cell, share, surface, out_ref, codes_ref):
     device = iota((128, 256), 0)
     named = [as_bf16(device == owner[m]) for m in range(2)]
     earlier = as_bf16(iota((256, 256), 0) < iota((256, 256), 1))
@@ -87,7 +87,14 @@
     ids = sum(
         dot_nt(named[m], jnp.where(slot == rank[m], cell[m], 0.0).astype(BF16)) for m in range(2)
     )
-    ids_ref[...] = ids[:, :SLOTS]
+    total = 128 * GROUP
+    line = iota((total, 256), 0)
+    place = as_bf16(
+        (line == owner[0] * GROUP + rank[0]) | (line == owner[1] * GROUP + rank[1])
+    )
+    id_place = as_bf16(iota((total, 128), 0) == iota((total, 128), 1) * GROUP + SLOTS)
+    blocks = jnp.concatenate([surface[:, :LANES], surface[:, LANES:]], axis=0)
+    out_ref[...] = pick(place, blocks) + dot(id_place, ids.astype(BF16))
     table = jnp.concatenate(
         [(owner[m] * SLOTS + rank[m]).astype(F32) for m in range(2)]
         + [share, jnp.zeros((124, 256), F32)],
@@ -96,21 +103,27 @@
     codes_ref[...] = jnp.transpose(table)
 
 
+def request_kernel(owner_ref, cell_ref, weight_ref, surface_ref, out_ref, codes_ref):
+    owner, cell, share = make_lists(owner_ref, cell_ref, weight_ref)
+    write_request(owner, cell, share, surface_ref[...], out_ref, codes_ref)
+
+
 def in_hbm(x):
     return pltpu.with_memory_space_constraint(x, pltpu.HBM)
 
 
-def make_request(owner, cell, weight):
+def make_request(owner, cell, weight, temp):
     return pl.pallas_call(
         request_kernel,
-        out_shape=(pltpu.VMEM((128, SLOTS), F32), pltpu.VMEM((256, LANES), F32)),
+        out_shape=(pltpu.VMEM((128 * GROUP, LANES), F32), pltpu.VMEM((256, LANES), F32)),
         grid=(1,),
-        in_specs=[pl.BlockSpec((2, 256), lambda i: (0, 0))] * 3,
+        in_specs=[pl.BlockSpec((2, 256), lambda i: (0, 0))] * 3
+        + [pl.BlockSpec((None, ROWS, 2 * LANES), lambda i: (0, 0, 0))],
         out_specs=(VM,) * 2,
         compiler_params=pltpu.CompilerParams(vmem_limit_bytes=LIMIT),
-        cost_estimate=pl.CostEstimate(flops=5 * 10**8, bytes_accessed=2**18, transcendentals=0),
+        cost_estimate=pl.CostEstimate(flops=5 * 10**8, bytes_accessed=2**20, transcendentals=0),
         name="request",
-    )(*[in_hbm(x) for x in (owner, cell, weight)])
+    )(*[in_hbm(x) for x in (owner, cell, weight, temp)])
 
 
 def pick_left(x, onehot):
@@ -118,11 +131,7 @@
     return dot(high, onehot) + (dot(middle, onehot) + dot(low, onehot))
 
 
-CHUNKS = 4
-CHUNK = ROWS // CHUNKS
-
-
-def edges_kernel(t_ref, s_ref, u_ref, v_ref, k_ref,
+def edges_kernel(t_ref, s_ref, u_ref, v_ref, k_ref, _,
                  lon_a_ref, lon_b_ref, lat_a_ref, lat_b_ref, west_ref,
                  t_buf, s_buf, u_buf, k_buf, v_row, k_row, sems, more_sems):
     last = pl.ds(ROWS - 8, 8)
@@ -132,31 +141,30 @@
     ]
     eastern = pl.ds(LANES, LANES)
 
-    def chunk_copies(c):
-        part = pl.ds(c * CHUNK, CHUNK)
-        return [
-            pltpu.make_async_copy(t_ref.at[:, part, :], t_buf.at[:, part, :], sems.at[0, c]),
-            pltpu.make_async_copy(s_ref.at[:, part, :], s_buf.at[:, part, :], sems.at[1, c]),
-            pltpu.make_async_copy(u_ref.at[:, part, eastern], u_buf.at[:, part, :], sems.at[2, c]),
-            pltpu.make_async_copy(k_ref.at[:, part, eastern], k_buf.at[:, part, :], sems.at[3, c]),
-        ]
-
-    for c in range(CHUNKS):
-        for copy in chunk_copies(c):
-            copy.start()
-    for copy in rows:
+    copies = [
+        pltpu.make_async_copy(t_ref, t_buf, sems.at[0]),
+        pltpu.make_async_copy(s_ref, s_buf, sems.at[1]),
+        pltpu.make_async_copy(u_ref.at[:, :, eastern], u_buf, sems.at[2]),
+        pltpu.make_async_copy(k_ref.at[:, :, eastern], k_buf, sems.at[3]),
+    ]
+    for copy in copies + rows:
         copy.start()
     odd = is_odd("lon")
-
-    for c in range(CHUNKS):
-        for copy in chunk_copies(c):
-            copy.wait()
-
-        part = slice(c * CHUNK, (c + 1) * CHUNK)
-        west, east = column_edges((t_buf, s_buf), (u_buf, k_buf), part, CHUNK)
-        west_ref[part, :] = west
-        lon_a_ref[part, :] = jnp.where(odd, west, east)
-        lon_b_ref[part, :] = jnp.where(odd, east, west)
+    columns = Columns(ROWS)
+    for t, ref in enumerate((t_buf, s_buf)):
+        copies[t].wait()
+        for k in range(LEVELS):
+            columns.add_west(LEVELS * t + k, ref[k, :, :LANES])
+        for k in range(LEVELS):
+            columns.add_east(LEVELS * t + k, ref[k, :, LANES:])
+    for f, ref in enumerate((u_buf, k_buf)):
+        copies[2 + f].wait()
+        for k in range(LEVELS):
+            columns.add_east(64 + LEVELS * f + k, ref[k])
+    west, east = columns.west, with_faces(columns)
+    west_ref[...] = west
+    lon_a_ref[...] = jnp.where(odd, west, east)
+    lon_b_ref[...] = jnp.where(odd, east, west)
     for copy in rows:
         copy.wait()
     south = jnp.concatenate(
@@ -180,7 +188,7 @@
     lat_b_ref[0:32, :] = jnp.where(odd, jnp.where(top, flipped(north), north), south)
 
 
-def make_edges(fields):
+def make_edges(fields, after):
     field = pltpu.VMEM((LEVELS, ROWS, 2 * LANES), F32)
     half = pltpu.VMEM((LEVELS, ROWS, LANES), F32)
     row = pltpu.VMEM((LEVELS, 8, 2 * LANES), F32)
@@ -193,49 +201,53 @@
             pltpu.VMEM((64, 2 * LANES), F32),
             pltpu.VMEM((ROWS, LANES), F32),
         ),
-        in_specs=[ANY] * 5,
+        in_specs=[ANY] * 6,
         out_specs=(VM,) * 5,
         scratch_shapes=[
             field, field, half, half, row, row,
-            pltpu.SemaphoreType.DMA((4, CHUNKS)),
+            pltpu.SemaphoreType.DMA((4,)),
             pltpu.SemaphoreType.DMA((2,)),
         ],
         compiler_params=pltpu.CompilerParams(vmem_limit_bytes=LIMIT),
         cost_estimate=pl.CostEstimate(flops=10**8, bytes_accessed=8 * 2**20, transcendentals=0),
         name="edges",
-    )(*[in_hbm(x) for x in fields])
-
-
-def answer_kernel(ids_ref, air_ref, wind_ref, *rest):
+    )(*[in_hbm(x) for x in fields], after)
+
+
+def answer_kernel(got_ref, air_ref, wind_ref, *rest):
     out_ref = rest[-1]
-    ids = ids_ref[...].astype(BF16)
+    ids = got_ref[pl.ds(SLOTS, 128, stride=GROUP), :].astype(BF16)
     patches = jnp.concatenate([air_ref[...], wind_ref[...]], axis=1)
     high, middle, low = pieces(patches)
-    spread = jnp.ones((SLOTS, 256), BF16)
+    spread = jnp.ones((128, 256), BF16)
     chunk = 128
     for part in range(8):
         line = iota((chunk, 128), 0) + part * chunk
         lane = iota((chunk, 128), 1)
         rows = dot(as_bf16(line // SLOTS == lane), ids)
-        rows = jnp.where(lane[:, :SLOTS] == line[:, :SLOTS] % SLOTS, rows, 0.0)
+        rows = jnp.where(lane == line % SLOTS, rows, 0.0)
         wanted = dot(rows.astype(BF16), spread).astype(jnp.int32)
         onehot = as_bf16(wanted == iota((chunk, 256), 1))
         found = dot(onehot, high) + (dot(onehot, middle) + dot(onehot, low))
-        sources = slice(part * 16, part * 16 + 16)
-        out_ref[sources, :SLOTS, :] = found[:, :LANES].reshape(16, SLOTS, LANES)
-        out_ref[sources, SLOTS:, :] = found[:, LANES:].reshape(16, SLOTS, LANES)
-
-
-def make_answer(ids, air, wind, after):
+        for s in range(chunk // SLOTS):
+            source = part * (chunk // SLOTS) + s
+            cells = got_ref[source * GROUP : source * GROUP + SLOTS, :]
+            here = found[s * SLOTS : (s + 1) * SLOTS]
+            out_ref[source * SLOTS : (source + 1) * SLOTS, :] = (
+                BULK * here[:, LANES:] * (here[:, :LANES] - cells)
+            )
+
+
+def make_answer(got, air, wind, after):
     return pl.pallas_call(
         answer_kernel,
-        out_shape=pltpu.VMEM((128, 2 * SLOTS, LANES), F32),
+        out_shape=pltpu.VMEM((128 * SLOTS, LANES), F32),
         in_specs=[VM] * 3 + [ANY] * len(after),
         out_specs=VM,
         compiler_params=pltpu.CompilerParams(vmem_limit_bytes=LIMIT),
-        cost_estimate=pl.CostEstimate(flops=10**9, bytes_accessed=2**21, transcendentals=0),
+        cost_estimate=pl.CostEstimate(flops=2 * 10**9, bytes_accessed=2**20, transcendentals=0),
         name="answer",
-    )(in_vmem(ids), air, wind, *after)
+    )(in_vmem(got), air, wind, *after)
 
 
 def is_odd(axis):
@@ -260,17 +272,7 @@
         self.east = jnp.where(self.lane == at, roll(x, at - 127, 1), self.east)
 
 
-def column_edges(tracers, extra, rows, count):
-    columns = Columns(count)
-    for t, ref in enumerate(tracers):
-        for k in range(LEVELS):
-            columns.add_west(LEVELS * t + k, ref[k, rows, :LANES])
-    for t, ref in enumerate(tracers):
-        for k in range(LEVELS):
-            columns.add_east(LEVELS * t + k, ref[k, rows, LANES:])
-    for f, ref in enumerate(extra):
-        for k in range(LEVELS):
-            columns.add_east(64 + LEVELS * f + k, ref[k, rows, :])
+def with_faces(columns):
     faces = jnp.where(columns.lane >= 64, columns.east, 0.0)
     tracers_east = jnp.where(columns.lane < 64, columns.east, 0.0)
     u = jnp.where(columns.lane < 80, faces, 0.0)
@@ -278,7 +280,7 @@
     u = roll(u, -32, 1)
     d = roll(d, -16, 1)
     east = tracers_east + (u + roll(u, 16, 1)) + (d + roll(d, 16, 1))
-    return columns.west, east
+    return east
 
 
 def swap_pairs(first, count):
@@ -440,21 +442,20 @@
 
 
 def first_kernel(t_hbm, s_hbm, u_hbm, v_hbm, k_hbm, mask_hbm, own_ref, lon_a, lon_b, lat_a, lat_b,
-                 t_out, s_out, top_out, west_out, east_out, south_out, north_out,
+                 t_new, s_out, top_out, west_out, east_out, south_out, north_out,
                  carry_ref, side_ref, north_ref,
-                 t_ref, s_ref, u_ref, v_ref, k_ref, t_new, s_new, mask_ref, sems, out_sems):
+                 t_ref, s_ref, u_ref, v_ref, k_ref, s_new, mask_ref, sems, out_sems):
     sources = (t_hbm, s_hbm, u_hbm, v_hbm, k_hbm)
     bufs = (t_ref, s_ref, u_ref, v_ref, k_ref)
     new_bufs = (t_new, s_new)
-    outs = (t_out, s_out)
 
     def copy_in(f, index):
         rows = pl.ds(pl.multiple_of(index * 8, 8), 8)
         return pltpu.make_async_copy(sources[f].at[:, rows, :], bufs[f].at[:, rows, :], sems.at[f, index])
 
-    def copy_out(t, index):
+    def copy_out(index):
         rows = pl.ds(pl.multiple_of(index * 8, 8), 8)
-        return pltpu.make_async_copy(new_bufs[t].at[:, rows, :], outs[t].at[:, rows, :], out_sems.at[t, index])
+        return pltpu.make_async_copy(s_new.at[:, rows, :], s_out.at[:, rows, :], out_sems.at[index])
 
     def start(index, carry):
         for f in range(5):
@@ -494,8 +495,7 @@
         step_strip(strip, last, load, u_ref, v_ref, k_ref, mask_ref, side_ref, north_ref, carry_ref, emit)
         west_out[pl.ds(strip, 8), :] = columns.west
         east_out[pl.ds(strip, 8), :] = columns.east
-        for t in range(2):
-            copy_out(t, index).start()
+        copy_out(index).start()
 
     strips(body)
     south_out[...] = jnp.concatenate([ref[k, 0:1, :] for ref in new_bufs for k in range(LEVELS)], axis=0)
@@ -504,8 +504,7 @@
     )
 
     def finish(index, carry):
-        for t in range(2):
-            copy_out(t, index).wait()
+        copy_out(index).wait()
         return carry
 
     lax.fori_loop(0, STRIPS, finish, 0)
@@ -525,7 +524,7 @@
     return pl.pallas_call(
         first_kernel,
         out_shape=(
-            shape,
+            buf,
             shape,
             pltpu.VMEM((ROWS, 2 * LANES), F32),
             pltpu.VMEM((ROWS, LANES), F32),
@@ -534,40 +533,29 @@
             pltpu.VMEM((2 * LEVELS, 2 * LANES), F32),
         ),
         in_specs=[ANY] * 6 + [VM] * 5,
-        out_specs=(ANY, ANY) + (VM,) * 5,
+        out_specs=(VM, ANY) + (VM,) * 5,
         scratch_shapes=STEP_SCRATCH
-        + [buf] * 7
-        + [pltpu.VMEM((ROWS, 2 * LANES), jnp.int32), pltpu.SemaphoreType.DMA((6, STRIPS)), pltpu.SemaphoreType.DMA((2, STRIPS))],
+        + [buf] * 6
+        + [pltpu.VMEM((ROWS, 2 * LANES), jnp.int32), pltpu.SemaphoreType.DMA((6, STRIPS)), pltpu.SemaphoreType.DMA((STRIPS,))],
         compiler_params=pltpu.CompilerParams(vmem_limit_bytes=LIMIT),
         cost_estimate=STEP_COST,
         name="first_step",
     )(*[in_hbm(x) for x in fields], in_hbm(mask), own, *got)
 
 
-def heat_kernel(top_ref, west_ref, east_ref, south_ref, north_ref, mask_hbm, t_hbm, t1_hbm, s1_hbm, back_ref, codes_ref,
-                t1_out, s1_out, heat_out, top_out, lon_a_ref, lon_b_ref, lat_a_ref, lat_b_ref, own_out, mask_ref, t_ref, sems):
+def heat_kernel(top_ref, west_ref, east_ref, south_ref, north_ref, mask_hbm, s1_hbm, back_ref, codes_ref,
+                s1_out, heat_out, top_out, lon_a_ref, lon_b_ref, lat_a_ref, lat_b_ref, own_out, mask_ref, sems):
     mask_copy = pltpu.make_async_copy(mask_hbm, mask_ref, sems.at[0])
     mask_copy.start()
-    t_copy = pltpu.make_async_copy(t_hbm.at[0], t_ref, sems.at[1])
-    t_copy.start()
-    moves = [
-        pltpu.make_async_copy(t1_hbm, t1_out, sems.at[2]),
-        pltpu.make_async_copy(s1_hbm, s1_out, sems.at[3]),
-    ]
-    for move in moves:
-        move.start()
-    air = back_ref[:, :SLOTS, :].reshape(128 * SLOTS, LANES)
-    wind = back_ref[:, SLOTS:, :].reshape(128 * SLOTS, LANES)
-    high, middle, low = pieces(jnp.concatenate([air, wind], axis=1))
+    move = pltpu.make_async_copy(s1_hbm, s1_out, sems.at[1])
+    move.start()
+    high, middle, low = pieces(back_ref[...])
     codes = codes_ref[...]
     lane = iota((256, 1024), 1)
-    t_copy.wait()
-    surface = jnp.concatenate([t_ref[:, :LANES], t_ref[:, LANES:]], axis=0)
     heat = None
     for m in range(2):
         onehot = as_bf16(codes[:, m : m + 1].astype(jnp.int32) == lane)
-        found = dot(onehot, high) + (dot(onehot, middle) + dot(onehot, low))
-        flux = BULK * found[:, LANES:] * (found[:, :LANES] - surface)
+        flux = dot(onehot, high) + (dot(onehot, middle) + dot(onehot, low))
         part = codes[:, 2 + m : 3 + m] * flux
         heat = part if heat is None else heat + part
     mask_copy.wait()
@@ -589,16 +577,14 @@
     south = jnp.concatenate([top_out[0:1, :], south_ref[1:, :]], axis=0)
     north = jnp.concatenate([top_out[ROWS - 1 : ROWS, :], north_ref[1:, :]], axis=0)
     send_rows(south, north, lat_a_ref, lat_b_ref)
-    for move in moves:
-        move.wait()
-
-
-def add_heat(t1, s1, top, west, east, south, north, mask, temp, back, codes):
+    move.wait()
+
+
+def add_heat(s1, top, west, east, south, north, mask, back, codes):
     field = pltpu.VMEM((LEVELS, ROWS, 2 * LANES), F32)
     return pl.pallas_call(
         heat_kernel,
         out_shape=(
-            field,
             field,
             pltpu.VMEM((ROWS, 2 * LANES), F32),
             pltpu.VMEM((ROWS, 2 * LANES), F32),
@@ -608,17 +594,16 @@
             pltpu.VMEM((32, 2 * LANES), F32),
             pltpu.VMEM((ROWS, LANES), F32),
         ),
-        in_specs=[VM] * 5 + [ANY] * 4 + [VM] * 2,
-        out_specs=(VM,) * 9,
+        in_specs=[VM] * 5 + [ANY] * 2 + [VM] * 2,
+        out_specs=(VM,) * 8,
         scratch_shapes=[
             pltpu.VMEM((ROWS, 2 * LANES), jnp.int32),
-            pltpu.VMEM((ROWS, 2 * LANES), F32),
-            pltpu.SemaphoreType.DMA((4,)),
+            pltpu.SemaphoreType.DMA((2,)),
         ],
         compiler_params=pltpu.CompilerParams(vmem_limit_bytes=LIMIT),
         cost_estimate=pl.CostEstimate(flops=10**9, bytes_accessed=2**20, transcendentals=0),
         name="heat",
-    )(*[in_vmem(x) for x in (top, west, east, south, north)], in_hbm(mask), in_hbm(temp), in_hbm(t1), in_hbm(s1), in_vmem(back), in_vmem(codes))
+    )(*[in_vmem(x) for x in (top, west, east, south, north)], in_hbm(mask), in_hbm(s1), in_vmem(back), in_vmem(codes))
 
 
 def second_kernel(t_ref, s_ref, u_hbm, v_hbm, k_hbm, mask_hbm, top_ref, heat_ref, own_ref,
@@ -657,7 +642,7 @@
             rho_buf[at] = density_of(new[0][h], new[1][h])
 
     def copies(index):
-        rows = pl.ds(pl.multiple_of(index * 8, 8), 8)
+        rows = pl.ds(pl.multiple_of(index * 16, 16), 16)
         return [
             pltpu.make_async_copy(bufs[n].at[:, rows, :], outs[n].at[:, rows, :], sems.at[n, index])
             for n in range(3)
@@ -668,8 +653,15 @@
         for f in range(3):
             copy_in(f, index).wait()
         step_strip(strip, last, load, u_ref, v_ref, k_ref, mask_ref, side_ref, north_ref, carry_ref, emit, heat_ref)
-        for copy in copies(index):
-            copy.start()
+
+        def send():
+            for copy in copies(index // 2):
+                copy.start()
+
+        if last:
+            send()
+        else:
+            pl.when(lax.rem(index, 2) == 1)(send)
 
     strips(body)
 
@@ -678,7 +670,7 @@
             copy.wait()
         return carry
 
-    lax.fori_loop(0, STRIPS, finish, 0)
+    lax.fori_loop(0, STRIPS // 2, finish, 0)
 
 
 def second_step(t, s, fields, mask, top, heat, own, got, coefs):
@@ -691,7 +683,7 @@
         out_specs=(ANY, ANY, ANY),
         scratch_shapes=STEP_SCRATCH
         + [buf] * 6
-        + [pltpu.VMEM((ROWS, 2 * LANES), jnp.int32), pltpu.SemaphoreType.DMA((4, STRIPS)), pltpu.SemaphoreType.DMA((3, STRIPS))],
+        + [pltpu.VMEM((ROWS, 2 * LANES), jnp.int32), pltpu.SemaphoreType.DMA((4, STRIPS)), pltpu.SemaphoreType.DMA((3, STRIPS // 2))],
         compiler_params=pltpu.CompilerParams(vmem_limit_bytes=LIMIT),
         cost_estimate=STEP_COST,
         name="second_step",
@@ -715,18 +707,20 @@
         return jnp.transpose(x.reshape(256, 2))
 
     fields = (temp, salt, east_face_velocity, v_face, kappa)
-    ids, codes = make_request(
-        lists(margin_owner_device), lists(margin_cell), lists(margin_weight)
-    )
-    ids = lax.all_to_all(ids, AXES, split_axis=0, concat_axis=0, tiled=True)
-    *sent, own = make_edges(fields)
+    request, codes = make_request(
+        lists(margin_owner_device), lists(margin_cell), lists(margin_weight), temp
+    )
+    request = request.reshape(128, 1, GROUP * LANES)
+    got = lax.all_to_all(request, AXES, split_axis=0, concat_axis=0, tiled=True)
+    got = got.reshape(128 * GROUP, LANES)
+    *sent, own = make_edges(fields, codes)
     halos = [in_vmem(g) for g in exchange(*sent)]
     answer = make_answer(
-        ids, air_temp.reshape(256, LANES), wind_speed.reshape(256, LANES), halos
+        got, air_temp.reshape(256, LANES), wind_speed.reshape(256, LANES), halos
     )
     back = lax.all_to_all(answer, AXES, split_axis=0, concat_axis=0, tiled=True)
     t1, s1, *edges = first_step(fields, land_mask, in_vmem(own), halos)
-    t1, s1, heat, top, *sent, own = add_heat(t1, s1, *edges, land_mask, temp, back, codes)
+    s1, heat, top, *sent, own = add_heat(s1, *edges, land_mask, back, codes)
     later = exchange(*sent)
     return second_step(t1, s1, fields[2:], land_mask, top, heat, own, later, halos)
 

time: 81.4 us -> 78.8 us (0.968)
  blocking collectives: 16.8 us -> 0 us
  starting transfers between devices: 22.6 us -> 32.5 us
  waiting for transfers between devices: 10.3 us -> 14.2 us
  Pallas kernels: 30.1 us -> 31 us
    all_to_all x1 -> x0, blocking collectives: 16.8 us -> none  [body(): ids = lax.all_to_all(ids, AXES, split_axis=0, concat_axis=0, tiled=True)]
    all_to_all x0 -> x1, starting transfers between devices: none -> 10.2 us  [body(): got = lax.all_to_all(request, AXES, split_axis=0, concat_axis=0, tiled=True)]
    ppermute x2, waiting for transfers between devices: 3.68 us -> 11.5 us  [exchange(): got_lat_b = lax.ppermute(lat_b, AXES, route)]
    all_to_all x1, waiting for transfers between devices: 6.56 us -> 1.1 us  [body(): back = lax.all_to_all(answer, AXES, split_axis=0, concat_axis=0, tiled=True)]
    ppermute x2, starting transfers between devices: 6.63 us -> 8.82 us  [exchange(): got_lon_b = lax.ppermute(lon_b, 'lon', ring)]
    ppermute x2, starting transfers between devices: 7.05 us -> 4.94 us  [exchange(): got_lat_b = lax.ppermute(lat_b, AXES, route)]
    pallas_call x4, Pallas kernels: 16.9 us -> 18.3 us  [the longest x1 10.4 us: first_step(): pl.pallas_call(first_kernel, out_shape=(buf, shape, pltpu.VMEM((ROWS, 2 *...]
    ppermute x2, waiting for transfers between devices: 0.01 us -> 1.36 us  [exchange(): got_lat_a = lax.ppermute(lat_a, 'lat', swap_pairs(0, n_lat))]
  transfers between devices with their start and end apart: 9 -> 10, of which waited for: 2 -> 6; matrix products, arithmetic and copies ran while one was open for 0% -> 0% of each run, Pallas kernels for 15% -> 18%
where the time goes in v4:
time: 78.8 us; the launch traced here: 78.4 us
  starting transfers between devices  32.5 us (41%)
  Pallas kernels  31 us (39%)
  waiting for transfers between devices  14.2 us (18%)
    ppermute x2, waiting for transfers between devices, exchange(): got_lat_b = lax.ppermute(lat_b, AXES, route)  11.5 us
    pallas_call x1, Pallas kernels, first_step(): pl.pallas_call(first_kernel, out_shape=(buf, shape, pltpu.VMEM((ROWS, 2 *...  10.4 us
    all_to_all x1, starting transfers between devices, body(): got = lax.all_to_all(request, AXES, split_axis=0, concat_axis=0, tiled=True)  10.2 us
    ppermute x2, starting transfers between devices, exchange(): got_lon_b = lax.ppermute(lon_b, 'lon', ring)  8.82 us
    pallas_call x1, Pallas kernels, second_step(): pl.pallas_call(second_kernel, out_shape=(shape, shape, shape), in_specs=[...  8.7 us
    all_to_all x1, starting transfers between devices, body(): back = lax.all_to_all(answer, AXES, split_axis=0, concat_axis=0, tiled=True)  6.56 us
    ppermute x2, starting transfers between devices, exchange(): got_lat_b = lax.ppermute(lat_b, AXES, route)  4.94 us
    pallas_call x1, Pallas kernels, make_edges(): pl.pallas_call(edges_kernel, out_shape=(pltpu.VMEM((ROWS, LANES), F32), p...  3.96 us
  transfers between devices with their start and end apart: 10, of which 6 were waited for; matrix products, arithmetic and copies ran while one was open for 0% of the time, Pallas kernels for 18%

profile of v4, /device:TPU:38, one launch (start us, length us, event | category | flops | bytes accessed | tf_op | source)
XLA Modules:
  0.0 78.4 jit_solution(17903713278491085852)
XLA Ops:
  0.6 2.9 %request.1 = (f32[1152,128]{1,0:T(8,128)}, f32[256,128]{1,0:T(8,128)S(1)}) custom-call(s32[2,256]{1,0:T(2,128)} %bitcast.19, s32[2,256]{1,0:T(2,128)} %bitcast.20, f32[2,256]{1,0:T(2,128)} %bitcast.21, f32[16,128,256]{2,1,0:T(8,128)} %t_hbm.1), custom_call_target="tpu_custom_call" | custom-call | flops 500000000 | bytes 1048576 | tf_op jit(solution)/shard_map/request/pallas_call | solution.py:116
  3.5 10.2 %all-to-all-start = ((f32[128,1,1152]{2,1,0:T(1,128)}), f32[128,1,1152]{2,1,0:T(1,128)S(1)}, u32[]{:S(2)}, u32[]{:S(2)}) async-start(f32[128,1,1152]{2,1,0:T(1,128)} %bitcast.6), calls=%async_computation | async-start | bytes 1179648 | tf_op jit(solution)/shard_map/all_to_all | solution.py:714
  13.7 0.0 copy-start
  13.7 0.0 copy-start.1
  13.8 4.0 %edges.1 = (f32[128,128]{1,0:T(8,128)S(1)}, f32[128,128]{1,0:T(8,128)S(1)}, f32[64,256]{1,0:T(8,128)S(1)}, f32[64,256]{1,0:T(8,128)S(1)}, f32[128,128]{1,0:T(8,128)S(1)}) custom-call(f32[16,128,256]{2,1,0:T(8,128)} %t_hbm.1, f32[16,128,256]{2,1,0:T(8,128)} %s_hbm.1, f32[16,128,256]{2,1,0:T(8,128)} %u_hbm.3, f32[16,128,256]{2,1,0:T(8,128)} %v_hbm.3, ...), custom_call_target="tpu_custom_call" | custom-call | flops 100000000 | bytes 8388608 | tf_op jit(solution)/shard_map/edges/pallas_call | solution.py:195
  17.7 0.2 collective-permute-start
  17.9 4.9 %collective-permute-start.1 = (f32[128,128]{1,0:T(8,128)S(1)}, f32[128,128]{1,0:T(8,128)S(1)}, u32[]{:S(2)}, u32[]{:S(2)}) collective-permute-start(f32[128,128]{1,0:T(8,128)S(1)} %get-tuple-element.28), channel_id=1, source_target_pairs={{8,16},{16,8},{24,32},{32,24},{40,48},{48,40},{56,64},{64,56},{72,... | collective-permute-start | bytes 196616 | tf_op jit(solution)/shard_map/ppermute | solution.py:297
  22.8 0.8 %collective-permute-start.2 = (f32[64,256]{1,0:T(8,128)S(1)}, f32[64,256]{1,0:T(8,128)S(1)}, u32[]{:S(2)}, u32[]{:S(2)}) collective-permute-start(f32[64,256]{1,0:T(8,128)S(1)} %get-tuple-element.29), channel_id=1, source_target_pairs={{0,1},{1,0},{2,3},{3,2},{4,5},{5,4},{6,7},{7,6},{8,9},{9,8},{10,11... | collective-permute-start | bytes 196616 | tf_op jit(solution)/shard_map/ppermute | solution.py:298
  23.7 2.1 %collective-permute-start.3 = (f32[64,256]{1,0:T(8,128)S(1)}, f32[64,256]{1,0:T(8,128)S(1)}, u32[]{:S(2)}, u32[]{:S(2)}) collective-permute-start(f32[64,256]{1,0:T(8,128)S(1)} %get-tuple-element.30), channel_id=1, source_target_pairs={{1,2},{2,1},{3,4},{4,3},{5,6},{6,5},{9,10},{10,9},{11,12},{12,11},... | collective-permute-start | bytes 196616 | tf_op jit(solution)/shard_map/ppermute | solution.py:303
  25.8 0.0 collective-permute-done.lon_a.rest_0_.c_lon_a
  25.8 0.2 collective-permute-done.1.lon_b.rest_1_.c_lon_b
  26.0 1.1 %collective-permute-done.2.lat_a.rest_2_.c_lat_a = f32[64,256]{1,0:T(8,128)S(1)} collective-permute-done((f32[64,256]{1,0:T(8,128)S(1)}, f32[64,256]{1,0:T(8,128)S(1)}, u32[]{:S(2)}, u32[]{:S(2)}) %collective-permute-start.2) | collective-permute-done | bytes 65568 | tf_op jit(solution)/shard_map/ppermute | solution.py:298
  27.1 5.8 %collective-permute-done.3.lat_b.rest_3_.c_lat_b = f32[64,256]{1,0:T(8,128)S(1)} collective-permute-done((f32[64,256]{1,0:T(8,128)S(1)}, f32[64,256]{1,0:T(8,128)S(1)}, u32[]{:S(2)}, u32[]{:S(2)}) %collective-permute-start.3) | collective-permute-done | bytes 65568 | tf_op jit(solution)/shard_map/ppermute | solution.py:303
  32.9 0.0 all-to-all-done
  32.9 0.0 copy-done
  32.9 0.0 copy-done.1
  32.9 2.5 %answer.1 = f32[1024,128]{1,0:T(8,128)} custom-call(f32[1152,128]{1,0:T(8,128)S(1)} %bitcast.15, f32[256,128]{1,0:T(8,128)S(1)} %bitcast.17, f32[256,128]{1,0:T(8,128)S(1)} %bitcast.18, f32[128,128]{1,0:T(8,128)S(1)} %collective-permute-done.lon_a.rest_0_.c_lon_a, f32[128,128]{1,0:T(8,128)S(1)} %collective-permute-done.1.lon_b.rest_1_.c_lon_b, ...), custom_call_target="tpu_custom_call" | custom-call | flops 2000000000 | bytes 1048576 | tf_op jit(solution)/shard_map/answer/pallas_call | solution.py:242
  35.3 6.6 %all-to-all-start.1 = ((f32[128,8,128]{2,1,0:T(8,128)}), f32[128,8,128]{2,1,0:T(8,128)S(1)}, u32[]{:S(2)}, u32[]{:S(2)}) async-start(f32[128,8,128]{2,1,0:T(8,128)} %bitcast.10), calls=%async_computation.1 | async-start | bytes 1048576 | tf_op jit(solution)/shard_map/all_to_all | solution.py:721
  41.9 10.4 %first_step.1 = (f32[16,128,256]{2,1,0:T(8,128)S(1)}, f32[16,128,256]{2,1,0:T(8,128)}, f32[128,256]{1,0:T(8,128)S(1)}, f32[128,128]{1,0:T(8,128)S(1)}, f32[128,1...) custom-call(f32[16,128,256]{2,1,0:T(8,128)} %t_hbm.1, f32[16,128,256]{2,1,0:T(8,128)} %s_hbm.1, ...), custom_call_target="tpu_custom_call" | custom-call | flops 70000000 | bytes 26214400 | tf_op jit(solution)/shard_map/first_step/pallas_call | solution.py:524
  52.3 1.1 %all-to-all-done.1 = f32[128,8,128]{2,1,0:T(8,128)S(1)} async-done(((f32[128,8,128]{2,1,0:T(8,128)}), f32[128,8,128]{2,1,0:T(8,128)S(1)}, u32[]{:S(2)}, u32[]{:S(2)}) %all-to-all-start.1) | async-done | bytes 524320 | tf_op jit(solution)/shard_map/all_to_all | solution.py:721
  53.4 2.6 %heat.1 = (f32[16,128,256]{2,1,0:T(8,128)S(1)}, f32[128,256]{1,0:T(8,128)S(1)}, f32[128,256]{1,0:T(8,128)S(1)}, f32[128,128]{1,0:T(8,128)S(1)}, f32[128,128]{1,0...) custom-call(f32[128,256]{1,0:T(8,128)S(1)} %get-tuple-element.32.top_ref, ...), custom_call_target="tpu_custom_call" | custom-call | flops 1000000000 | bytes 1048576 | tf_op jit(solution)/shard_map/heat/pallas_call | solution.py:585
  56.0 0.1 collective-permute-start.4
  56.1 3.9 %collective-permute-start.5 = (f32[128,128]{1,0:T(8,128)S(1)}, f32[128,128]{1,0:T(8,128)S(1)}, u32[]{:S(2)}, u32[]{:S(2)}) collective-permute-start(f32[128,128]{1,0:T(8,128)S(1)} %get-tuple-element.44), channel_id=1, source_target_pairs={{8,16},{16,8},{24,32},{32,24},{40,48},{48,40},{56,64},{64,56},{72,... | collective-permute-start | bytes 196616 | tf_op jit(solution)/shard_map/ppermute | solution.py:297
  60.0 0.8 %collective-permute-start.6 = (f32[32,256]{1,0:T(8,128)S(1)}, f32[32,256]{1,0:T(8,128)S(1)}, u32[]{:S(2)}, u32[]{:S(2)}) collective-permute-start(f32[32,256]{1,0:T(8,128)S(1)} %get-tuple-element.45), channel_id=1, source_target_pairs={{0,1},{1,0},{2,3},{3,2},{4,5},{5,4},{6,7},{7,6},{8,9},{9,8},{10,11... | collective-permute-start | bytes 98312 | tf_op jit(solution)/shard_map/ppermute | solution.py:298
  60.8 2.9 %collective-permute-start.7 = (f32[32,256]{1,0:T(8,128)S(1)}, f32[32,256]{1,0:T(8,128)S(1)}, u32[]{:S(2)}, u32[]{:S(2)}) collective-permute-start(f32[32,256]{1,0:T(8,128)S(1)} %get-tuple-element.46), channel_id=1, source_target_pairs={{1,2},{2,1},{3,4},{4,3},{5,6},{6,5},{9,10},{10,9},{11,12},{12,11},... | collective-permute-start | bytes 98312 | tf_op jit(solution)/shard_map/ppermute | solution.py:303
  63.7 0.2 collective-permute-done.6.lat_a
  63.9 5.8 %collective-permute-done.7.lat_b = f32[32,256]{1,0:T(8,128)S(1)} collective-permute-done((f32[32,256]{1,0:T(8,128)S(1)}, f32[32,256]{1,0:T(8,128)S(1)}, u32[]{:S(2)}, u32[]{:S(2)}) %collective-permute-start.7) | collective-permute-done | bytes 32800 | tf_op jit(solution)/shard_map/ppermute | solution.py:303
  69.7 0.0 collective-permute-done.4.lon_a
  69.7 0.0 collective-permute-done.5.lon_b
  69.7 8.7 %second_step.1 = (f32[16,128,256]{2,1,0:T(8,128)}, f32[16,128,256]{2,1,0:T(8,128)}, f32[16,128,256]{2,1,0:T(8,128)}) custom-call(f32[16,128,256]{2,1,0:T(8,128)S(1)} %get-tuple-element.31.t_ref, f32[16,128,256]{2,1,0:T(8,128)S(1)} %get-tuple-element.39.s_ref, f32[16,128,256]{2,1,0:T(8,128)} %u_hbm.3, f32[16,128,256]{2,1,0:T(8,128)} %v_hbm.3, ...), custom_call_target="tpu_custom_call" | custom-call | flops 70000000 | bytes 26214400 | tf_op jit(solution)/shard_map/second_step/pallas_call | solution.py:679
Async XLA Ops:
  3.5 29.3 %all-to-all-start = ((f32[128,1,1152]{2,1,0:T(1,128)}), f32[128,1,1152]{2,1,0:T(1,128)S(1)}, u32[]{:S(2)}, u32[]{:S(2)}) async-start(f32[128,1,1152]{2,1,0:T(1,128)} %bitcast.6), calls=%async_computation | async-start | bytes 1179648 | tf_op jit(solution)/shard_map/all_to_all | solution.py:714
  13.7 19.1 %copy-start = (f32[1,1,256,128]{3,2,1,0:T(8,128)S(1)}, f32[1,1,256,128]{3,2,1,0:T(8,128)}, u32[]{:S(2)}) copy-start(f32[1,1,256,128]{3,2,1,0:T(8,128)} %param.20) | copy-start | bytes 393220
  13.7 19.1 %copy-start.1 = (f32[1,1,256,128]{3,2,1,0:T(8,128)S(1)}, f32[1,1,256,128]{3,2,1,0:T(8,128)}, u32[]{:S(2)}) copy-start(f32[1,1,256,128]{3,2,1,0:T(8,128)} %param.21) | copy-start | bytes 393220
  17.7 8.1 %collective-permute-start = (f32[128,128]{1,0:T(8,128)S(1)}, f32[128,128]{1,0:T(8,128)S(1)}, u32[]{:S(2)}, u32[]{:S(2)}) collective-permute-start(f32[128,128]{1,0:T(8,128)S(1)} %get-tuple-element.27), channel_id=1, source_target_pairs={{0,8},{8,0},{16,24},{24,16},{32,40},{40,32},{48,56},{56,48},{64,72... | collective-permute-start | bytes 196616 | tf_op jit(solution)/shard_map/ppermute | solution.py:296
  17.9 8.0 %collective-permute-start.1 = (f32[128,128]{1,0:T(8,128)S(1)}, f32[128,128]{1,0:T(8,128)S(1)}, u32[]{:S(2)}, u32[]{:S(2)}) collective-permute-start(f32[128,128]{1,0:T(8,128)S(1)} %get-tuple-element.28), channel_id=1, source_target_pairs={{8,16},{16,8},{24,32},{32,24},{40,48},{48,40},{56,64},{64,56},{72,... | collective-permute-start | bytes 196616 | tf_op jit(solution)/shard_map/ppermute | solution.py:297
  22.8 4.3 %collective-permute-start.2 = (f32[64,256]{1,0:T(8,128)S(1)}, f32[64,256]{1,0:T(8,128)S(1)}, u32[]{:S(2)}, u32[]{:S(2)}) collective-permute-start(f32[64,256]{1,0:T(8,128)S(1)} %get-tuple-element.29), channel_id=1, source_target_pairs={{0,1},{1,0},{2,3},{3,2},{4,5},{5,4},{6,7},{7,6},{8,9},{9,8},{10,11... | collective-permute-start | bytes 196616 | tf_op jit(solution)/shard_map/ppermute | solution.py:298
  23.7 9.2 %collective-permute-start.3 = (f32[64,256]{1,0:T(8,128)S(1)}, f32[64,256]{1,0:T(8,128)S(1)}, u32[]{:S(2)}, u32[]{:S(2)}) collective-permute-start(f32[64,256]{1,0:T(8,128)S(1)} %get-tuple-element.30), channel_id=1, source_target_pairs={{1,2},{2,1},{3,4},{4,3},{5,6},{6,5},{9,10},{10,9},{11,12},{12,11},... | collective-permute-start | bytes 196616 | tf_op jit(solution)/shard_map/ppermute | solution.py:303
  35.3 18.1 %all-to-all-start.1 = ((f32[128,8,128]{2,1,0:T(8,128)}), f32[128,8,128]{2,1,0:T(8,128)S(1)}, u32[]{:S(2)}, u32[]{:S(2)}) async-start(f32[128,8,128]{2,1,0:T(8,128)} %bitcast.10), calls=%async_computation.1 | async-start | bytes 1048576 | tf_op jit(solution)/shard_map/all_to_all | solution.py:721
  56.0 13.7 %collective-permute-start.4 = (f32[128,128]{1,0:T(8,128)S(1)}, f32[128,128]{1,0:T(8,128)S(1)}, u32[]{:S(2)}, u32[]{:S(2)}) collective-permute-start(f32[128,128]{1,0:T(8,128)S(1)} %get-tuple-element.43), channel_id=1, source_target_pairs={{0,8},{8,0},{16,24},{24,16},{32,40},{40,32},{48,56},{56,48},{64,72... | collective-permute-start | bytes 196616 | tf_op jit(solution)/shard_map/ppermute | solution.py:296
  56.1 13.6 %collective-permute-start.5 = (f32[128,128]{1,0:T(8,128)S(1)}, f32[128,128]{1,0:T(8,128)S(1)}, u32[]{:S(2)}, u32[]{:S(2)}) collective-permute-start(f32[128,128]{1,0:T(8,128)S(1)} %get-tuple-element.44), channel_id=1, source_target_pairs={{8,16},{16,8},{24,32},{32,24},{40,48},{48,40},{56,64},{64,56},{72,... | collective-permute-start | bytes 196616 | tf_op jit(solution)/shard_map/ppermute | solution.py:297
  60.0 3.9 %collective-permute-start.6 = (f32[32,256]{1,0:T(8,128)S(1)}, f32[32,256]{1,0:T(8,128)S(1)}, u32[]{:S(2)}, u32[]{:S(2)}) collective-permute-start(f32[32,256]{1,0:T(8,128)S(1)} %get-tuple-element.45), channel_id=1, source_target_pairs={{0,1},{1,0},{2,3},{3,2},{4,5},{5,4},{6,7},{7,6},{8,9},{9,8},{10,11... | collective-permute-start | bytes 98312 | tf_op jit(solution)/shard_map/ppermute | solution.py:298
  60.8 8.8 %collective-permute-start.7 = (f32[32,256]{1,0:T(8,128)S(1)}, f32[32,256]{1,0:T(8,128)S(1)}, u32[]{:S(2)}, u32[]{:S(2)}) collective-permute-start(f32[32,256]{1,0:T(8,128)S(1)} %get-tuple-element.46), channel_id=1, source_target_pairs={{1,2},{2,1},{3,4},{4,3},{5,6},{6,5},{9,10},{10,9},{11,12},{12,11},... | collective-permute-start | bytes 98312 | tf_op jit(solution)/shard_map/ppermute | solution.py:303

commit v5 on v4

--- a/solution.py
+++ b/solution.py
@@ -220,8 +220,8 @@
     patches = jnp.concatenate([air_ref[...], wind_ref[...]], axis=1)
     high, middle, low = pieces(patches)
     spread = jnp.ones((128, 256), BF16)
-    chunk = 128
-    for part in range(8):
+    chunk = 512
+    for part in range(2):
         line = iota((chunk, 128), 0) + part * chunk
         lane = iota((chunk, 128), 1)
         rows = dot(as_bf16(line // SLOTS == lane), ids)
@@ -552,12 +552,12 @@
     high, middle, low = pieces(back_ref[...])
     codes = codes_ref[...]
     lane = iota((256, 1024), 1)
-    heat = None
-    for m in range(2):
-        onehot = as_bf16(codes[:, m : m + 1].astype(jnp.int32) == lane)
-        flux = dot(onehot, high) + (dot(onehot, middle) + dot(onehot, low))
-        part = codes[:, 2 + m : 3 + m] * flux
-        heat = part if heat is None else heat + part
+    onehot = jnp.concatenate(
+        [as_bf16(codes[:, m : m + 1].astype(jnp.int32) == lane) for m in range(2)], axis=0
+    )
+    upper = dot(onehot, jnp.concatenate([high, middle], axis=1))
+    flux = upper[:, :LANES] + (upper[:, LANES:] + dot(onehot, low))
+    heat = codes[:, 2:3] * flux[:256] + codes[:, 3:4] * flux[256:]
     mask_copy.wait()
     mask = mask_ref[...].astype(F32)
     added = []

time: 78.8 us -> 77.7 us (0.986)
  Pallas kernels: 31 us -> 29.8 us
    pallas_call x1, Pallas kernels: 2.45 us -> 1.64 us  [make_answer(): pl.pallas_call(answer_kernel, out_shape=pltpu.VMEM((128 * SLOTS, LANES),...]
  transfers between devices with their start and end apart: 10 -> 10, of which waited for: 6 -> 6; matrix products, arithmetic and copies ran while one was open for 0% -> 0% of each run, Pallas kernels for 18% -> 19%
where the time goes in v5:
time: 77.7 us; the launch traced here: 77.2 us
  starting transfers between devices  32.5 us (42%)
  Pallas kernels  29.8 us (38%)
  waiting for transfers between devices  14.2 us (18%)
    ppermute x2, waiting for transfers between devices, exchange(): got_lat_b = lax.ppermute(lat_b, AXES, route)  11.5 us
    pallas_call x1, Pallas kernels, first_step(): pl.pallas_call(first_kernel, out_shape=(buf, shape, pltpu.VMEM((ROWS, 2 *...  10.4 us
    all_to_all x1, starting transfers between devices, body(): got = lax.all_to_all(request, AXES, split_axis=0, concat_axis=0, tiled=True)  10.2 us
    ppermute x2, starting transfers between devices, exchange(): got_lon_b = lax.ppermute(lon_b, 'lon', ring)  8.82 us
    pallas_call x1, Pallas kernels, second_step(): pl.pallas_call(second_kernel, out_shape=(shape, shape, shape), in_specs=[...  8.7 us
    all_to_all x1, starting transfers between devices, body(): back = lax.all_to_all(answer, AXES, split_axis=0, concat_axis=0, tiled=True)  6.56 us
    ppermute x2, starting transfers between devices, exchange(): got_lat_b = lax.ppermute(lat_b, AXES, route)  4.95 us
    pallas_call x1, Pallas kernels, make_edges(): pl.pallas_call(edges_kernel, out_shape=(pltpu.VMEM((ROWS, LANES), F32), p...  3.96 us
  transfers between devices with their start and end apart: 10, of which 6 were waited for; matrix products, arithmetic and copies ran while one was open for 0% of the time, Pallas kernels for 19%

profile of v5, /device:TPU:38, one launch (start us, length us, event | category | flops | bytes accessed | tf_op | source)
XLA Modules:
  0.0 77.2 jit_solution(17125406498766869863)
XLA Ops:
  0.6 2.9 %request.1 = (f32[1152,128]{1,0:T(8,128)}, f32[256,128]{1,0:T(8,128)S(1)}) custom-call(s32[2,256]{1,0:T(2,128)} %bitcast.19, s32[2,256]{1,0:T(2,128)} %bitcast.20, f32[2,256]{1,0:T(2,128)} %bitcast.21, f32[16,128,256]{2,1,0:T(8,128)} %t_hbm.1), custom_call_target="tpu_custom_call" | custom-call | flops 500000000 | bytes 1048576 | tf_op jit(solution)/shard_map/request/pallas_call | solution.py:116
  3.5 10.2 %all-to-all-start = ((f32[128,1,1152]{2,1,0:T(1,128)}), f32[128,1,1152]{2,1,0:T(1,128)S(1)}, u32[]{:S(2)}, u32[]{:S(2)}) async-start(f32[128,1,1152]{2,1,0:T(1,128)} %bitcast.6), calls=%async_computation | async-start | bytes 1179648 | tf_op jit(solution)/shard_map/all_to_all | solution.py:714
  13.7 0.0 copy-start
  13.7 0.0 copy-start.1
  13.8 4.0 %edges.1 = (f32[128,128]{1,0:T(8,128)S(1)}, f32[128,128]{1,0:T(8,128)S(1)}, f32[64,256]{1,0:T(8,128)S(1)}, f32[64,256]{1,0:T(8,128)S(1)}, f32[128,128]{1,0:T(8,128)S(1)}) custom-call(f32[16,128,256]{2,1,0:T(8,128)} %t_hbm.1, f32[16,128,256]{2,1,0:T(8,128)} %s_hbm.1, f32[16,128,256]{2,1,0:T(8,128)} %u_hbm.3, f32[16,128,256]{2,1,0:T(8,128)} %v_hbm.3, ...), custom_call_target="tpu_custom_call" | custom-call | flops 100000000 | bytes 8388608 | tf_op jit(solution)/shard_map/edges/pallas_call | solution.py:195
  17.7 0.2 collective-permute-start
  17.9 4.9 %collective-permute-start.1 = (f32[128,128]{1,0:T(8,128)S(1)}, f32[128,128]{1,0:T(8,128)S(1)}, u32[]{:S(2)}, u32[]{:S(2)}) collective-permute-start(f32[128,128]{1,0:T(8,128)S(1)} %get-tuple-element.28), channel_id=1, source_target_pairs={{8,16},{16,8},{24,32},{32,24},{40,48},{48,40},{56,64},{64,56},{72,... | collective-permute-start | bytes 196616 | tf_op jit(solution)/shard_map/ppermute | solution.py:297
  22.8 0.8 %collective-permute-start.2 = (f32[64,256]{1,0:T(8,128)S(1)}, f32[64,256]{1,0:T(8,128)S(1)}, u32[]{:S(2)}, u32[]{:S(2)}) collective-permute-start(f32[64,256]{1,0:T(8,128)S(1)} %get-tuple-element.29), channel_id=1, source_target_pairs={{0,1},{1,0},{2,3},{3,2},{4,5},{5,4},{6,7},{7,6},{8,9},{9,8},{10,11... | collective-permute-start | bytes 196616 | tf_op jit(solution)/shard_map/ppermute | solution.py:298
  23.7 2.1 %collective-permute-start.3 = (f32[64,256]{1,0:T(8,128)S(1)}, f32[64,256]{1,0:T(8,128)S(1)}, u32[]{:S(2)}, u32[]{:S(2)}) collective-permute-start(f32[64,256]{1,0:T(8,128)S(1)} %get-tuple-element.30), channel_id=1, source_target_pairs={{1,2},{2,1},{3,4},{4,3},{5,6},{6,5},{9,10},{10,9},{11,12},{12,11},... | collective-permute-start | bytes 196616 | tf_op jit(solution)/shard_map/ppermute | solution.py:303
  25.8 0.0 collective-permute-done.lon_a.rest_0_.c_lon_a
  25.8 0.2 collective-permute-done.1.lon_b.rest_1_.c_lon_b
  26.0 1.1 %collective-permute-done.2.lat_a.rest_2_.c_lat_a = f32[64,256]{1,0:T(8,128)S(1)} collective-permute-done((f32[64,256]{1,0:T(8,128)S(1)}, f32[64,256]{1,0:T(8,128)S(1)}, u32[]{:S(2)}, u32[]{:S(2)}) %collective-permute-start.2) | collective-permute-done | bytes 65568 | tf_op jit(solution)/shard_map/ppermute | solution.py:298
  27.1 5.8 %collective-permute-done.3.lat_b.rest_3_.c_lat_b = f32[64,256]{1,0:T(8,128)S(1)} collective-permute-done((f32[64,256]{1,0:T(8,128)S(1)}, f32[64,256]{1,0:T(8,128)S(1)}, u32[]{:S(2)}, u32[]{:S(2)}) %collective-permute-start.3) | collective-permute-done | bytes 65568 | tf_op jit(solution)/shard_map/ppermute | solution.py:303
  32.9 0.0 all-to-all-done
  32.9 0.0 copy-done
  32.9 0.0 copy-done.1
  32.9 1.6 %answer.1 = f32[1024,128]{1,0:T(8,128)} custom-call(f32[1152,128]{1,0:T(8,128)S(1)} %bitcast.15, f32[256,128]{1,0:T(8,128)S(1)} %bitcast.17, f32[256,128]{1,0:T(8,128)S(1)} %bitcast.18, f32[128,128]{1,0:T(8,128)S(1)} %collective-permute-done.lon_a.rest_0_.c_lon_a, f32[128,128]{1,0:T(8,128)S(1)} %collective-permute-done.1.lon_b.rest_1_.c_lon_b, ...), custom_call_target="tpu_custom_call" | custom-call | flops 2000000000 | bytes 1048576 | tf_op jit(solution)/shard_map/answer/pallas_call | solution.py:242
  34.5 6.6 %all-to-all-start.1 = ((f32[128,8,128]{2,1,0:T(8,128)}), f32[128,8,128]{2,1,0:T(8,128)S(1)}, u32[]{:S(2)}, u32[]{:S(2)}) async-start(f32[128,8,128]{2,1,0:T(8,128)} %bitcast.10), calls=%async_computation.1 | async-start | bytes 1048576 | tf_op jit(solution)/shard_map/all_to_all | solution.py:721
  41.1 10.4 %first_step.1 = (f32[16,128,256]{2,1,0:T(8,128)S(1)}, f32[16,128,256]{2,1,0:T(8,128)}, f32[128,256]{1,0:T(8,128)S(1)}, f32[128,128]{1,0:T(8,128)S(1)}, f32[128,1...) custom-call(f32[16,128,256]{2,1,0:T(8,128)} %t_hbm.1, f32[16,128,256]{2,1,0:T(8,128)} %s_hbm.1, ...), custom_call_target="tpu_custom_call" | custom-call | flops 70000000 | bytes 26214400 | tf_op jit(solution)/shard_map/first_step/pallas_call | solution.py:524
  51.5 1.1 %all-to-all-done.1 = f32[128,8,128]{2,1,0:T(8,128)S(1)} async-done(((f32[128,8,128]{2,1,0:T(8,128)}), f32[128,8,128]{2,1,0:T(8,128)S(1)}, u32[]{:S(2)}, u32[]{:S(2)}) %all-to-all-start.1) | async-done | bytes 524320 | tf_op jit(solution)/shard_map/all_to_all | solution.py:721
  52.6 2.2 %heat.1 = (f32[16,128,256]{2,1,0:T(8,128)S(1)}, f32[128,256]{1,0:T(8,128)S(1)}, f32[128,256]{1,0:T(8,128)S(1)}, f32[128,128]{1,0:T(8,128)S(1)}, f32[128,128]{1,0...) custom-call(f32[128,256]{1,0:T(8,128)S(1)} %get-tuple-element.32.top_ref, ...), custom_call_target="tpu_custom_call" | custom-call | flops 1000000000 | bytes 1048576 | tf_op jit(solution)/shard_map/heat/pallas_call | solution.py:585
  54.8 0.1 collective-permute-start.4
  54.9 3.9 %collective-permute-start.5 = (f32[128,128]{1,0:T(8,128)S(1)}, f32[128,128]{1,0:T(8,128)S(1)}, u32[]{:S(2)}, u32[]{:S(2)}) collective-permute-start(f32[128,128]{1,0:T(8,128)S(1)} %get-tuple-element.44), channel_id=1, source_target_pairs={{8,16},{16,8},{24,32},{32,24},{40,48},{48,40},{56,64},{64,56},{72,... | collective-permute-start | bytes 196616 | tf_op jit(solution)/shard_map/ppermute | solution.py:297
  58.8 0.8 %collective-permute-start.6 = (f32[32,256]{1,0:T(8,128)S(1)}, f32[32,256]{1,0:T(8,128)S(1)}, u32[]{:S(2)}, u32[]{:S(2)}) collective-permute-start(f32[32,256]{1,0:T(8,128)S(1)} %get-tuple-element.45), channel_id=1, source_target_pairs={{0,1},{1,0},{2,3},{3,2},{4,5},{5,4},{6,7},{7,6},{8,9},{9,8},{10,11... | collective-permute-start | bytes 98312 | tf_op jit(solution)/shard_map/ppermute | solution.py:298
  59.7 2.9 %collective-permute-start.7 = (f32[32,256]{1,0:T(8,128)S(1)}, f32[32,256]{1,0:T(8,128)S(1)}, u32[]{:S(2)}, u32[]{:S(2)}) collective-permute-start(f32[32,256]{1,0:T(8,128)S(1)} %get-tuple-element.46), channel_id=1, source_target_pairs={{1,2},{2,1},{3,4},{4,3},{5,6},{6,5},{9,10},{10,9},{11,12},{12,11},... | collective-permute-start | bytes 98312 | tf_op jit(solution)/shard_map/ppermute | solution.py:303
  62.5 0.2 collective-permute-done.6.lat_a
  62.8 5.8 %collective-permute-done.7.lat_b = f32[32,256]{1,0:T(8,128)S(1)} collective-permute-done((f32[32,256]{1,0:T(8,128)S(1)}, f32[32,256]{1,0:T(8,128)S(1)}, u32[]{:S(2)}, u32[]{:S(2)}) %collective-permute-start.7) | collective-permute-done | bytes 32800 | tf_op jit(solution)/shard_map/ppermute | solution.py:303
  68.5 0.0 collective-permute-done.4.lon_a
  68.5 0.0 collective-permute-done.5.lon_b
  68.5 8.7 %second_step.1 = (f32[16,128,256]{2,1,0:T(8,128)}, f32[16,128,256]{2,1,0:T(8,128)}, f32[16,128,256]{2,1,0:T(8,128)}) custom-call(f32[16,128,256]{2,1,0:T(8,128)S(1)} %get-tuple-element.31.t_ref, f32[16,128,256]{2,1,0:T(8,128)S(1)} %get-tuple-element.39.s_ref, f32[16,128,256]{2,1,0:T(8,128)} %u_hbm.3, f32[16,128,256]{2,1,0:T(8,128)} %v_hbm.3, ...), custom_call_target="tpu_custom_call" | custom-call | flops 70000000 | bytes 26214400 | tf_op jit(solution)/shard_map/second_step/pallas_call | solution.py:679
Async XLA Ops:
  3.5 29.3 %all-to-all-start = ((f32[128,1,1152]{2,1,0:T(1,128)}), f32[128,1,1152]{2,1,0:T(1,128)S(1)}, u32[]{:S(2)}, u32[]{:S(2)}) async-start(f32[128,1,1152]{2,1,0:T(1,128)} %bitcast.6), calls=%async_computation | async-start | bytes 1179648 | tf_op jit(solution)/shard_map/all_to_all | solution.py:714
  13.7 19.1 %copy-start = (f32[1,1,256,128]{3,2,1,0:T(8,128)S(1)}, f32[1,1,256,128]{3,2,1,0:T(8,128)}, u32[]{:S(2)}) copy-start(f32[1,1,256,128]{3,2,1,0:T(8,128)} %param.20) | copy-start | bytes 393220
  13.7 19.1 %copy-start.1 = (f32[1,1,256,128]{3,2,1,0:T(8,128)S(1)}, f32[1,1,256,128]{3,2,1,0:T(8,128)}, u32[]{:S(2)}) copy-start(f32[1,1,256,128]{3,2,1,0:T(8,128)} %param.21) | copy-start | bytes 393220
  17.7 8.1 %collective-permute-start = (f32[128,128]{1,0:T(8,128)S(1)}, f32[128,128]{1,0:T(8,128)S(1)}, u32[]{:S(2)}, u32[]{:S(2)}) collective-permute-start(f32[128,128]{1,0:T(8,128)S(1)} %get-tuple-element.27), channel_id=1, source_target_pairs={{0,8},{8,0},{16,24},{24,16},{32,40},{40,32},{48,56},{56,48},{64,72... | collective-permute-start | bytes 196616 | tf_op jit(solution)/shard_map/ppermute | solution.py:296
  17.9 8.0 %collective-permute-start.1 = (f32[128,128]{1,0:T(8,128)S(1)}, f32[128,128]{1,0:T(8,128)S(1)}, u32[]{:S(2)}, u32[]{:S(2)}) collective-permute-start(f32[128,128]{1,0:T(8,128)S(1)} %get-tuple-element.28), channel_id=1, source_target_pairs={{8,16},{16,8},{24,32},{32,24},{40,48},{48,40},{56,64},{64,56},{72,... | collective-permute-start | bytes 196616 | tf_op jit(solution)/shard_map/ppermute | solution.py:297
  22.8 4.3 %collective-permute-start.2 = (f32[64,256]{1,0:T(8,128)S(1)}, f32[64,256]{1,0:T(8,128)S(1)}, u32[]{:S(2)}, u32[]{:S(2)}) collective-permute-start(f32[64,256]{1,0:T(8,128)S(1)} %get-tuple-element.29), channel_id=1, source_target_pairs={{0,1},{1,0},{2,3},{3,2},{4,5},{5,4},{6,7},{7,6},{8,9},{9,8},{10,11... | collective-permute-start | bytes 196616 | tf_op jit(solution)/shard_map/ppermute | solution.py:298
  23.7 9.2 %collective-permute-start.3 = (f32[64,256]{1,0:T(8,128)S(1)}, f32[64,256]{1,0:T(8,128)S(1)}, u32[]{:S(2)}, u32[]{:S(2)}) collective-permute-start(f32[64,256]{1,0:T(8,128)S(1)} %get-tuple-element.30), channel_id=1, source_target_pairs={{1,2},{2,1},{3,4},{4,3},{5,6},{6,5},{9,10},{10,9},{11,12},{12,11},... | collective-permute-start | bytes 196616 | tf_op jit(solution)/shard_map/ppermute | solution.py:303
  34.5 18.1 %all-to-all-start.1 = ((f32[128,8,128]{2,1,0:T(8,128)}), f32[128,8,128]{2,1,0:T(8,128)S(1)}, u32[]{:S(2)}, u32[]{:S(2)}) async-start(f32[128,8,128]{2,1,0:T(8,128)} %bitcast.10), calls=%async_computation.1 | async-start | bytes 1048576 | tf_op jit(solution)/shard_map/all_to_all | solution.py:721
  54.8 13.7 %collective-permute-start.4 = (f32[128,128]{1,0:T(8,128)S(1)}, f32[128,128]{1,0:T(8,128)S(1)}, u32[]{:S(2)}, u32[]{:S(2)}) collective-permute-start(f32[128,128]{1,0:T(8,128)S(1)} %get-tuple-element.43), channel_id=1, source_target_pairs={{0,8},{8,0},{16,24},{24,16},{32,40},{40,32},{48,56},{56,48},{64,72... | collective-permute-start | bytes 196616 | tf_op jit(solution)/shard_map/ppermute | solution.py:296
  54.9 13.6 %collective-permute-start.5 = (f32[128,128]{1,0:T(8,128)S(1)}, f32[128,128]{1,0:T(8,128)S(1)}, u32[]{:S(2)}, u32[]{:S(2)}) collective-permute-start(f32[128,128]{1,0:T(8,128)S(1)} %get-tuple-element.44), channel_id=1, source_target_pairs={{8,16},{16,8},{24,32},{32,24},{40,48},{48,40},{56,64},{64,56},{72,... | collective-permute-start | bytes 196616 | tf_op jit(solution)/shard_map/ppermute | solution.py:297
  58.8 3.9 %collective-permute-start.6 = (f32[32,256]{1,0:T(8,128)S(1)}, f32[32,256]{1,0:T(8,128)S(1)}, u32[]{:S(2)}, u32[]{:S(2)}) collective-permute-start(f32[32,256]{1,0:T(8,128)S(1)} %get-tuple-element.45), channel_id=1, source_target_pairs={{0,1},{1,0},{2,3},{3,2},{4,5},{5,4},{6,7},{7,6},{8,9},{9,8},{10,11... | collective-permute-start | bytes 98312 | tf_op jit(solution)/shard_map/ppermute | solution.py:298
  59.7 8.8 %collective-permute-start.7 = (f32[32,256]{1,0:T(8,128)S(1)}, f32[32,256]{1,0:T(8,128)S(1)}, u32[]{:S(2)}, u32[]{:S(2)}) collective-permute-start(f32[32,256]{1,0:T(8,128)S(1)} %get-tuple-element.46), channel_id=1, source_target_pairs={{1,2},{2,1},{3,4},{4,3},{5,6},{6,5},{9,10},{10,9},{11,12},{12,11},... | collective-permute-start | bytes 98312 | tf_op jit(solution)/shard_map/ppermute | solution.py:303

commit v6 on v5

--- a/solution.py
+++ b/solution.py
@@ -656,7 +656,7 @@
 
         def send():
             for copy in copies(index // 2):
-                copy.start()
+                copy.start(priority=1)
 
         if last:
             send()

time: 77.7 us -> 77.7 us (level)
  no operation moved by 1% of the time
where the time goes in v6:
time: 77.7 us; the launch traced here: 77.2 us
  starting transfers between devices  32.5 us (42%)
  Pallas kernels  29.8 us (38%)
  waiting for transfers between devices  14.2 us (18%)
    ppermute x2, waiting for transfers between devices, exchange(): got_lat_b = lax.ppermute(lat_b, AXES, route)  11.5 us
    pallas_call x1, Pallas kernels, first_step(): pl.pallas_call(first_kernel, out_shape=(buf, shape, pltpu.VMEM((ROWS, 2 *...  10.4 us
    all_to_all x1, starting transfers between devices, body(): got = lax.all_to_all(request, AXES, split_axis=0, concat_axis=0, tiled=True)  10.2 us
    ppermute x2, starting transfers between devices, exchange(): got_lon_b = lax.ppermute(lon_b, 'lon', ring)  8.82 us
    pallas_call x1, Pallas kernels, second_step(): pl.pallas_call(second_kernel, out_shape=(shape, shape, shape), in_specs=[...  8.7 us
    all_to_all x1, starting transfers between devices, body(): back = lax.all_to_all(answer, AXES, split_axis=0, concat_axis=0, tiled=True)  6.56 us
    ppermute x2, starting transfers between devices, exchange(): got_lat_b = lax.ppermute(lat_b, AXES, route)  4.95 us
    pallas_call x1, Pallas kernels, make_edges(): pl.pallas_call(edges_kernel, out_shape=(pltpu.VMEM((ROWS, LANES), F32), p...  3.96 us
  transfers between devices with their start and end apart: 10, of which 6 were waited for; matrix products, arithmetic and copies ran while one was open for 0% of the time, Pallas kernels for 19%

profile of v6, /device:TPU:38, one launch (start us, length us, event | category | flops | bytes accessed | tf_op | source)
XLA Modules:
  0.0 77.2 jit_solution(9649280948001396063)
XLA Ops:
  0.6 2.9 %request.1 = (f32[1152,128]{1,0:T(8,128)}, f32[256,128]{1,0:T(8,128)S(1)}) custom-call(s32[2,256]{1,0:T(2,128)} %bitcast.19, s32[2,256]{1,0:T(2,128)} %bitcast.20, f32[2,256]{1,0:T(2,128)} %bitcast.21, f32[16,128,256]{2,1,0:T(8,128)} %t_hbm.1), custom_call_target="tpu_custom_call" | custom-call | flops 500000000 | bytes 1048576 | tf_op jit(solution)/shard_map/request/pallas_call | solution.py:116
  3.5 10.2 %all-to-all-start = ((f32[128,1,1152]{2,1,0:T(1,128)}), f32[128,1,1152]{2,1,0:T(1,128)S(1)}, u32[]{:S(2)}, u32[]{:S(2)}) async-start(f32[128,1,1152]{2,1,0:T(1,128)} %bitcast.6), calls=%async_computation | async-start | bytes 1179648 | tf_op jit(solution)/shard_map/all_to_all | solution.py:714
  13.7 0.0 copy-start
  13.7 0.0 copy-start.1
  13.8 4.0 %edges.1 = (f32[128,128]{1,0:T(8,128)S(1)}, f32[128,128]{1,0:T(8,128)S(1)}, f32[64,256]{1,0:T(8,128)S(1)}, f32[64,256]{1,0:T(8,128)S(1)}, f32[128,128]{1,0:T(8,128)S(1)}) custom-call(f32[16,128,256]{2,1,0:T(8,128)} %t_hbm.1, f32[16,128,256]{2,1,0:T(8,128)} %s_hbm.1, f32[16,128,256]{2,1,0:T(8,128)} %u_hbm.3, f32[16,128,256]{2,1,0:T(8,128)} %v_hbm.3, ...), custom_call_target="tpu_custom_call" | custom-call | flops 100000000 | bytes 8388608 | tf_op jit(solution)/shard_map/edges/pallas_call | solution.py:195
  17.7 0.2 collective-permute-start
  17.9 4.9 %collective-permute-start.1 = (f32[128,128]{1,0:T(8,128)S(1)}, f32[128,128]{1,0:T(8,128)S(1)}, u32[]{:S(2)}, u32[]{:S(2)}) collective-permute-start(f32[128,128]{1,0:T(8,128)S(1)} %get-tuple-element.28), channel_id=1, source_target_pairs={{8,16},{16,8},{24,32},{32,24},{40,48},{48,40},{56,64},{64,56},{72,... | collective-permute-start | bytes 196616 | tf_op jit(solution)/shard_map/ppermute | solution.py:297
  22.8 0.8 %collective-permute-start.2 = (f32[64,256]{1,0:T(8,128)S(1)}, f32[64,256]{1,0:T(8,128)S(1)}, u32[]{:S(2)}, u32[]{:S(2)}) collective-permute-start(f32[64,256]{1,0:T(8,128)S(1)} %get-tuple-element.29), channel_id=1, source_target_pairs={{0,1},{1,0},{2,3},{3,2},{4,5},{5,4},{6,7},{7,6},{8,9},{9,8},{10,11... | collective-permute-start | bytes 196616 | tf_op jit(solution)/shard_map/ppermute | solution.py:298
  23.7 2.1 %collective-permute-start.3 = (f32[64,256]{1,0:T(8,128)S(1)}, f32[64,256]{1,0:T(8,128)S(1)}, u32[]{:S(2)}, u32[]{:S(2)}) collective-permute-start(f32[64,256]{1,0:T(8,128)S(1)} %get-tuple-element.30), channel_id=1, source_target_pairs={{1,2},{2,1},{3,4},{4,3},{5,6},{6,5},{9,10},{10,9},{11,12},{12,11},... | collective-permute-start | bytes 196616 | tf_op jit(solution)/shard_map/ppermute | solution.py:303
  25.8 0.0 collective-permute-done.lon_a.rest_0_.c_lon_a
  25.8 0.2 collective-permute-done.1.lon_b.rest_1_.c_lon_b
  26.0 1.1 %collective-permute-done.2.lat_a.rest_2_.c_lat_a = f32[64,256]{1,0:T(8,128)S(1)} collective-permute-done((f32[64,256]{1,0:T(8,128)S(1)}, f32[64,256]{1,0:T(8,128)S(1)}, u32[]{:S(2)}, u32[]{:S(2)}) %collective-permute-start.2) | collective-permute-done | bytes 65568 | tf_op jit(solution)/shard_map/ppermute | solution.py:298
  27.1 5.8 %collective-permute-done.3.lat_b.rest_3_.c_lat_b = f32[64,256]{1,0:T(8,128)S(1)} collective-permute-done((f32[64,256]{1,0:T(8,128)S(1)}, f32[64,256]{1,0:T(8,128)S(1)}, u32[]{:S(2)}, u32[]{:S(2)}) %collective-permute-start.3) | collective-permute-done | bytes 65568 | tf_op jit(solution)/shard_map/ppermute | solution.py:303
  32.9 0.0 all-to-all-done
  32.9 0.0 copy-done
  32.9 0.0 copy-done.1
  32.9 1.6 %answer.1 = f32[1024,128]{1,0:T(8,128)} custom-call(f32[1152,128]{1,0:T(8,128)S(1)} %bitcast.15, f32[256,128]{1,0:T(8,128)S(1)} %bitcast.17, f32[256,128]{1,0:T(8,128)S(1)} %bitcast.18, f32[128,128]{1,0:T(8,128)S(1)} %collective-permute-done.lon_a.rest_0_.c_lon_a, f32[128,128]{1,0:T(8,128)S(1)} %collective-permute-done.1.lon_b.rest_1_.c_lon_b, ...), custom_call_target="tpu_custom_call" | custom-call | flops 2000000000 | bytes 1048576 | tf_op jit(solution)/shard_map/answer/pallas_call | solution.py:242
  34.5 6.6 %all-to-all-start.1 = ((f32[128,8,128]{2,1,0:T(8,128)}), f32[128,8,128]{2,1,0:T(8,128)S(1)}, u32[]{:S(2)}, u32[]{:S(2)}) async-start(f32[128,8,128]{2,1,0:T(8,128)} %bitcast.10), calls=%async_computation.1 | async-start | bytes 1048576 | tf_op jit(solution)/shard_map/all_to_all | solution.py:721
  41.1 10.4 %first_step.1 = (f32[16,128,256]{2,1,0:T(8,128)S(1)}, f32[16,128,256]{2,1,0:T(8,128)}, f32[128,256]{1,0:T(8,128)S(1)}, f32[128,128]{1,0:T(8,128)S(1)}, f32[128,1...) custom-call(f32[16,128,256]{2,1,0:T(8,128)} %t_hbm.1, f32[16,128,256]{2,1,0:T(8,128)} %s_hbm.1, ...), custom_call_target="tpu_custom_call" | custom-call | flops 70000000 | bytes 26214400 | tf_op jit(solution)/shard_map/first_step/pallas_call | solution.py:524
  51.5 1.1 %all-to-all-done.1 = f32[128,8,128]{2,1,0:T(8,128)S(1)} async-done(((f32[128,8,128]{2,1,0:T(8,128)}), f32[128,8,128]{2,1,0:T(8,128)S(1)}, u32[]{:S(2)}, u32[]{:S(2)}) %all-to-all-start.1) | async-done | bytes 524320 | tf_op jit(solution)/shard_map/all_to_all | solution.py:721
  52.6 2.2 %heat.1 = (f32[16,128,256]{2,1,0:T(8,128)S(1)}, f32[128,256]{1,0:T(8,128)S(1)}, f32[128,256]{1,0:T(8,128)S(1)}, f32[128,128]{1,0:T(8,128)S(1)}, f32[128,128]{1,0...) custom-call(f32[128,256]{1,0:T(8,128)S(1)} %get-tuple-element.32.top_ref, ...), custom_call_target="tpu_custom_call" | custom-call | flops 1000000000 | bytes 1048576 | tf_op jit(solution)/shard_map/heat/pallas_call | solution.py:585
  54.8 0.1 collective-permute-start.4
  54.9 3.9 %collective-permute-start.5 = (f32[128,128]{1,0:T(8,128)S(1)}, f32[128,128]{1,0:T(8,128)S(1)}, u32[]{:S(2)}, u32[]{:S(2)}) collective-permute-start(f32[128,128]{1,0:T(8,128)S(1)} %get-tuple-element.44), channel_id=1, source_target_pairs={{8,16},{16,8},{24,32},{32,24},{40,48},{48,40},{56,64},{64,56},{72,... | collective-permute-start | bytes 196616 | tf_op jit(solution)/shard_map/ppermute | solution.py:297
  58.8 0.8 %collective-permute-start.6 = (f32[32,256]{1,0:T(8,128)S(1)}, f32[32,256]{1,0:T(8,128)S(1)}, u32[]{:S(2)}, u32[]{:S(2)}) collective-permute-start(f32[32,256]{1,0:T(8,128)S(1)} %get-tuple-element.45), channel_id=1, source_target_pairs={{0,1},{1,0},{2,3},{3,2},{4,5},{5,4},{6,7},{7,6},{8,9},{9,8},{10,11... | collective-permute-start | bytes 98312 | tf_op jit(solution)/shard_map/ppermute | solution.py:298
  59.7 2.9 %collective-permute-start.7 = (f32[32,256]{1,0:T(8,128)S(1)}, f32[32,256]{1,0:T(8,128)S(1)}, u32[]{:S(2)}, u32[]{:S(2)}) collective-permute-start(f32[32,256]{1,0:T(8,128)S(1)} %get-tuple-element.46), channel_id=1, source_target_pairs={{1,2},{2,1},{3,4},{4,3},{5,6},{6,5},{9,10},{10,9},{11,12},{12,11},... | collective-permute-start | bytes 98312 | tf_op jit(solution)/shard_map/ppermute | solution.py:303
  62.5 0.2 collective-permute-done.6.lat_a
  62.8 5.8 %collective-permute-done.7.lat_b = f32[32,256]{1,0:T(8,128)S(1)} collective-permute-done((f32[32,256]{1,0:T(8,128)S(1)}, f32[32,256]{1,0:T(8,128)S(1)}, u32[]{:S(2)}, u32[]{:S(2)}) %collective-permute-start.7) | collective-permute-done | bytes 32800 | tf_op jit(solution)/shard_map/ppermute | solution.py:303
  68.5 0.0 collective-permute-done.4.lon_a
  68.5 0.0 collective-permute-done.5.lon_b
  68.5 8.7 %second_step.1 = (f32[16,128,256]{2,1,0:T(8,128)}, f32[16,128,256]{2,1,0:T(8,128)}, f32[16,128,256]{2,1,0:T(8,128)}) custom-call(f32[16,128,256]{2,1,0:T(8,128)S(1)} %get-tuple-element.31.t_ref, f32[16,128,256]{2,1,0:T(8,128)S(1)} %get-tuple-element.39.s_ref, f32[16,128,256]{2,1,0:T(8,128)} %u_hbm.3, f32[16,128,256]{2,1,0:T(8,128)} %v_hbm.3, ...), custom_call_target="tpu_custom_call" | custom-call | flops 70000000 | bytes 26214400 | tf_op jit(solution)/shard_map/second_step/pallas_call | solution.py:679
Async XLA Ops:
  3.5 29.3 %all-to-all-start = ((f32[128,1,1152]{2,1,0:T(1,128)}), f32[128,1,1152]{2,1,0:T(1,128)S(1)}, u32[]{:S(2)}, u32[]{:S(2)}) async-start(f32[128,1,1152]{2,1,0:T(1,128)} %bitcast.6), calls=%async_computation | async-start | bytes 1179648 | tf_op jit(solution)/shard_map/all_to_all | solution.py:714
  13.7 19.1 %copy-start = (f32[1,1,256,128]{3,2,1,0:T(8,128)S(1)}, f32[1,1,256,128]{3,2,1,0:T(8,128)}, u32[]{:S(2)}) copy-start(f32[1,1,256,128]{3,2,1,0:T(8,128)} %param.20) | copy-start | bytes 393220
  13.7 19.1 %copy-start.1 = (f32[1,1,256,128]{3,2,1,0:T(8,128)S(1)}, f32[1,1,256,128]{3,2,1,0:T(8,128)}, u32[]{:S(2)}) copy-start(f32[1,1,256,128]{3,2,1,0:T(8,128)} %param.21) | copy-start | bytes 393220
  17.7 8.1 %collective-permute-start = (f32[128,128]{1,0:T(8,128)S(1)}, f32[128,128]{1,0:T(8,128)S(1)}, u32[]{:S(2)}, u32[]{:S(2)}) collective-permute-start(f32[128,128]{1,0:T(8,128)S(1)} %get-tuple-element.27), channel_id=1, source_target_pairs={{0,8},{8,0},{16,24},{24,16},{32,40},{40,32},{48,56},{56,48},{64,72... | collective-permute-start | bytes 196616 | tf_op jit(solution)/shard_map/ppermute | solution.py:296
  17.9 8.0 %collective-permute-start.1 = (f32[128,128]{1,0:T(8,128)S(1)}, f32[128,128]{1,0:T(8,128)S(1)}, u32[]{:S(2)}, u32[]{:S(2)}) collective-permute-start(f32[128,128]{1,0:T(8,128)S(1)} %get-tuple-element.28), channel_id=1, source_target_pairs={{8,16},{16,8},{24,32},{32,24},{40,48},{48,40},{56,64},{64,56},{72,... | collective-permute-start | bytes 196616 | tf_op jit(solution)/shard_map/ppermute | solution.py:297
  22.8 4.3 %collective-permute-start.2 = (f32[64,256]{1,0:T(8,128)S(1)}, f32[64,256]{1,0:T(8,128)S(1)}, u32[]{:S(2)}, u32[]{:S(2)}) collective-permute-start(f32[64,256]{1,0:T(8,128)S(1)} %get-tuple-element.29), channel_id=1, source_target_pairs={{0,1},{1,0},{2,3},{3,2},{4,5},{5,4},{6,7},{7,6},{8,9},{9,8},{10,11... | collective-permute-start | bytes 196616 | tf_op jit(solution)/shard_map/ppermute | solution.py:298
  23.7 9.2 %collective-permute-start.3 = (f32[64,256]{1,0:T(8,128)S(1)}, f32[64,256]{1,0:T(8,128)S(1)}, u32[]{:S(2)}, u32[]{:S(2)}) collective-permute-start(f32[64,256]{1,0:T(8,128)S(1)} %get-tuple-element.30), channel_id=1, source_target_pairs={{1,2},{2,1},{3,4},{4,3},{5,6},{6,5},{9,10},{10,9},{11,12},{12,11},... | collective-permute-start | bytes 196616 | tf_op jit(solution)/shard_map/ppermute | solution.py:303
  34.5 18.1 %all-to-all-start.1 = ((f32[128,8,128]{2,1,0:T(8,128)}), f32[128,8,128]{2,1,0:T(8,128)S(1)}, u32[]{:S(2)}, u32[]{:S(2)}) async-start(f32[128,8,128]{2,1,0:T(8,128)} %bitcast.10), calls=%async_computation.1 | async-start | bytes 1048576 | tf_op jit(solution)/shard_map/all_to_all | solution.py:721
  54.8 13.7 %collective-permute-start.4 = (f32[128,128]{1,0:T(8,128)S(1)}, f32[128,128]{1,0:T(8,128)S(1)}, u32[]{:S(2)}, u32[]{:S(2)}) collective-permute-start(f32[128,128]{1,0:T(8,128)S(1)} %get-tuple-element.43), channel_id=1, source_target_pairs={{0,8},{8,0},{16,24},{24,16},{32,40},{40,32},{48,56},{56,48},{64,72... | collective-permute-start | bytes 196616 | tf_op jit(solution)/shard_map/ppermute | solution.py:296
  54.9 13.6 %collective-permute-start.5 = (f32[128,128]{1,0:T(8,128)S(1)}, f32[128,128]{1,0:T(8,128)S(1)}, u32[]{:S(2)}, u32[]{:S(2)}) collective-permute-start(f32[128,128]{1,0:T(8,128)S(1)} %get-tuple-element.44), channel_id=1, source_target_pairs={{8,16},{16,8},{24,32},{32,24},{40,48},{48,40},{56,64},{64,56},{72,... | collective-permute-start | bytes 196616 | tf_op jit(solution)/shard_map/ppermute | solution.py:297
  58.8 3.9 %collective-permute-start.6 = (f32[32,256]{1,0:T(8,128)S(1)}, f32[32,256]{1,0:T(8,128)S(1)}, u32[]{:S(2)}, u32[]{:S(2)}) collective-permute-start(f32[32,256]{1,0:T(8,128)S(1)} %get-tuple-element.45), channel_id=1, source_target_pairs={{0,1},{1,0},{2,3},{3,2},{4,5},{5,4},{6,7},{7,6},{8,9},{9,8},{10,11... | collective-permute-start | bytes 98312 | tf_op jit(solution)/shard_map/ppermute | solution.py:298
  59.7 8.8 %collective-permute-start.7 = (f32[32,256]{1,0:T(8,128)S(1)}, f32[32,256]{1,0:T(8,128)S(1)}, u32[]{:S(2)}, u32[]{:S(2)}) collective-permute-start(f32[32,256]{1,0:T(8,128)S(1)} %get-tuple-element.46), channel_id=1, source_target_pairs={{1,2},{2,1},{3,4},{4,3},{5,6},{6,5},{9,10},{10,9},{11,12},{12,11},... | collective-permute-start | bytes 98312 | tf_op jit(solution)/shard_map/ppermute | solution.py:303
